TPU v7x, 128 devices: a whole 4x4x4 slice. The times are simulated.
128 devices in a mesh: seq: 32 (over y, x_lo, z), fsdp: 4 (over x_hi, core).
Axes of the slice: x: 4 (x_hi: 2, x_lo: 2; x = x_hi * 2 + x_lo), y: 4, z: 4, core: 2. Of those that a mesh axis runs over, the one named last changes fastest.
Arguments:
- tokens: float32 [4, 8192, 1024], P('fsdp', 'seq'), may hold values from -6 to 6
- cotangent: float32 [4, 8192, 1024], P('fsdp', 'seq'), may hold values from -6 to 6
- norm1_gain: bfloat16 [1024], P(('seq', 'fsdp')), may hold values from 0.099609375 to 1.8984375
- in_weight: bfloat16 [1024, 3072], P(('seq', 'fsdp')), may hold values from -0.1875 to 0.1875
- conv_taps: bfloat16 [3, 1024], P(None, ('seq', 'fsdp')), may hold values from -3.5 to 3.5
- out_weight: bfloat16 [1024, 1024], P(('seq', 'fsdp')), may hold values from -0.1875 to 0.1875
- norm2_gain: bfloat16 [1024], P(('seq', 'fsdp')), may hold values from 0.099609375 to 1.8984375
- gate_weight: bfloat16 [1024, 4608], P(('seq', 'fsdp')), may hold values from -0.1875 to 0.1875
- up_weight: bfloat16 [1024, 4608], P(('seq', 'fsdp')), may hold values from -0.1875 to 0.1875
- down_weight: bfloat16 [4608, 1024], P(('seq', 'fsdp')), may hold values from -0.09375 to 0.09375
Outputs:
- block_out: float32 [4, 8192, 1024], P('fsdp', 'seq')
- input_grad: float32 [4, 8192, 1024], P('fsdp', 'seq')
- norm1_gain_grad: float32 [1024], P(('seq', 'fsdp'))
- in_weight_grad: float32 [1024, 3072], P(('seq', 'fsdp'))
- conv_taps_grad: float32 [3, 1024], P(None, ('seq', 'fsdp'))
- out_weight_grad: float32 [1024, 1024], P(('seq', 'fsdp'))
- norm2_gain_grad: float32 [1024], P(('seq', 'fsdp'))
- gate_weight_grad: float32 [1024, 4608], P(('seq', 'fsdp'))
- up_weight_grad: float32 [1024, 4608], P(('seq', 'fsdp'))
- down_weight_grad: float32 [4608, 1024], P(('seq', 'fsdp'))
All inputs are finite; a program needn't handle non-finite values.
Results may differ from a plain program's by a relative error of at most 0.0097.
Values may be sent and summed in bfloat16 or wider, within the bound.
A program may use at most 128 MiB of HBM per device.

v0:
```python
import math

import jax
import jax.numpy as jnp
from jax import lax
from jax.sharding import PartitionSpec as P

norm_eps = 1e-05


def shifted(shard, axis, by):
    peers = lax.axis_size(axis)
    pairs = [(i, i + by) for i in range(peers) if 0 <= i + by < peers]
    return lax.ppermute(shard, axis, pairs)


def side_by_side(arrays, axis, split_dim, concat_dim, along):
    widths = [a.shape[along] for a in arrays]
    both = jnp.concatenate(arrays, axis=along)
    result = lax.all_to_all(both, axis, split_axis=split_dim, concat_axis=concat_dim, tiled=True)
    return tuple(jnp.split(result, [sum(widths[:k]) for k in range(1, len(widths))], axis=along))


def in_one_piece(arrays, axis, dim, along):
    columns = [a.reshape(*a.shape[:along], -1) for a in arrays]
    both = jnp.concatenate(columns, axis=along)
    result, at, gathered = (lax.all_gather(both, axis, axis=dim, tiled=True), 0, [])
    for a, column in zip(arrays, columns):
        slab = result[..., at : at + column.shape[along]]
        gathered.append(slab.reshape(*slab.shape[:along], *a.shape[along:]))
        at += column.shape[along]
    return tuple(gathered)


def in_one_piece_2(arrays, axis, dim, along):
    ends, at = ([], 0)
    for a in arrays[:-1]:
        at += a.shape[along]
        ends.append(at)
    both = jnp.concatenate(arrays, axis=along)
    return tuple(jnp.split(lax.all_gather(both, axis, axis=dim, tiled=True), ends, axis=along))


def in_blocks(shard, dim, peers):
    before, after = (shard.shape[:dim], shard.shape[dim + 1 :])
    return jnp.moveaxis(shard.reshape(*before, peers, -1, *after), dim, 0)


def summed_on_arrival(shard, axis, dim):
    parts = in_blocks(shard, dim, lax.axis_size(axis))
    arrived = lax.all_to_all(parts, axis, split_axis=0, concat_axis=0, tiled=True)
    return arrived.sum(axis=0)


def from_everyone(shard, axis):
    peers = lax.axis_size(axis)
    return lax.all_to_all(
        jnp.broadcast_to(shard[None], (peers, *shard.shape)), axis, 0, 0, tiled=True
    )


def in_order(parts, dim):
    dims = list(parts.shape[1:])
    dims[dim] *= parts.shape[0]
    return jnp.moveaxis(parts, 0, dim).reshape(dims)


def gathered_copies(shard, axis, dim):
    parts = from_everyone(shard, axis)
    return in_order(parts, dim)


def in_one_piece_3(arrays, axis, dim, along):
    widths = [a.shape[along] for a in arrays]
    both = jnp.concatenate(arrays, axis=along)
    result = lax.psum_scatter(both, axis, scatter_dimension=dim, tiled=True)
    return tuple(jnp.split(result, [sum(widths[:k]) for k in range(1, len(widths))], axis=along))


def rms_inverse(values):
    return lax.rsqrt(jnp.mean(values * values, axis=-1, keepdims=True) + norm_eps)


def conv_forward(gated, taps):
    earlier = shifted(gated[:, -2:], "seq", 1)
    padded = jnp.concatenate([earlier, gated], axis=1)
    convolved = taps[0] * padded[:, :-2] + taps[1] * padded[:, 1:-1] + taps[2] * padded[:, 2:]
    return (padded, convolved)


def conv_backward(d_conv, padded, taps):
    grad_taps = jnp.stack(
        [
            jnp.sum(d_conv * padded[:, :-2], axis=(0, 1)),
            jnp.sum(d_conv * padded[:, 1:-1], axis=(0, 1)),
            jnp.sum(d_conv * padded[:, 2:], axis=(0, 1)),
        ]
    )
    later = shifted(d_conv[:, :2], "seq", -1)
    dconv_pad = jnp.concatenate([d_conv, later], axis=1)
    d_gated = (
        taps[0] * dconv_pad[:, 2:] + taps[1] * dconv_pad[:, 1:-1] + taps[2] * dconv_pad[:, :-2]
    )
    return (grad_taps, d_gated)


def mixer_forward(hidden_rows, w_inproj, taps, seq_count):
    projected = jnp.dot(hidden_rows, w_inproj, preferred_element_type=jnp.float32)
    feat_cols = w_inproj.shape[1] // 3
    b_mat = projected[:, :feat_cols]
    c_mat = projected[:, feat_cols : 2 * feat_cols]
    x_mat = projected[:, 2 * feat_cols :]
    gated = (b_mat * x_mat).reshape(seq_count, -1, feat_cols)
    padded, convolved = conv_forward(gated, taps)
    convolved = convolved.reshape(-1, feat_cols)
    y_mat = (c_mat * convolved).astype(jnp.bfloat16)
    return ((b_mat, c_mat, x_mat, padded, convolved), y_mat)


def mixer_backward(dres_half, y_mat, w_outproj, pieces, taps, hidden_rows, w_inproj):
    b_mat, c_mat, x_mat, padded, convolved = pieces
    grad_out = jnp.dot(y_mat.T, dres_half, preferred_element_type=jnp.float32)
    d_ymat = jnp.dot(dres_half, w_outproj.T, preferred_element_type=jnp.float32)
    d_cmat = d_ymat * convolved
    d_conv = d_ymat * c_mat
    feat_cols = c_mat.shape[1]
    grad_taps, d_gated = conv_backward(d_conv.reshape(padded.shape[0], -1, feat_cols), padded, taps)
    d_gated = d_gated.reshape(-1, feat_cols)
    d_proj = jnp.concatenate([d_gated * x_mat, d_cmat, d_gated * b_mat], axis=1).astype(
        jnp.bfloat16
    )
    grad_in = jnp.dot(hidden_rows.T, d_proj, preferred_element_type=jnp.float32)
    d_hidden_one = jnp.dot(d_proj, w_inproj.T, preferred_element_type=jnp.float32)
    return (grad_out, grad_taps, grad_in, d_hidden_one)


def ffn_forward(hidden_two, w_gate, w_upproj, w_down):
    gate = jnp.dot(hidden_two, w_gate, preferred_element_type=jnp.float32)
    up_vals = jnp.dot(hidden_two, w_upproj, preferred_element_type=jnp.float32)
    sigma_gate = jax.nn.sigmoid(gate)
    activated = (gate * sigma_gate * up_vals).astype(jnp.bfloat16)
    out_part = jnp.dot(activated, w_down, preferred_element_type=jnp.float32)
    return ((gate, up_vals, sigma_gate, activated), out_part)


def ffn_backward(cot_rows, hidden_two, saved, w_gate, w_upproj, w_down):
    gate, up_vals, sigma_gate, activated = saved
    grad_down = jnp.dot(activated.T, cot_rows, preferred_element_type=jnp.float32)
    d_act = jnp.dot(cot_rows, w_down.T, preferred_element_type=jnp.float32)
    d_gate = (d_act * up_vals * sigma_gate * (1.0 + gate * (1.0 - sigma_gate))).astype(jnp.bfloat16)
    d_upvals = (d_act * gate * sigma_gate).astype(jnp.bfloat16)
    grad_gate = jnp.dot(hidden_two.T, d_gate, preferred_element_type=jnp.float32)
    grad_up = jnp.dot(hidden_two.T, d_upvals, preferred_element_type=jnp.float32)
    d_hidden_two = jnp.dot(d_gate, w_gate.T, preferred_element_type=jnp.float32) + jnp.dot(
        d_upvals, w_upproj.T, preferred_element_type=jnp.float32
    )
    return (grad_down, grad_gate, grad_up, d_hidden_two)


def norm_backward(d_hidden, gain, normed, inverse, base):
    grad_gain = jnp.sum(d_hidden * normed, axis=0)
    scaled = d_hidden * gain
    result = base + inverse * (scaled - normed * jnp.mean(scaled * normed, axis=-1, keepdims=True))
    return (grad_gain, result)


def own_rows(values, my_index, groups):
    return lax.dynamic_slice_in_dim(
        values.reshape(groups, -1, values.shape[-1]), my_index, 1, 0
    ).reshape(-1, values.shape[-1])


def shards(
    tokens,
    cotangent,
    norm1_gain,
    in_weight,
    conv_taps,
    out_weight,
    norm2_gain,
    gate_weight,
    up_weight,
    down_weight,
):
    width = tokens.shape[-1]
    inputs = tokens.reshape(-1, width)
    upstream = cotangent.reshape(-1, width)
    total_rows = inputs.shape[0] * lax.axis_size("seq") * lax.axis_size("fsdp")
    factor = 1.0 / math.sqrt(total_rows)
    inv_one = rms_inverse(inputs)
    normed_one = inputs * inv_one
    cot_half = upstream.astype(jnp.bfloat16)
    n_seq = lax.axis_size("seq")
    n_fsdp = lax.axis_size("fsdp")
    my_index = lax.axis_index("fsdp")
    narrow = width // (n_seq * n_fsdp)
    ff_narrow = gate_weight.shape[1] // (n_seq * n_fsdp)
    tile_one = jnp.broadcast_to(norm1_gain.reshape(1, 1, 1, narrow), (1, 1, n_fsdp, narrow))
    tile_two = jnp.broadcast_to(norm2_gain.reshape(1, 1, 1, narrow), (1, 1, n_fsdp, narrow))
    swapped = (
        lax.all_to_all(
            in_weight.reshape(narrow, 3 * n_seq, n_fsdp, narrow),
            "fsdp",
            split_axis=2,
            concat_axis=0,
            tiled=True,
        ),
        *side_by_side(
            (
                gate_weight.reshape(narrow, n_seq, n_fsdp, ff_narrow),
                up_weight.reshape(narrow, n_seq, n_fsdp, ff_narrow),
            ),
            "fsdp",
            2,
            0,
            1,
        ),
        *side_by_side((tile_one, tile_two), "fsdp", 2, 0, 1),
    )
    columns = (
        *in_one_piece((swapped[0], swapped[1], swapped[2]), "seq", 0, 1),
        *in_one_piece_2((swapped[3], swapped[4]), "seq", 0, 1),
        lax.all_gather(out_weight, "seq", axis=0, tiled=True),
        lax.all_gather(down_weight, "seq", axis=0, tiled=True),
        lax.all_gather(conv_taps, "seq", axis=1, tiled=True),
    )
    w_inproj = columns[0].reshape(width, -1)
    w_gate = columns[1].reshape(width, -1)
    w_upproj = columns[2].reshape(width, -1)
    gain_one = columns[3].reshape(-1).astype(jnp.float32)
    gain_two = columns[4].reshape(-1).astype(jnp.float32)
    w_outproj = columns[5]
    w_down = columns[6]
    taps = columns[7].astype(jnp.float32)
    hidden_one = (normed_one * gain_one).astype(jnp.bfloat16)
    row_sets = in_one_piece_2((hidden_one[None], cot_half[None]), "fsdp", 0, 1)
    hidden_rows = row_sets[0].reshape(-1, width)
    cot_rows = row_sets[1].reshape(-1, width)
    pieces, y_mat = mixer_forward(hidden_rows, w_inproj, taps, n_fsdp)
    mixed = jnp.dot(y_mat, w_outproj, preferred_element_type=jnp.float32).reshape(n_fsdp, -1, width)
    own_slot = (jnp.arange(n_fsdp) == my_index).astype(jnp.float32).reshape(n_fsdp, 1, 1)
    resid_all = lax.psum(mixed + own_slot * inputs[None], "fsdp").reshape(-1, width)
    inv_two = rms_inverse(resid_all)
    normed_two = resid_all * inv_two
    hidden_two = (normed_two * gain_two).astype(jnp.bfloat16)
    saved, out_part = ffn_forward(hidden_two, w_gate, w_upproj, w_down)
    ffn_own = summed_on_arrival(out_part.reshape(n_fsdp, -1, width), "fsdp", 0).reshape(-1, width)
    block_out = own_rows(resid_all, my_index, n_fsdp) + ffn_own
    grad_down, grad_gate, grad_up, d_hidden_part = ffn_backward(
        cot_rows, hidden_two, saved, w_gate, w_upproj, w_down
    )
    d_hidden_two = summed_on_arrival(d_hidden_part.reshape(n_fsdp, -1, width), "fsdp", 0).reshape(
        -1, width
    )
    normed_own = own_rows(normed_two, my_index, n_fsdp)
    inverse_own = own_rows(inv_two, my_index, n_fsdp)
    grad_gain_two, d_resid = norm_backward(
        d_hidden_two, gain_two, normed_own, inverse_own, upstream
    )
    dres_half = d_resid.astype(jnp.bfloat16)
    dres_rows = gathered_copies(dres_half[None], "fsdp", 0).reshape(-1, width)
    grad_out, grad_taps, grad_in, d_hidden_part_one = mixer_backward(
        dres_rows, y_mat, w_outproj, pieces, taps, hidden_rows, w_inproj
    )
    d_hidden_one = summed_on_arrival(
        d_hidden_part_one.reshape(n_fsdp, -1, width), "fsdp", 0
    ).reshape(-1, width)
    grad_gain_one, input_grad = norm_backward(d_hidden_one, gain_one, normed_one, inv_one, d_resid)
    partial_value = (
        *in_one_piece_3((grad_in, grad_gate, grad_up), "seq", 0, 1),
        lax.psum_scatter(grad_out, "seq", scatter_dimension=0, tiled=True),
        lax.psum_scatter(grad_down, "seq", scatter_dimension=0, tiled=True),
        lax.psum_scatter(grad_taps, "seq", scatter_dimension=1, tiled=True),
        lax.psum_scatter(grad_gain_one, "seq", scatter_dimension=0, tiled=True),
        lax.psum_scatter(grad_gain_two, "seq", scatter_dimension=0, tiled=True),
    )
    returned = (
        lax.all_to_all(
            partial_value[0].reshape(n_fsdp * narrow, 3 * n_seq, 1, narrow),
            "fsdp",
            split_axis=0,
            concat_axis=2,
            tiled=True,
        ),
        *side_by_side(
            (
                partial_value[1].reshape(n_fsdp * narrow, n_seq, 1, ff_narrow),
                partial_value[2].reshape(n_fsdp * narrow, n_seq, 1, ff_narrow),
            ),
            "fsdp",
            0,
            2,
            1,
        ),
        *side_by_side(
            (
                partial_value[6].reshape(n_fsdp * narrow, 1, 1, 1),
                partial_value[7].reshape(n_fsdp * narrow, 1, 1, 1),
            ),
            "fsdp",
            0,
            2,
            1,
        ),
    )
    results = (
        jnp.sum(returned[3], axis=2).reshape(-1),
        returned[0].reshape(narrow, -1),
        partial_value[5],
        partial_value[3],
        jnp.sum(returned[4], axis=2).reshape(-1),
        returned[1].reshape(narrow, -1),
        returned[2].reshape(narrow, -1),
        partial_value[4],
    )
    return (
        block_out.reshape(tokens.shape),
        input_grad.reshape(tokens.shape),
        results[0] * factor,
        results[1] * factor,
        results[2] * factor,
        results[3] * factor,
        results[4] * factor,
        results[5] * factor,
        results[6] * factor,
        results[7] * factor,
    )


def solution(mesh):
    in_specs = (
        P("fsdp", "seq", None),
        P("fsdp", "seq", None),
        P(("seq", "fsdp")),
        P(("seq", "fsdp"), None),
        P(None, ("seq", "fsdp")),
        P(("seq", "fsdp"), None),
        P(("seq", "fsdp")),
        P(("seq", "fsdp"), None),
        P(("seq", "fsdp"), None),
        P(("seq", "fsdp"), None),
    )
    out_specs = (
        P("fsdp", "seq", None),
        P("fsdp", "seq", None),
        P(("seq", "fsdp")),
        P(("seq", "fsdp"), None),
        P(None, ("seq", "fsdp")),
        P(("seq", "fsdp"), None),
        P(("seq", "fsdp")),
        P(("seq", "fsdp"), None),
        P(("seq", "fsdp"), None),
        P(("seq", "fsdp"), None),
    )
    return jax.shard_map(shards, mesh=mesh, in_specs=in_specs, out_specs=out_specs, check_vma=False)
```

profile of v0, /device:TPU:1, one launch (start us, length us, event | category | flops | bytes accessed | tf_op | source)
XLA Modules:
  0.0 1175.6 jit_solution(13166942069127446127)
XLA Ops:
  9.2 5.8 all-to-all-start
  19.5 68.0 %all-gather = bf16[128,1,2,1,8]{4,2,3,1,0:T(2,128)(2,1)S(1)} all-gather(bf16[4,1,2,1,8]{4,2,3,1,0:T(2,128)(2,1)S(1)} %copy.132), channel_id=2, replica_groups=mesh['seq'=32,'fsdp'=4] {'seq'}, dimensions={0}, use_global_device_ids=true | all-gather | bytes 4224 | tf_op jit(solution)/shard_map/all_gather | solution.py:41
  91.3 18.0 %all-to-all-start.1 = ((bf16[8,96,4,8]{1,3,0,2:T(8,128)(2,1)}), bf16[8,96,4,8]{1,3,0,2:T(8,128)(2,1)S(1)}, u32[]{:S(2)}, u32[]{:S(2)}) async-start(bf16[8,96,4,8]{1,3,0,2:T(8,128)(2,1)} %copy.133), calls=%async_computation.1 | async-start | bytes 131072 | tf_op jit(solution)/shard_map/all_to_all | solution.py:201
  114.7 4.0 all-to-all-start.2
  120.0 6.0 all-to-all-done.2
  129.6 63.8 %all-gather.1 = bf16[32,8,3]{1,2,0:T(4,128)(2,1)S(1)} all-gather(bf16[1,8,3]{1,2,0:T(4,128)(2,1)S(1)} %bitcast.220), channel_id=1, replica_groups=mesh['seq'=32,'fsdp'=4] {'seq'}, dimensions={0}, use_global_device_ids=true | all-gather | bytes 1584 | tf_op jit(solution)/shard_map/all_gather | solution.py:225
  193.7 70.7 %all_gather.22 = bf16[256,1024]{1,0:T(8,128)(2,1)S(1)} all-gather(bf16[8,1024]{1,0:T(8,128)(2,1)S(1)} %copy-done.23), channel_id=1, replica_groups=mesh['seq'=32,'fsdp'=4] {'seq'}, dimensions={0}, use_global_device_ids=true | all-gather | bytes 540672 | tf_op jit(solution)/shard_map/all_gather | solution.py:223
  264.4 4.9 fusion.45
  269.3 15.0 %all-gather.9.cloned.1.call-done = bf16[1024,3072]{1,0:T(8,128)(2,1)} async-done(((bf16[32,3072]{1,0:T(8,128)(2,1)}), bf16[1024,3072]{1,0:T(8,128)(2,1)}) %all-gather.9.cloned.1.call-update) | async-done | bytes 6291472 | tf_op jit(solution)/shard_map/all_gather | solution.py:27
  284.3 3.8 fusion.16
  292.4 2.7 multiply_add_fusion
  295.2 144.9 %all-gather.11.cloned.1.call-done = bf16[32,36,1024]{2,1,0:T(8,128)(2,1)} async-done(((bf16[1,36,1024]{2,1,0:T(8,128)(2,1)}), bf16[32,36,1024]{2,1,0:T(8,128)(2,1)}) %all-gather.11.cloned.1.call-update) | async-done | bytes 2359312 | tf_op jit(solution)/shard_map/all_gather | solution.py:224
  440.1 2.7 reshape.400
  442.7 7.5 fusion.54
  450.2 105.9 %all-reduce.8.cloned.1.call-done = f32[4,256,1024]{2,1,0:T(8,128)} async-done(((f32[4,256,1024]{2,1,0:T(8,128)}), f32[4,256,1024]{2,1,0:T(8,128)}) %all-reduce.8.cloned.1.call-update) | async-done | bytes 4194320 | tf_op jit(solution)/shard_map/psum | solution.py:242
  556.2 2.7 multiply_reduce_fusion
  560.1 5.5 fusion.5
  565.7 6.7 multiply_convert_fusion.1
  572.4 2.9 fusion.3
  575.3 4.6 fusion.11
  579.9 5.3 all-to-all-start.4
  585.2 48.8 %all-to-all-done.4 = f32[4,1,256,1024]{3,2,1,0:T(8,128)} async-done(((f32[4,1,256,1024]{3,2,1,0:T(8,128)}), f32[4,1,256,1024]{3,2,1,0:T(8,128)}, u32[]{:S(2)}, u32[]{:S(2)}) %all-to-all-start.4) | async-done | bytes 4194336 | tf_op jit(solution)/shard_map/all_to_all | solution.py:51
  634.0 2.7 reduce_sum.136
  641.6 5.3 all-to-all-start.5
  646.9 7.5 fusion.56
  654.4 4.7 fusion.55
  659.1 14.2 %all-to-all-done.5 = bf16[4,1,256,1024]{3,2,1,0:T(8,128)(2,1)} async-done(((bf16[4,1,256,1024]{3,2,1,0:T(8,128)(2,1)}), bf16[4,1,256,1024]{3,2,1,0:T(8,128)(2,1)}, u32[]{:S(2)}, u32[]{:S(2)}) %all-to-all-start.5) | async-done | bytes 2097184 | tf_op jit(solution)/shard_map/all_to_all | solution.py:57
  673.3 3.5 fusion.57
  676.9 3.7 multiply_reduce_fusion.3
  688.6 5.1 pad_maximum_fusion
  693.7 7.2 fusion.53
  700.9 6.8 all-to-all-start.3
  707.8 7.2 fusion.58
  715.0 5.2 fusion.14
  720.2 40.1 %all-to-all-done.3 = f32[4,1,256,1024]{3,2,1,0:T(8,128)} async-done(((f32[4,1,256,1024]{3,2,1,0:T(8,128)}), f32[4,1,256,1024]{3,2,1,0:T(8,128)}, u32[]{:S(2)}, u32[]{:S(2)}) %all-to-all-start.3) | async-done | bytes 4194336 | tf_op jit(solution)/shard_map/all_to_all | solution.py:51
  760.4 5.7 all-to-all-start.6
  766.0 151.8 %fusion = f32[40,1024]{1,0:T(8,128)S(1)} fusion(f32[1152,1024]{1,0:T(8,128)} %fusion.58), kind=kCustom, calls=%all-reduce-scatter | all-reduce-scatter fusion | flops 1310721 | bytes 4882944
  923.1 2.9 collective-permute-start.5
  928.5 4.2 collective-permute-done.2
  932.7 6.9 concatenate.42
  941.2 3.7 reduce_sum.134
  946.4 3.7 reduce_sum.139
  951.7 137.2 %all-reduce.5 = (f32[1024]{0:T(1024)S(1)}, f32[1024]{0:T(1024)S(1)}, f32[3,256]{1,0:T(4,128)S(1)}) all-reduce(f32[1024]{0:T(1024)S(1)} %get-tuple-element.10, f32[1024]{0:T(1024)S(1)} %get-tuple-element.14, f32[3,256]{1,0:T(4,128)S(1)} %pad_maximum_fusion.10), channel_id=4, replica_groups=mesh['seq'=32,'fsdp'=4] {'seq'}, use_global_device_ids=true, to_apply=%region_11.0.clone | all-reduce | flops 2816 | bytes 22528
  1089.7 39.9 %all-to-all-start.7 = ((f32[32,2,1,1]{1,3,2,0:T(1,128)}), f32[32,2,1,1]{1,3,2,0:T(1,128)S(1)}, u32[]{:S(2)}, u32[]{:S(2)}) async-start(f32[32,2,1,1]{1,3,2,0:T(1,128)} %copy.144), calls=%async_computation.7 | async-start | bytes 32768 | tf_op jit(solution)/shard_map/all_to_all | solution.py:20
  1129.7 3.6 fusion.26
  1137.4 4.5 all-to-all-start.8
  1150.1 4.8 all-to-all-start.9
  1158.1 3.8 all-to-all-done.9
  (204 shorter events, 72.1 us)
Async XLA Ops:
  7.2 80.8 %copy-start.1 = (f32[1,256,1024]{2,1,0:T(8,128)S(1)}, f32[1,256,1024]{2,1,0:T(8,128)}, u32[]{:S(2)}) copy-start(f32[1,256,1024]{2,1,0:T(8,128)} %param.10) | copy-start | bytes 3145732
  9.2 10.3 all-to-all-start
  15.0 249.4 %all-gather.7.cloned.1.call-start = ((), (), s32[]{:S(2)}) async-start(), calls=%async_computation.12 | async-start | bytes 5242880 | tf_op jit(solution)/shard_map/all_gather | solution.py:41
  16.4 72.8 %copy-start.22 = (bf16[8,3072]{1,0:T(8,128)(2,1)S(1)}, bf16[8,3072]{1,0:T(8,128)(2,1)}, u32[]{:S(2)}) copy-start(bf16[8,3072]{1,0:T(8,128)(2,1)} %param.13) | copy-start | bytes 147460
  88.0 21.3 %copy-start.20 = (bf16[8,4608]{1,0:T(8,128)(2,1)S(1)}, bf16[8,4608]{1,0:T(8,128)(2,1)}, u32[]{:S(2)}) copy-start(bf16[8,4608]{1,0:T(8,128)(2,1)} %param.18) | copy-start | bytes 221188
  88.0 22.0 %copy-start.21 = (bf16[8,4608]{1,0:T(8,128)(2,1)S(1)}, bf16[8,4608]{1,0:T(8,128)(2,1)}, u32[]{:S(2)}) copy-start(bf16[8,4608]{1,0:T(8,128)(2,1)} %param.17) | copy-start | bytes 221188
  91.3 23.4 %all-to-all-start.1 = ((bf16[8,96,4,8]{1,3,0,2:T(8,128)(2,1)}), bf16[8,96,4,8]{1,3,0,2:T(8,128)(2,1)S(1)}, u32[]{:S(2)}, u32[]{:S(2)}) async-start(bf16[8,96,4,8]{1,3,0,2:T(8,128)(2,1)} %copy.133), calls=%async_computation.1 | async-start | bytes 131072 | tf_op jit(solution)/shard_map/all_to_all | solution.py:201
  114.7 11.4 all-to-all-start.2
  118.7 165.6 %all-gather.9.cloned.1.call-start = ((), (), s32[]{:S(2)}) async-start(), calls=%async_computation.13 | async-start | bytes 6488064 | tf_op jit(solution)/shard_map/all_gather | solution.py:27
  118.7 10.9 copy-start.25
  118.7 75.0 %copy-start.23 = (bf16[8,1024]{1,0:T(8,128)(2,1)S(1)}, bf16[8,1024]{1,0:T(8,128)(2,1)}, u32[]{:S(2)}) copy-start(bf16[8,1024]{1,0:T(8,128)(2,1)} %param.15) | copy-start | bytes 49156
  128.8 311.2 %all-gather.11.cloned.1.call-start = ((), (), s32[]{:S(2)}) async-start(), calls=%async_computation.17 | async-start | bytes 2703360 | tf_op jit(solution)/shard_map/all_gather | solution.py:224
  129.6 426.6 %all-reduce.8.cloned.1.call-start = ((), (), s32[]{:S(2)}) async-start(), calls=%async_computation.14 | async-start | bytes 8388608 | tf_op jit(solution)/shard_map/psum | solution.py:242
  264.4 27.0 %copy-start.10 = (bf16[256,1024]{1,0:T(8,128)(2,1)}, bf16[256,1024]{1,0:T(8,128)(2,1)S(1)}, u32[]{:S(2)}) copy-start(bf16[256,1024]{1,0:T(8,128)(2,1)S(1)} %all_gather.22) | copy-start | bytes 1572868
  288.2 3.9 copy-start.8
  288.3 2.6 collective-permute-start
  442.7 7.5 copy-start.9
  559.6 6.0 slice-start.4
  559.6 6.0 slice-start.6
  560.0 5.6 copy-start.11
  560.0 5.6 slice-start.5
  560.1 5.6 slice-start.7
  579.9 54.2 %all-to-all-start.4 = ((f32[4,1,256,1024]{3,2,1,0:T(8,128)}), f32[4,1,256,1024]{3,2,1,0:T(8,128)}, u32[]{:S(2)}, u32[]{:S(2)}) async-start(f32[4,1,256,1024]{3,2,1,0:T(8,128)} %bitcast.193), calls=%async_computation.4 | async-start | bytes 8388608 | tf_op jit(solution)/shard_map/all_to_all | solution.py:51
  585.2 53.2 %copy-start.4 = (f32[1,256,1024]{2,1,0:T(8,128)S(1)}, f32[1,256,1024]{2,1,0:T(8,128)}, u32[]{:S(2)}) copy-start(f32[1,256,1024]{2,1,0:T(8,128)} %param.11) | copy-start | bytes 3145732
  641.6 31.7 %all-to-all-start.5 = ((bf16[4,1,256,1024]{3,2,1,0:T(8,128)(2,1)}), bf16[4,1,256,1024]{3,2,1,0:T(8,128)(2,1)}, u32[]{:S(2)}, u32[]{:S(2)}) async-start(bf16[4,1,256,1024]{3,2,1,0:T(8,128)(2,1)} %broadcast_in_dim.8), calls=%async_computation.5 | async-start | bytes 4194304 | tf_op jit(solution)/shard_map/all_to_all | solution.py:57
  646.9 298.1 %reduce-scatter.8.cloned.1.call-start = ((), (), s32[]{:S(2)}) async-start(), calls=%async_computation.16 | async-start | bytes 1081344 | tf_op jit(solution)/shard_map/reduce_scatter | solution.py:271
  646.9 7.5 copy-start.12
  646.9 7.5 copy-start.27
  676.8 458.6 %reduce-scatter.6.cloned.1.call-start = ((), (), s32[]{:S(2)}) async-start(), calls=%async_computation.15 | async-start | bytes 12976128 | tf_op jit(solution)/shard_map/reduce_scatter | solution.py:76
  676.9 5.2 copy-start.3
  676.9 5.2 copy-start.6
  680.6 4.4 collective-permute-start.1
  682.1 6.4 slice-start
  682.1 6.4 slice-start.2
  682.5 4.1 copy-start.13
  700.9 59.4 %all-to-all-start.3 = ((f32[4,1,256,1024]{3,2,1,0:T(8,128)}), f32[4,1,256,1024]{3,2,1,0:T(8,128)}, u32[]{:S(2)}, u32[]{:S(2)}) async-start(f32[4,1,256,1024]{3,2,1,0:T(8,128)} %bitcast.194), calls=%async_computation.3 | async-start | bytes 8388608 | tf_op jit(solution)/shard_map/all_to_all | solution.py:51
  707.8 7.2 copy-start.15
  707.8 7.2 copy-start.17
  707.8 7.2 copy-start.19
  760.4 186.0 %all-to-all-start.6 = ((f32[4,1,256,1024]{3,2,1,0:T(8,128)}), f32[4,1,256,1024]{3,2,1,0:T(8,128)}, u32[]{:S(2)}, u32[]{:S(2)}) async-start(f32[4,1,256,1024]{3,2,1,0:T(8,128)} %bitcast.192), calls=%async_computation.6 | async-start | bytes 8388608 | tf_op jit(solution)/shard_map/all_to_all | solution.py:51
  766.0 159.9 %copy-start.24 = (u32[128]{0:T(128)S(1)}, u32[128]{0:T(128)}, u32[]{:S(2)}) copy-start(u32[128]{0:T(128)} %constant.41) | copy-start | bytes 1540
  917.8 10.7 collective-permute-start.4
  919.1 9.4 collective-permute-start.3
  921.1 11.6 collective-permute-start.2
  923.1 5.5 collective-permute-start.5
  1089.7 44.6 %all-to-all-start.7 = ((f32[32,2,1,1]{1,3,2,0:T(1,128)}), f32[32,2,1,1]{1,3,2,0:T(1,128)S(1)}, u32[]{:S(2)}, u32[]{:S(2)}) async-start(f32[32,2,1,1]{1,3,2,0:T(1,128)} %copy.144), calls=%async_computation.7 | async-start | bytes 32768 | tf_op jit(solution)/shard_map/all_to_all | solution.py:20
  1137.4 12.7 %all-to-all-start.8 = ((f32[32,96,1,8]{1,3,2,0:T(8,128)}), f32[32,96,1,8]{1,3,2,0:T(8,128)S(1)}, u32[]{:S(2)}, u32[]{:S(2)}) async-start(f32[32,96,1,8]{1,3,2,0:T(8,128)} %copy.148), calls=%async_computation.9 | async-start | bytes 262144 | tf_op jit(solution)/shard_map/all_to_all | solution.py:278
  1150.1 11.8 %all-to-all-start.9 = ((f32[4,1,18432]{2,1,0:T(1,128)}), f32[4,1,18432]{2,1,0:T(1,128)S(1)}, u32[]{:S(2)}, u32[]{:S(2)}) async-start(f32[4,1,18432]{2,1,0:T(1,128)} %reshape.422), calls=%async_computation.11 | async-start | bytes 589824 | tf_op jit(solution)/shard_map/all_to_all | solution.py:20
  (11 other events, 25.9 us)
Sparse Core Ops, SparseCore 0:
  89.3 50.2 all-gather.6
  141.8 142.3 all-gather.8
  285.9 154.1 all-gather.10
  442.4 113.6 all-reduce.7
  677.0 141.2 reduce-scatter.7
  820.6 215.7 reduce-scatter.5
where the time goes:
time: 1180 us
  blocking collectives  491 us (42%)
  waiting for transfers between devices  391 us (33%)
  starting transfers between devices  112 us (9%)
  matrix products  72.7 us (6%)
  other arithmetic  46.7 us (4%)
  local copies, waits for them, and re-layouts  44.2 us (4%)
  between operations  17.4 us (1%)
    unnamed x2, blocking collectives  289 us
    all_gather x1, waiting for transfers between devices, shards(): lax.all_gather(down_weight, 'seq', axis=0, tiled=True)  145 us
    psum x1, waiting for transfers between devices, shards(): lax.psum(mixed + own_slot * inputs[None], 'fsdp').reshape(-1, width)  106 us
    all_to_all x3, waiting for transfers between devices, summed_on_arrival(): lax.all_to_all(parts, axis, split_axis=0, concat_axis=0, tiled=True)  89 us
    all_gather x1, blocking collectives, shards(): lax.all_gather(out_weight, 'seq', axis=0, tiled=True)  70.7 us
    all_gather x1, blocking collectives, in_one_piece_2(): lax.all_gather(both, axis, axis=dim, tiled=True)  68 us
    all_gather x1, blocking collectives, shards(): lax.all_gather(conv_taps, 'seq', axis=1, tiled=True)  63.8 us
    all_to_all x4, starting transfers between devices, side_by_side(): lax.all_to_all(both, axis, split_axis=split_dim, concat_axis=concat_dim,...  54.5 us
  transfers between devices with their start and end apart: 22, of which 14 were waited for; matrix products, arithmetic and copies ran while one was open for 23% of the time, Pallas kernels for 0%

commit v1 on v0

v1 whole, which is shorter than its diff:
```python
import math

import jax
import jax.numpy as jnp
from jax import lax
from jax.experimental import pallas as pl
from jax.experimental.pallas import tpu as pltpu
from jax.sharding import PartitionSpec as P

norm_eps = 1e-05
MESH = pl.DeviceIdType.MESH
F32, BF16 = jnp.float32, jnp.bfloat16

CHIPS = (4, 2, 4, 2)
ARRAYS = (
    ((16, 640), "xyz"),
    ((16, 512), "yzx"),
    ((16, 1024), "zxy"),
    ((16, 2304), "xyz"),
    ((16, 2304), "yzx"),
    ((72, 512), "zxy"),
)


def position():
    s, f = lax.axis_index("seq"), lax.axis_index("fsdp")
    y, x_lo, z = lax.div(s, 8), lax.rem(lax.div(s, 4), 2), lax.rem(s, 4)
    x_hi, core = lax.div(f, 2), lax.rem(f, 2)
    return {"x": x_hi * 2 + x_lo, "y": y, "z": z}, core


def device(at, core):
    x_lo, x_hi = lax.rem(at["x"], 2), lax.div(at["x"], 2)
    return ((at["y"] * 2 + x_lo) * 4 + at["z"], x_hi * 2 + core)


def moved(at, axis, by):
    return {**at, axis: lax.rem(at[axis] + by, 4)}


def chip_index(at, whole):
    y = slice(None) if "y" in whole else pl.ds(at["y"], 1)
    z = slice(None) if "z" in whole else pl.ds(at["z"], 1)
    if "x" in whole:
        x_lo = x_hi = slice(None)
    else:
        x_lo, x_hi = pl.ds(lax.rem(at["x"], 2), 1), pl.ds(lax.div(at["x"], 2), 1)
    return (y, x_lo, z, x_hi)


def halves(columns):
    first = (columns // 128 + 1) // 2 * 128
    return slice(0, first), slice(first, columns)


def enter(at, core):
    barrier = pltpu.get_barrier_semaphore()
    for axis in "xyz":
        for by in (1, 3):
            pl.semaphore_signal(
                barrier, inc=1, device_id=device(moved(at, axis, by), core), device_id_type=MESH
            )
    pl.semaphore_signal(barrier, inc=1, device_id=device(at, 1 - core), device_id_type=MESH)
    pl.semaphore_wait(barrier, 7)


def remote(src, dst, sends, recvs, target, sem):
    return pltpu.make_async_remote_copy(
        src_ref=src,
        dst_ref=dst,
        send_sem=sends.at[sem],
        recv_sem=recvs.at[sem],
        device_id=target,
        device_id_type=MESH,
    )


def gather_kernel(*refs):
    count = len(ARRAYS)
    shards, (tok, cot) = refs[:count], refs[count : count + 2]
    full = refs[count + 2 : 2 * count + 2]
    out_half, down_half, tok_pair, cot_pair = refs[2 * count + 2 : 2 * count + 6]
    theirs = refs[2 * count + 6 : 3 * count + 6]
    block = refs[3 * count + 6 : 4 * count + 6]
    sends, recvs, local = refs[4 * count + 6 :]
    at, core = position()
    sibling = device(at, 1 - core)
    enter(at, core)
    sent, kept = [], []

    swaps = []
    for k in range(count):
        copy = remote(shards[k].at[1 - core], theirs[k], sends, recvs, sibling, 12 * count + k)
        copy.start()
        swaps.append(copy)
    pairs = []
    for k, (src, dst) in enumerate(((tok, tok_pair), (cot, cot_pair))):
        copy = remote(src, dst.at[core], sends, recvs, sibling, 13 * count + k)
        copy.start()
        pairs.append(copy)
        own = pltpu.make_async_copy(src, dst.at[core], local.at[count + k])
        own.start()
        kept.append(own)

    def send(k, src, dst, target, sem):
        copy = remote(src, dst, sends, recvs, target, sem)
        copy.start()
        sent.append(copy)

    def arrived(ref, sem):
        remote(ref, ref, sends, recvs, sibling, sem).wait_recv()

    own_copies = []
    for k in range(count):
        swaps[k].wait_recv()
        block[k][...] = shards_value(shards[k], core) + theirs[k][...]
        own = pltpu.make_async_copy(
            block[k], full[k].at[lax.div(lax.rem(at["y"], 4), 1), lax.rem(at["x"], 2), at["z"], lax.div(at["x"], 2)], local.at[k]
        )
        own.start()
        own_copies.append(own)
        axis = ARRAYS[k][1][0]
        here = (at["y"], lax.rem(at["x"], 2), at["z"], lax.div(at["x"], 2))
        base = 12 * k
        send(k, block[k], full[k].at[here], device(moved(at, axis, 1), core), base)
        send(k, block[k], full[k].at[here], device(moved(at, axis, 3), core), base + 1)

    for phase in range(3):
        for k, ((_, columns), order) in enumerate(ARRAYS):
            axis, whole, base = order[phase], order[:phase], 12 * k + 4 * phase
            first, second = halves(columns)
            right, left = moved(at, axis, 1), moved(at, axis, 3)
            from_left = full[k].at[chip_index(left, whole)]
            arrived(from_left, base)
            part = full[k].at[(*chip_index(left, whole), slice(None), first)]
            send(k, part, part, device(right, core), base + 2)
            from_right = full[k].at[chip_index(right, whole)]
            arrived(from_right, base + 1)
            part = full[k].at[(*chip_index(right, whole), slice(None), second)]
            send(k, part, part, device(left, core), base + 3)
        for k, ((_, columns), order) in enumerate(ARRAYS):
            axis, whole, base = order[phase], order[:phase], 12 * k + 4 * phase
            first, second = halves(columns)
            across = moved(at, axis, 2)
            arrived(full[k].at[(*chip_index(across, whole), slice(None), first)], base + 2)
            arrived(full[k].at[(*chip_index(across, whole), slice(None), second)], base + 3)
            if phase == 0:
                own_copies[k].wait()
            if phase < 2:
                axis, whole, base = order[phase + 1], order[: phase + 1], base + 4
                mine = full[k].at[chip_index(at, whole)]
                send(k, mine, mine, device(moved(at, axis, 1), core), base)
                send(k, mine, mine, device(moved(at, axis, 3), core), base + 1)
            elif k in (2, 5):
                columns = slice(512, 1024) if k == 2 else slice(0, 512)
                dst = out_half if k == 2 else down_half
                rest = (slice(None),) * 4
                mine = full[k].at[(pl.ds(2 * core, 2), *rest, columns)]
                other = full[k].at[(pl.ds(2 - 2 * core, 2), *rest, columns)]
                copy = remote(other, dst.at[core], sends, recvs, sibling, 13 * count + k)
                copy.start()
                pairs.append(copy)
                own = pltpu.make_async_copy(mine, dst.at[core], local.at[count + k])
                own.start()
                kept.append(own)

    for copy in sent:
        copy.wait_send()
    for copy in swaps:
        copy.wait_send()
    for copy in pairs:
        copy.wait()
    for copy in kept:
        copy.wait()


def shards_value(ref, core):
    return jnp.where(core == 0, ref[0], ref[1])


def gather(shards, tok, cot):
    count = len(ARRAYS)
    hbm, vmem = pl.BlockSpec(memory_space=pl.ANY), pl.BlockSpec(memory_space=pltpu.VMEM)
    outs = [jax.ShapeDtypeStruct((*CHIPS, *shape), BF16) for shape, _ in ARRAYS]
    outs += [
        jax.ShapeDtypeStruct((2, 2, 2, 4, 2, 16, 512), BF16),
        jax.ShapeDtypeStruct((2, 2, 2, 4, 2, 72, 512), BF16),
        jax.ShapeDtypeStruct((2, *tok.shape), F32),
        jax.ShapeDtypeStruct((2, *cot.shape), F32),
    ]
    blocks = [pltpu.VMEM(shape, BF16) for shape, _ in ARRAYS]
    return pl.pallas_call(
        gather_kernel,
        out_shape=outs,
        in_specs=[vmem] * count + [hbm] * 2,
        out_specs=[hbm] * len(outs),
        scratch_shapes=[
            *blocks,
            *blocks,
            pltpu.SemaphoreType.DMA((14 * count,)),
            pltpu.SemaphoreType.DMA((14 * count,)),
            pltpu.SemaphoreType.DMA((2 * count,)),
        ],
        compiler_params=pltpu.CompilerParams(
            collective_id=0, has_side_effects=True, vmem_limit_bytes=24 * 2**20
        ),
        name="gather_weights",
    )(*shards, tok, cot)


def reduce_kernel(*refs):
    count = len(ARRAYS)
    grads, (out_grad, down_grad) = refs[: count - 1], refs[count - 1 : count + 1]
    totals = refs[count + 1 : 2 * count + 1]
    data = refs[2 * count + 1 : 3 * count + 1]
    arriving = refs[3 * count + 1 : 15 * count + 1]
    sends, recvs, local = refs[15 * count + 1 :]
    at, core = position()
    sibling = device(at, 1 - core)
    enter(at, core)
    sent = []
    rest = (slice(None),) * 4

    def buffer(k, phase, which):
        return arriving[12 * k + 4 * phase + which]

    def send(src, dst, target, sem):
        copy = remote(src, dst, sends, recvs, target, sem)
        copy.start()
        sent.append(copy)

    def arrived(ref, sem):
        remote(ref, ref, sends, recvs, sibling, sem).wait_recv()

    loads = [[] for _ in range(count)]
    for k in range(count):
        if k < count - 1:
            dst = data[k].at[(*rest, slice(None), slice(0, 512))] if k == 2 else data[k]
            copy = pltpu.make_async_copy(grads[k], dst, local.at[k])
            copy.start()
            loads[k].append(copy)
        if k in (2, 5):
            columns = slice(512, 1024) if k == 2 else slice(0, 512)
            src = out_grad if k == 2 else down_grad
            dst = data[k].at[(pl.ds(2 * core, 2), *rest, columns)]
            copy = pltpu.make_async_copy(src.at[core], dst, local.at[count + k])
            copy.start()
            loads[k].append(copy)
            send(src.at[1 - core], dst, sibling, 12 * count + k)

    def add_part(k, into, source, where, leads, columns):
        sizes = source.shape[:4]

        def body(t, carry):
            i3 = lax.rem(t, sizes[3])
            t3 = lax.div(t, sizes[3])
            i2 = lax.rem(t3, sizes[2])
            t2 = lax.div(t3, sizes[2])
            i1 = lax.rem(t2, sizes[1])
            i0 = lax.div(t2, sizes[1])
            spot = tuple(i + b for i, b in zip((i0, i1, i2, i3), where))
            value = into[(*spot, slice(None), columns)].astype(F32)
            value = value + source[i0, i1, i2, i3].astype(F32)
            into[(*spot, slice(None), columns)] = value.astype(BF16)
            return carry

        lax.fori_loop(0, math.prod(sizes), body, 0)

    def add_both(k, into, one, two, where, total):
        sizes = one.shape[:4]

        def body(t, carry):
            i3 = lax.rem(t, sizes[3])
            t3 = lax.div(t, sizes[3])
            i2 = lax.rem(t3, sizes[2])
            t2 = lax.div(t3, sizes[2])
            i1 = lax.rem(t2, sizes[1])
            i0 = lax.div(t2, sizes[1])
            spot = tuple(i + b for i, b in zip((i0, i1, i2, i3), where))
            value = into[spot].astype(F32) + one[i0, i1, i2, i3].astype(F32)
            value = value + two[i0, i1, i2, i3].astype(F32)
            if total is None:
                into[spot] = value.astype(BF16)
            else:
                total[...] = value
            return carry

        lax.fori_loop(0, math.prod(sizes), body, 0)

    def start_of(position_, whole):
        y = 0 if "y" in whole else position_["y"]
        z = 0 if "z" in whole else position_["z"]
        if "x" in whole:
            return (y, 0, z, 0)
        return (y, lax.rem(position_["x"], 2), z, lax.div(position_["x"], 2))

    def first_sends(k, phase):
        (_, columns), order = ARRAYS[k]
        axis, whole = order[2 - phase], order[: 2 - phase]
        first, second = halves(columns)
        across = chip_index(moved(at, axis, 2), whole)
        base = 12 * k + 4 * phase
        for part, which, by in ((first, 0, 1), (second, 1, 3)):
            send(
                data[k].at[(*across, slice(None), part)],
                buffer(k, phase, which),
                device(moved(at, axis, by), core),
                base + which,
            )

    for k in range(count):
        for copy in loads[k]:
            copy.wait()
        if k in (2, 5):
            columns = slice(512, 1024) if k == 2 else slice(0, 512)
            arrived(data[k].at[(pl.ds(2 - 2 * core, 2), *rest, columns)], 12 * count + k)
        first_sends(k, 0)

    for phase in range(3):
        for k, ((_, columns), order) in enumerate(ARRAYS):
            axis, whole = order[2 - phase], order[: 2 - phase]
            base = 12 * k + 4 * phase
            for part, which, by in zip(halves(columns), (0, 1), (1, 3)):
                near = moved(at, axis, by)
                arrived(buffer(k, phase, which), base + which)
                add_part(k, data[k], buffer(k, phase, which), start_of(near, whole), None, part)
                send(
                    data[k].at[chip_index(near, whole)],
                    buffer(k, phase, 2 + which),
                    device(near, core),
                    base + 2 + which,
                )
        for k, ((_, columns), order) in enumerate(ARRAYS):
            axis, whole = order[2 - phase], order[: 2 - phase]
            base = 12 * k + 4 * phase
            arrived(buffer(k, phase, 2), base + 2)
            arrived(buffer(k, phase, 3), base + 3)
            last = phase == 2
            mine = totals[k].at[core] if last else None
            add_both(k, data[k], buffer(k, phase, 2), buffer(k, phase, 3), start_of(at, whole), mine)
            if not last:
                first_sends(k, phase + 1)
            else:
                send(mine, mine, sibling, 13 * count + k)
    for k in range(count):
        arrived(totals[k].at[1 - core], 13 * count + k)
    for copy in sent:
        copy.wait_send()


def reduce(grads, out_grad, down_grad):
    count = len(ARRAYS)
    hbm, vmem = pl.BlockSpec(memory_space=pl.ANY), pl.BlockSpec(memory_space=pltpu.VMEM)
    buffers = []
    for (rows, columns), order in ARRAYS:
        for phase in range(3):
            whole = order[: 2 - phase]
            lead = (
                4 if "y" in whole else 1,
                2 if "x" in whole else 1,
                4 if "z" in whole else 1,
                2 if "x" in whole else 1,
            )
            for part in halves(columns):
                buffers.append(pltpu.VMEM((*lead, rows, part.stop - part.start), BF16))
            buffers += [pltpu.VMEM((*lead, rows, columns), BF16)] * 2
    return pl.pallas_call(
        reduce_kernel,
        out_shape=[jax.ShapeDtypeStruct((2, *shape), F32) for shape, _ in ARRAYS],
        in_specs=[hbm] * (count + 1),
        out_specs=[vmem] * count,
        scratch_shapes=[
            *[pltpu.VMEM((*CHIPS, *shape), BF16) for shape, _ in ARRAYS],
            *buffers,
            pltpu.SemaphoreType.DMA((14 * count,)),
            pltpu.SemaphoreType.DMA((14 * count,)),
            pltpu.SemaphoreType.DMA((2 * count,)),
        ],
        compiler_params=pltpu.CompilerParams(
            collective_id=1, has_side_effects=True, vmem_limit_bytes=52 * 2**20
        ),
        name="sum_gradients",
    )(*grads, out_grad, down_grad)


def rms_inverse(values):
    return lax.rsqrt(jnp.mean(values * values, axis=-1, keepdims=True) + norm_eps)


def dot(a, b):
    return jnp.dot(a, b, preferred_element_type=F32)


def dot_t(a, b):
    return lax.dot_general(a, b, (((1,), (1,)), ((), ())), preferred_element_type=F32)


def t_dot(a, b):
    return lax.dot_general(a, b, (((0,), (0,)), ((), ())), preferred_element_type=F32)


def swap_pair(value):
    return lax.ppermute(value, "fsdp", [(0, 1), (1, 0), (2, 3), (3, 2)])


def shifted(value, by):
    peers = lax.axis_size("seq")
    return lax.ppermute(
        value, "seq", [(i, i + by) for i in range(peers) if 0 <= i + by < peers]
    )


def rows_for_pair(shard, core):
    rows = shard.shape[0]
    both = jnp.concatenate([shard, shard], axis=0)
    mine = lax.broadcasted_iota(jnp.int32, both.shape, 0) // rows == core
    return jnp.where(mine, both, jnp.zeros_like(both))


def shards(
    tokens,
    cotangent,
    norm1_gain,
    in_weight,
    conv_taps,
    out_weight,
    norm2_gain,
    gate_weight,
    up_weight,
    down_weight,
):
    width = tokens.shape[-1]
    inputs = tokens.reshape(-1, width)
    upstream = cotangent.reshape(-1, width)
    rows = inputs.shape[0]
    total_rows = rows * lax.axis_size("seq") * lax.axis_size("fsdp")
    factor = 1.0 / math.sqrt(total_rows)
    core = lax.rem(lax.axis_index("fsdp"), 2)

    small = jnp.concatenate(
        [norm1_gain[:, None], norm2_gain[:, None], conv_taps.T, jnp.zeros((8, 123), BF16)], axis=1
    )

    def by_half(*columns):
        return jnp.stack(
            [
                rows_for_pair(
                    jnp.concatenate(
                        [
                            c if c.shape[1] == 128 else c[:, h * c.shape[1] // 2 : (h + 1) * c.shape[1] // 2]
                            for c in columns
                        ],
                        axis=1,
                    ),
                    core,
                )
                for h in range(2)
            ]
        )

    b_w, c_w, x_w = in_weight[:, :width], in_weight[:, width : 2 * width], in_weight[:, 2 * width :]
    pieces = (
        by_half(b_w, small),
        by_half(c_w),
        by_half(x_w, out_weight),
        by_half(gate_weight),
        by_half(up_weight),
        by_half(down_weight),
    )
    full0, full1, full2, w_gate, w_up, _, w_out, w_down, tok, cot = gather(pieces, inputs, upstream)
    full0 = full0.reshape(width, -1)
    w_b, small = full0[:, :512], full0[:, 512:].T.astype(F32)
    w_c = full1.reshape(width, -1)
    w_x = full2.reshape(width, -1)[:, :512]
    w_gate = w_gate.reshape(width, -1)
    w_up = w_up.reshape(width, -1)
    w_out = w_out.reshape(2, 512, 512)
    w_down = w_down.reshape(2, 2304, 512)
    gain_one, gain_two = small[0], small[1]
    taps = lax.dynamic_slice_in_dim(small[2:5], core * 512, 512, axis=1)
    tok, cot = tok.reshape(-1, width), cot.reshape(-1, width)

    inv_one = rms_inverse(tok)
    normed_one = tok * inv_one
    hidden_one = (normed_one * gain_one).astype(BF16)
    b_mat, c_mat, x_mat = dot(hidden_one, w_b), dot(hidden_one, w_c), dot(hidden_one, w_x)
    gated = (b_mat * x_mat).reshape(2, rows, 512)
    padded = jnp.concatenate([shifted(gated[:, -2:], 1), gated], axis=1)
    convolved = taps[0] * padded[:, :-2] + taps[1] * padded[:, 1:-1] + taps[2] * padded[:, 2:]
    convolved = convolved.reshape(-1, 512)
    y_mat = (c_mat * convolved).astype(BF16)

    mixed = jnp.concatenate([dot(y_mat, w_out[0]), dot(y_mat, w_out[1])], axis=1)
    resid = tok + (mixed + swap_pair(mixed))
    inv_two = rms_inverse(resid)
    normed_two = resid * inv_two
    hidden_two = (normed_two * gain_two).astype(BF16)
    gate, up_vals = dot(hidden_two, w_gate), dot(hidden_two, w_up)
    sigma = jax.nn.sigmoid(gate)
    act = (gate * sigma * up_vals).astype(BF16)
    out_part = jnp.concatenate([dot(act, w_down[0]), dot(act, w_down[1])], axis=1)

    def own(value):
        return lax.dynamic_slice_in_dim(value, core * rows, rows, axis=0)

    def others(value):
        return lax.dynamic_slice_in_dim(value, (1 - core) * rows, rows, axis=0)

    block_out = own(resid) + (own(out_part) + swap_pair(others(out_part)))

    cot_half = cot.astype(BF16)
    g_down = jnp.stack([t_dot(act, cot_half[:, :512]), t_dot(act, cot_half[:, 512:])]).astype(BF16)
    d_act = dot_t(cot_half[:, :512], w_down[0]) + dot_t(cot_half[:, 512:], w_down[1])
    d_gate = (d_act * up_vals * sigma * (1.0 + gate * (1.0 - sigma))).astype(BF16)
    d_up = (d_act * gate * sigma).astype(BF16)
    g_gate = t_dot(hidden_two, d_gate).astype(BF16)
    g_up = t_dot(hidden_two, d_up).astype(BF16)
    d_hid2 = dot_t(d_gate, w_gate) + dot_t(d_up, w_up)
    d_hid2 = d_hid2 + swap_pair(d_hid2)

    g_norm2 = jnp.sum(d_hid2 * normed_two, axis=0)
    scaled = d_hid2 * gain_two
    d_resid = cot + inv_two * (
        scaled - normed_two * jnp.mean(scaled * normed_two, axis=-1, keepdims=True)
    )
    dres = d_resid.astype(BF16)
    g_out = jnp.stack([t_dot(y_mat, dres[:, :512]), t_dot(y_mat, dres[:, 512:])]).astype(BF16)
    d_y = dot_t(dres[:, :512], w_out[0]) + dot_t(dres[:, 512:], w_out[1])
    d_c = d_y * convolved
    d_conv = (d_y * c_mat).reshape(2, rows, 512)
    g_taps = [
        jnp.sum(d_conv * padded[:, :-2], axis=(0, 1)),
        jnp.sum(d_conv * padded[:, 1:-1], axis=(0, 1)),
        jnp.sum(d_conv * padded[:, 2:], axis=(0, 1)),
    ]
    after = jnp.concatenate([d_conv, shifted(d_conv[:, :2], -1)], axis=1)
    d_gated = taps[0] * after[:, 2:] + taps[1] * after[:, 1:-1] + taps[2] * after[:, :-2]
    d_gated = d_gated.reshape(-1, 512)
    d_b, d_c, d_x = (
        (d_gated * x_mat).astype(BF16),
        d_c.astype(BF16),
        (d_gated * b_mat).astype(BF16),
    )
    g_b, g_c, g_x = (t_dot(hidden_one, d).astype(BF16) for d in (d_b, d_c, d_x))
    d_hid1_part = dot_t(d_b, w_b) + dot_t(d_c, w_c) + dot_t(d_x, w_x)
    g_norm1 = jnp.sum(d_hid1_part * normed_one, axis=0)
    d_hid1 = own(d_hid1_part) + swap_pair(others(d_hid1_part))
    scaled = d_hid1 * gain_one
    own_normed = own(normed_one)
    input_grad = own(d_resid) + own(inv_one) * (
        scaled - own_normed * jnp.mean(scaled * own_normed, axis=-1, keepdims=True)
    )

    tap_rows = lax.dynamic_update_slice(
        jnp.zeros((3, width), F32), jnp.stack(g_taps), (0, core * 512)
    )
    g_small = jnp.concatenate(
        [g_norm1[None], g_norm2[None] * 0.5, tap_rows, jnp.zeros((123, width), F32)], axis=0
    )
    grads = (
        jnp.concatenate([g_b, g_small.T.astype(BF16)], axis=1).reshape(*CHIPS, 16, 640),
        g_c.reshape(*CHIPS, 16, 512),
        g_x.reshape(*CHIPS, 16, 512),
        g_gate.reshape(*CHIPS, 16, 2304),
        g_up.reshape(*CHIPS, 16, 2304),
    )
    totals = reduce(
        grads, g_out.reshape(2, 2, 2, 4, 2, 16, 512), g_down.reshape(2, 2, 2, 4, 2, 72, 512)
    )

    def whole(total, columns=slice(None)):
        count = total.shape[1] // 2
        mine = lax.dynamic_slice_in_dim(total, core * count, count, axis=1)[:, :, columns]
        return jnp.concatenate([mine[0], mine[1]], axis=1) * factor

    t_b, t_c, t_x, t_gate, t_up, t_down = totals
    count = 8
    t_small = lax.dynamic_slice_in_dim(t_b[0] + t_b[1], core * count, count, axis=0)[:, 512:] * factor
    left = slice(0, 512)
    return (
        block_out.reshape(tokens.shape),
        input_grad.reshape(tokens.shape),
        t_small[:, 0],
        jnp.concatenate([whole(t_b, left), whole(t_c), whole(t_x, left)], axis=1),
        t_small[:, 2:5].T,
        whole(t_x, slice(512, 1024)),
        t_small[:, 1],
        whole(t_gate),
        whole(t_up),
        whole(t_down),
    )


def solution(mesh):
    tokens = P("fsdp", "seq", None)
    vector, matrix, taps = P(("seq", "fsdp")), P(("seq", "fsdp"), None), P(None, ("seq", "fsdp"))
    weights = (vector, matrix, taps, matrix, vector, matrix, matrix, matrix)
    return jax.shard_map(
        shards,
        mesh=mesh,
        in_specs=(tokens, tokens, *weights),
        out_specs=(tokens, tokens, *weights),
        check_vma=False,
    )
```

time: 1180 us -> 324 us (0.27)
  blocking collectives: 491 us -> 0 us
  waiting for transfers between devices: 391 us -> 2.16 us
  Pallas kernels: 0 us -> 183 us
  starting transfers between devices: 112 us -> 4.3 us
  matrix products: 72.7 us -> 52 us
  other arithmetic: 46.7 us -> 29.1 us
  between operations: 17.4 us -> 1.69 us
    unnamed x2 -> x0, blocking collectives: 289 us -> none
    all_gather x3 -> x0, blocking collectives: 202 us -> none  [the longest x1 70.7 us: shards(): lax.all_gather(out_weight, 'seq', axis=0, tiled=True)]
    pallas_call x0 -> x2, Pallas kernels: none -> 183 us  [the longest x1 91.4 us: reduce(): pl.pallas_call(reduce_kernel, out_shape=[jax.ShapeDtypeStruct((2, *shape)...]
    all_gather x3 -> x0, waiting for transfers between devices: 160 us -> none  [the longest x1 145 us: shards(): lax.all_gather(down_weight, 'seq', axis=0, tiled=True)]
    all_to_all x10 -> x0, waiting for transfers between devices: 118 us -> none  [the longest x3 89 us: summed_on_arrival(): lax.all_to_all(parts, axis, split_axis=0, concat_axis=0, tiled=True)]
    psum x1 -> x0, waiting for transfers between devices: 106 us -> none  [shards(): lax.psum(mixed + own_slot * inputs[None], 'fsdp').reshape(-1, width)]
    all_to_all x10 -> x0, starting transfers between devices: 100 us -> none  [the longest x4 54.5 us: side_by_side(): lax.all_to_all(both, axis, split_axis=split_dim, concat_axis=concat_dim,...]
    dot_general x15 -> x27, matrix products: 72.7 us -> 52 us  [the longest x9 20.8 us: dot(): return jnp.dot(a, b, preferred_element_type=F32)]
  transfers between devices with their start and end apart: 22 -> 6, of which waited for: 14 -> 1; matrix products, arithmetic and copies ran while one was open for 23% -> 11% of each run, Pallas kernels for 0% -> 0%
where the time goes in v1:
time: 324 us; the launch traced here: 318 us
  Pallas kernels  183 us (56%)
  matrix products  52 us (16%)
  local copies, waits for them, and re-layouts  45.8 us (14%)
  other arithmetic  29.1 us (9%)
  starting transfers between devices  4.3 us (1%)
    pallas_call x1, Pallas kernels, reduce(): pl.pallas_call(reduce_kernel, out_shape=[jax.ShapeDtypeStruct((2, *shape)...  91.4 us
    pallas_call x1, Pallas kernels, gather(): pl.pallas_call(gather_kernel, out_shape=outs, in_specs=[vmem] * count + [...  91.2 us
    unnamed x109, local copies, waits for them, and re-layouts  26.3 us
    dot_general x9, matrix products, dot(): return jnp.dot(a, b, preferred_element_type=F32)  20.8 us
    dot_general x9, matrix products, t_dot(): lax.dot_general(a, b, (((0,), (0,)), ((), ())), preferred_element_type=F32)  16.6 us
    dot_general x9, matrix products, dot_t(): lax.dot_general(a, b, (((1,), (1,)), ((), ())), preferred_element_type=F32)  14.6 us
  transfers between devices with their start and end apart: 6, of which 1 were waited for; matrix products, arithmetic and copies ran while one was open for 11% of the time, Pallas kernels for 0%

profile of v1, /device:TPU:1, one launch (start us, length us, event | category | flops | bytes accessed | tf_op | source)
XLA Modules:
  0.0 317.6 jit_solution(13477685467406748172)
XLA Ops:
  7.1 91.2 %gather_weights.1 = (bf16[4,2,4,2,16,640]{5,4,3,2,1,0:T(8,128)(2,1)S(1)}, bf16[4,2,4,2,16,512]{5,4,3,2,1,0:T(8,128)(2,1)S(1)}, bf16[4,2,4,2,16,1024]{5,4,3,2,1,0...) custom-call(bf16[2,16,640]{2,1,0:T(8,128)(2,1)S(1)} %pad_maximum_fus, ...), custom_call_target="tpu_custom_call" | custom-call | tf_op jit(solution)/shard_map/gather_weights/pallas_call | solution.py:192
  98.3 1.3 copy-done
  99.7 2.2 copy-done.2
  101.8 2.2 copy-done.3
  104.0 1.0 copy-done.4
  106.0 1.3 copy-done.10
  107.3 2.2 copy-done.13
  110.2 1.8 copy.77
  112.0 1.0 convert_bitcast_fusion
  114.0 1.9 copy.61
  115.9 3.3 %multiply_convert_fusion.4 = (bf16[512,1024]{0,1:T(8,128)(2,1)S(1)}, f32[512,1024]{0,1:T(8,128)}) fusion(f32[1024]{0:T(1024)S(1)} %bitcast.208, f32[512,1024]{0,1:T(8,128)} %copy.61, f32[512]{0:T(512)S(1)} %bitcast.225), kind=kLoop, calls=%fused_computation.23 | loop fusion | flops 1572864 | bytes 5249024 | tf_op jit(solution)/shard_map/convert_element_type | solution.py:485
  120.2 1.7 fusion.54
  122.9 1.4 collective-permute-start
  125.1 1.2 multiply_convert_fusion.5
  126.3 2.4 fusion.49
  129.9 1.7 fusion.13
  133.4 1.5 pad_maximum_fusion.1
  136.1 1.8 copy.64
  138.2 2.7 fusion.48
  140.8 1.4 fusion.30
  142.3 1.5 convolution_add_fusion
  144.6 2.5 multiply_reduce_fusion.3
  147.4 4.4 %fusion.57 = f32[512,2304]{1,0:T(8,128)} fusion(bf16[512,1024]{0,1:T(8,128)(2,1)S(1)} %multiply_convert_fusion.3, bf16[1024,2304]{1,0:T(8,128)(2,1)S(1)} %bitcast.170), kind=kOutput, calls=%fused_computation.180 | convolution fusion | flops 2415919104 | bytes 10485760 | tf_op jit(solution)/shard_map/dot_general | solution.py:391
  151.8 8.4 %multiply_convert_fusion = (bf16[512,2304]{1,0:T(8,128)(2,1)}, bf16[512,2304]{1,0:T(8,128)(2,1)}, bf16[512,2304]{1,0:T(8,128)(2,1)S(1)}) fusion(f32[512,2304]{1,0:T(8,128)S(1)} %convolution_add_fusion, f32[512,2304]{1,0:T(8,128)} %fusion.57, bf16[512,1024]{0,1:T(8,128)(2,1)S(1)} %multiply_convert_fusion.3, bf16[1024,2304]{1,0:T(8,128)(2,1)S(1)} %bitcast.183), kind=kOutput, calls=%fused_computation.4 | convolution fusion | flops 2434793472 | bytes 22282240 | tf_op jit(solution)/shard_map/dot_general | solution.py:391
  160.3 1.4 fusion.59
  161.7 1.4 fusion.58
  163.4 2.6 fusion.60
  166.0 4.0 %convolution_add_fusion.1 = f32[512,1024]{0,1:T(8,128)} fusion(f32[512,1024]{0,1:T(8,128)S(1)} %fusion.60, bf16[512,2304]{1,0:T(8,128)(2,1)S(1)} %copy-done.46, bf16[1024,2304]{1,0:T(8,128)(2,1)S(1)} %bitcast.171), kind=kOutput, calls=%fused_computation.26 | convolution fusion | flops 2416443392 | bytes 11272192 | tf_op jit(solution)/shard_map/dot_general | solution.py:395
  170.5 1.4 convolution_convert_fusion.3
  172.2 1.4 copy-done.43
  173.6 1.4 convolution_convert_fusion.2
  175.0 2.6 pad_maximum_fusion.refs_6_
  177.6 4.5 %convolution_convert_fusion = bf16[1024,2304]{1,0:T(8,128)(2,1)} fusion(bf16[512,1024]{0,1:T(8,128)(2,1)S(1)} %multiply_convert_fusion.3, bf16[512,2304]{1,0:T(8,128)(2,1)S(1)} %copy-done.46), kind=kOutput, calls=%fused_computation | convolution fusion | flops 2418278400 | bytes 8126464 | tf_op jit(solution)/shard_map/dot_general | solution.py:399
  182.1 4.2 %convolution_convert_fusion.1 = bf16[1024,2304]{1,0:T(8,128)(2,1)} fusion(bf16[512,1024]{0,1:T(8,128)(2,1)S(1)} %multiply_convert_fusion.3, bf16[512,2304]{1,0:T(8,128)(2,1)S(1)} %copy-done.45), kind=kOutput, calls=%fused_computation.1 | convolution fusion | flops 2418278400 | bytes 8126464 | tf_op jit(solution)/shard_map/dot_general | solution.py:399
  186.2 1.4 fusion.9
  187.6 2.5 copy.69
  190.1 3.1 multiply_reduce_fusion
  193.2 4.3 %fusion.47 = (bf16[512,1024]{0,1:T(8,128)(2,1)S(1)}, f32[512,1024]{0,1:T(8,128)}) fusion(f32[512,1024]{0,1:T(8,128)S(1)} %copy-done.26, f32[512]{0:T(512)S(1)} %broadcast_multiply_fusion.1, f32[512,1024]{0,1:T(8,128)S(1)} %get-tuple-element.80, f32[1024]{0:T(1024)S(1)} %bitcast.214, f32[512,1024]{0,1:T(8,128)} %convolution_add_fusion.1, ...), kind=kLoop, calls=%fused_computation.170 | loop fusion | flops 4194304 | bytes 11542528 | tf_op jit(solution)/shard_map/convert_element_type | solution.py:526
  201.8 1.7 convolution_convert_fusion.5
  204.6 1.3 collective-permute-start.4
  205.9 1.1 pad_maximum_fusion.5.refs_5_
  207.1 2.2 collective-permute-done.4
  211.5 1.7 convolution_convert_fusion.4
  213.3 2.3 multiply_reduce_fusion.1
  215.8 1.7 copy.68
  217.6 91.4 %sum_gradients.1 = (f32[2,16,640]{2,1,0:T(8,128)S(1)}, f32[2,16,512]{2,1,0:T(8,128)S(1)}, f32[2,16,1024]{2,1,0:T(8,128)S(1)}, f32[2,16,2304]{2,1,0:T(8,128)S(1)}...) custom-call(bf16[4,2,4,2,16,640]{5,4,3,2,1,0:T(8,128)(2,1)} %bitcast.194, ...), custom_call_target="tpu_custom_call" | custom-call | tf_op jit(solution)/shard_map/sum_gradients/pallas_call | solution.py:367
  310.5 1.4 constant_dynamic-slice_fusion.1
  316.1 1.3 copy.70
  (195 shorter events, 31.4 us)
Async XLA Ops:
  4.7 2.4 copy-start.8
  4.7 2.4 copy-start.9
  98.3 1.3 copy-start
  99.7 2.2 copy-start.2
  101.8 2.2 copy-start.3
  106.0 1.3 copy-start.10
  107.3 2.2 copy-start.13
  115.9 3.3 %copy-start.11 = (bf16[4,2,4,2,16,1024]{5,4,3,2,1,0:T(8,128)(2,1)S(1)}, bf16[4,2,4,2,16,1024]{5,4,3,2,1,0:T(8,128)(2,1)}, u32[]{:S(2)}) copy-start(bf16[4,2,4,2,16,1024]{5,4,3,2,1,0:T(8,128)(2,1)} %copy-done.10) | copy-start | bytes 6291460
  120.2 1.7 copy-start.36
  122.9 5.9 %collective-permute-start = (f32[2,2,512]{2,1,0:T(2,128)S(1)}, f32[2,2,512]{2,1,0:T(2,128)S(1)}, u32[]{:S(2)}, u32[]{:S(2)}) collective-permute-start(f32[2,2,512]{2,1,0:T(2,128)S(1)} %slice.268), channel_id=1, source_target_pairs={{0,4},{4,8},{8,12},{12,16},{16,20},{20,24},{24,28},{28,32},{32,36}... | collective-permute-start | bytes 24584 | tf_op jit(solution)/shard_map/ppermute | solution.py:408
  126.3 2.5 copy-start.17
  126.3 2.9 copy-start.5
  129.1 2.5 copy-start.24
  129.9 1.7 copy-start.32
  131.7 1.2 copy-start.30
  132.2 2.8 copy-start.20
  133.4 1.7 copy-start.22
  133.4 2.7 copy-start.1
  135.1 8.8 %collective-permute-start.1 = (f32[512,1024]{0,1:T(8,128)}, f32[512,1024]{0,1:T(8,128)}, u32[]{:S(2)}, u32[]{:S(2)}) collective-permute-start(f32[512,1024]{0,1:T(8,128)} %pad_maximum_fusion.1), channel_id=1, source_target_pairs={{0,1},{1,0},{2,3},{3,2},{4,5},{5,4},{6,7},{7,6},{8,9},{9,8},{10,11... | collective-permute-start | bytes 6291464 | tf_op jit(solution)/shard_map/ppermute | solution.py:403
  142.3 5.1 %slice-start = ((s8[4718592]{0:T(1024)(128)(4,1)}), s8[4194304]{0:T(1024)(128)(4,1)S(1)}, s32[]{:S(2)}) async-start(s8[4718592]{0:T(1024)(128)(4,1)} %bitcast.168), calls=%async_computation | async-start | bytes 8388608
  142.3 1.7 copy-start.14
  142.3 2.0 copy-start.21
  142.3 2.3 copy-start.23
  142.3 5.1 %slice-start.1 = ((s8[4718592]{0:T(1024)(128)(4,1)}), s8[524288]{0:T(1024)(128)(4,1)S(1)}, s32[]{:S(2)}) async-start(s8[4718592]{0:T(1024)(128)(4,1)} %bitcast.168), calls=%async_computation.1 | async-start | bytes 1048576
  147.1 4.7 %slice-start.2 = ((s8[4718592]{0:T(1024)(128)(4,1)}), s8[4194304]{0:T(1024)(128)(4,1)S(1)}, s32[]{:S(2)}) async-start(s8[4718592]{0:T(1024)(128)(4,1)} %bitcast.181), calls=%async_computation.2 | async-start | bytes 8388608
  147.4 4.4 %slice-start.3 = ((s8[4718592]{0:T(1024)(128)(4,1)}), s8[524288]{0:T(1024)(128)(4,1)S(1)}, s32[]{:S(2)}) async-start(s8[4718592]{0:T(1024)(128)(4,1)} %bitcast.181), calls=%async_computation.3 | async-start | bytes 1048576
  160.2 10.2 %copy-start.42 = (bf16[512,2304]{1,0:T(8,128)(2,1)}, bf16[512,2304]{1,0:T(8,128)(2,1)S(1)}, u32[]{:S(2)}) copy-start(bf16[512,2304]{1,0:T(8,128)(2,1)S(1)} %get-tuple-element.85) | copy-start | bytes 7077892
  161.7 1.7 copy-start.44
  163.4 2.6 copy-start.46
  170.0 20.1 %collective-permute-start.3 = (f32[512,1024]{0,1:T(8,128)}, f32[512,1024]{0,1:T(8,128)}, u32[]{:S(2)}, u32[]{:S(2)}) collective-permute-start(f32[512,1024]{0,1:T(8,128)} %convolution_add_fusion.1), channel_id=1, source_target_pairs={{0,1},{1,0},{2,3},{3,2},{4,5},{5,4},{6,7},{7,6},{8,9},{9,8},{10,11... | collective-permute-start | bytes 6291464 | tf_op jit(solution)/shard_map/ppermute | solution.py:403
  171.9 1.7 copy-start.43
  172.0 14.2 %collective-permute-start.2 = (f32[256,1024]{0,1:T(8,128)S(1)}, f32[256,1024]{0,1:T(8,128)S(1)}, u32[]{:S(2)}, u32[]{:S(2)}) collective-permute-start(f32[256,1024]{0,1:T(8,128)S(1)} %fusion.5), channel_id=1, source_target_pairs={{0,1},{1,0},{2,3},{3,2},{4,5},{5,4},{6,7},{7,6},{8,9},{9,8},{10,11... | collective-permute-start | bytes 3145736 | tf_op jit(solution)/shard_map/ppermute | solution.py:403
  177.6 4.5 %copy-start.45 = (bf16[512,2304]{1,0:T(8,128)(2,1)S(1)}, bf16[512,2304]{1,0:T(8,128)(2,1)}, u32[]{:S(2)}) copy-start(bf16[512,2304]{1,0:T(8,128)(2,1)} %get-tuple-element.84) | copy-start | bytes 7077892
  190.1 3.1 copy-start.26
  193.2 4.3 %copy-start.29 = (bf16[512,512]{1,0:T(8,128)(2,1)S(1)}, bf16[512,512]{1,0:T(8,128)(2,1)}, u32[]{:S(2)}) copy-start(bf16[512,512]{1,0:T(8,128)(2,1)} %copy-done.28) | copy-start | bytes 1572868
  198.1 1.3 copy-start.18
  198.1 1.4 copy-start.33
  198.1 1.7 copy-start.40
  200.5 1.3 copy-start.35
  201.8 1.7 copy-start.6
  204.6 4.6 %collective-permute-start.4 = (f32[2,2,512]{2,1,0:T(2,128)S(1)}, f32[2,2,512]{2,1,0:T(2,128)S(1)}, u32[]{:S(2)}, u32[]{:S(2)}) collective-permute-start(f32[2,2,512]{2,1,0:T(2,128)S(1)} %slice.276), channel_id=1, source_target_pairs={{4,0},{8,4},{12,8},{16,12},{20,16},{24,20},{28,24},{32,28},{36,32}... | collective-permute-start | bytes 24584 | tf_op jit(solution)/shard_map/ppermute | solution.py:408
  205.9 3.6 %copy-start.37 = (f32[512,512]{1,0:T(8,128)S(1)}, f32[512,512]{1,0:T(8,128)}, u32[]{:S(2)}) copy-start(f32[512,512]{1,0:T(8,128)} %copy-done.36) | copy-start | bytes 3145732
  205.9 3.6 %copy-start.38 = (f32[512,512]{1,0:T(8,128)S(1)}, f32[512,512]{1,0:T(8,128)}, u32[]{:S(2)}) copy-start(f32[512,512]{1,0:T(8,128)} %get-tuple-element.143) | copy-start | bytes 3145732
  210.8 2.4 copy-start.15
  211.5 1.7 copy-start.12
  310.5 4.9 %copy-start.19 = (f32[512,1024]{0,1:T(8,128)S(1)}, f32[512,1024]{0,1:T(8,128)}, u32[]{:S(2)}) copy-start(f32[512,1024]{0,1:T(8,128)} %get-tuple-element.148) | copy-start | bytes 6291460
  312.0 3.5 %collective-permute-start.5 = (f32[256,1024]{0,1:T(8,128)S(1)}, f32[256,1024]{0,1:T(8,128)S(1)}, u32[]{:S(2)}, u32[]{:S(2)}) collective-permute-start(f32[256,1024]{0,1:T(8,128)S(1)} %constant_dynamic-slice_fusion.1), channel_id=1, source_target_pairs={{0,1},{1,0},{2,3},{3,2},{4,5},{5,4},{6,7},{7,6},{8,9},{9,8},{10,11... | collective-permute-start | bytes 3145736 | tf_op jit(solution)/shard_map/ppermute | solution.py:403
  312.8 3.0 copy-start.27
  (9 other events, 9.0 us)

commit v2 on v1

v2 whole, which is shorter than its diff:
```python
import math

import jax
import jax.numpy as jnp
from jax import lax
from jax.experimental import pallas as pl
from jax.experimental.pallas import tpu as pltpu
from jax.sharding import PartitionSpec as P

norm_eps = 1e-05
MESH = pl.DeviceIdType.MESH
F32, BF16 = jnp.float32, jnp.bfloat16

CHIPS = (4, 2, 4, 2)
ARRAYS = (
    ((16, 640), "xyz"),
    ((16, 512), "yzx"),
    ((16, 1024), "zxy"),
    ((16, 2304), "xyz"),
    ((16, 2304), "yzx"),
    ((72, 512), "zxy"),
)


def position():
    s, f = lax.axis_index("seq"), lax.axis_index("fsdp")
    y, x_lo, z = lax.div(s, 8), lax.rem(lax.div(s, 4), 2), lax.rem(s, 4)
    x_hi, core = lax.div(f, 2), lax.rem(f, 2)
    return {"x": x_hi * 2 + x_lo, "y": y, "z": z}, core


def device(at, core):
    x_lo, x_hi = lax.rem(at["x"], 2), lax.div(at["x"], 2)
    return ((at["y"] * 2 + x_lo) * 4 + at["z"], x_hi * 2 + core)


def moved(at, axis, by):
    return {**at, axis: lax.rem(at[axis] + by, 4)}


def chip_index(at, whole):
    y = slice(None) if "y" in whole else pl.ds(at["y"], 1)
    z = slice(None) if "z" in whole else pl.ds(at["z"], 1)
    if "x" in whole:
        x_lo = x_hi = slice(None)
    else:
        x_lo, x_hi = pl.ds(lax.rem(at["x"], 2), 1), pl.ds(lax.div(at["x"], 2), 1)
    return (y, x_lo, z, x_hi)


def halves(columns):
    first = (columns // 128 + 1) // 2 * 128
    return slice(0, first), slice(first, columns)


def enter(at, core):
    barrier = pltpu.get_barrier_semaphore()
    for axis in "xyz":
        for by in (1, 3):
            pl.semaphore_signal(
                barrier, inc=1, device_id=device(moved(at, axis, by), core), device_id_type=MESH
            )
    for other in (device(at, 1 - core), next_block(1), next_block(31)):
        pl.semaphore_signal(barrier, inc=1, device_id=other, device_id_type=MESH)
    pl.semaphore_wait(barrier, 9)


def next_block(by):
    return (lax.rem(lax.axis_index("seq") + by, 32), lax.axis_index("fsdp"))


def remote(src, dst, sends, recvs, target, sem):
    return pltpu.make_async_remote_copy(
        src_ref=src,
        dst_ref=dst,
        send_sem=sends.at[sem],
        recv_sem=recvs.at[sem],
        device_id=target,
        device_id_type=MESH,
    )


def dot(a, b):
    return jnp.dot(a, b, preferred_element_type=F32)


def dot_t(a, b):
    return lax.dot_general(a, b, (((1,), (1,)), ((), ())), preferred_element_type=F32)


def t_dot(a, b):
    return lax.dot_general(a, b, (((0,), (0,)), ((), ())), preferred_element_type=F32)


def flat(value):
    return value.reshape(-1, value.shape[-1])


def tile(j, size=256):
    return pl.ds(pl.multiple_of(j * size, size), size)


def rms_inverse(values):
    return lax.rsqrt(jnp.mean(values * values, axis=-1, keepdims=True) + norm_eps)


def steps(count, body):
    def run(i, carry):
        body(i)
        return carry

    lax.fori_loop(0, count, run, 0)


REST = (slice(None),) * 4
MIXER, FEED = (0, 1, 2), (3, 4, 5)
ROWS, WIDTH, HALF = 256, 1024, 512


def row_blocks(body, size=32):
    per = ROWS // size

    def run(i):
        body(lax.div(i, per), tile(lax.rem(i, per), size))

    steps(2 * per, run)


def picker():
    shape = (16, 128)
    same = lax.broadcasted_iota(jnp.int32, shape, 0) == lax.broadcasted_iota(jnp.int32, shape, 1)
    return jnp.where(same, 1.0, 0.0).astype(BF16)


def gather_kernel(*refs):
    count = len(ARRAYS)
    refs = list(refs)

    def take(n):
        taken = refs[:n]
        del refs[:n]
        return taken

    shards = take(count)
    tok, cot = take(2)
    w_b, w_c, w_x, out_half = take(4)
    feed_full = take(3)
    down_half, tok_pair, cot_pair = take(3)
    res, hid1, hid2, b_mat, c_mat, x_mat, gated, y_mat, small = take(9)
    theirs, block = take(count), take(count)
    full = take(3) + feed_full
    toks, mix, mix2, outw, halo = take(5)
    sends, recvs, local = refs
    at, core = position()
    sibling = device(at, 1 - core)
    enter(at, core)
    sent, kept = [], []

    def start(copy):
        copy.start()
        return copy

    def send(src, dst, target, sem):
        sent.append(start(remote(src, dst, sends, recvs, target, sem)))

    def arrived(ref, sem):
        remote(ref, ref, sends, recvs, sibling, sem).wait_recv()

    def keep(src, dst, sem):
        kept.append(start(pltpu.make_async_copy(src, dst, local.at[sem])))
        return kept[-1]

    for k in range(count):
        send(shards[k].at[1 - core], theirs[k], sibling, 12 * count + k)
    own_copies = []
    here = (at["y"], lax.rem(at["x"], 2), at["z"], lax.div(at["x"], 2))
    for k in range(count):
        arrived(theirs[k], 12 * count + k)
        block[k][...] = jnp.where(core == 0, shards[k][0], shards[k][1]) + theirs[k][...]
        own_copies.append(
            start(pltpu.make_async_copy(block[k], full[k].at[here], local.at[k]))
        )
        for by, sem in ((1, 0), (3, 1)):
            send(
                block[k],
                full[k].at[here],
                device(moved(at, ARRAYS[k][1][0], by), core),
                12 * k + sem,
            )
    send(tok, toks.at[core], sibling, 13 * count)
    own_tok = start(pltpu.make_async_copy(tok, toks.at[core], local.at[count]))
    send(cot, cot_pair.at[core], sibling, 13 * count + 1)
    keep(cot, cot_pair.at[core], count + 1)

    def pass_on(k, phase):
        (_, columns), order = ARRAYS[k]
        axis, whole, base = order[phase], order[:phase], 12 * k + 4 * phase
        right, left = moved(at, axis, 1), moved(at, axis, 3)
        for source, part, target, sem in zip((left, right), halves(columns), (right, left), (0, 1)):
            arrived(full[k].at[chip_index(source, whole)], base + sem)
            piece = full[k].at[(*chip_index(source, whole), slice(None), part)]
            send(piece, piece, device(target, core), base + 2 + sem)

    def complete(k, phase):
        (_, columns), order = ARRAYS[k]
        whole, base = order[:phase], 12 * k + 4 * phase
        across = moved(at, order[phase], 2)
        for part, sem in zip(halves(columns), (2, 3)):
            arrived(full[k].at[(*chip_index(across, whole), slice(None), part)], base + sem)
        if phase == 0:
            own_copies[k].wait()

    def begin(k, phase):
        order = ARRAYS[k][1]
        mine = full[k].at[chip_index(at, order[:phase])]
        for by, sem in ((1, 0), (3, 1)):
            send(mine, mine, device(moved(at, order[phase], by), core), 12 * k + 4 * phase + sem)

    def give_half(k, dst, columns):
        mine = full[k].at[(pl.ds(2 * core, 2), *REST, columns)]
        other = full[k].at[(pl.ds(2 - 2 * core, 2), *REST, columns)]
        send(other, dst.at[core], sibling, 13 * count + k)
        return start(pltpu.make_async_copy(mine, dst.at[core], local.at[count + k]))

    def each(step, arrays, phase):
        for k in arrays:
            step(k, phase)

    each(pass_on, MIXER, 0)
    each(pass_on, FEED, 0)
    each(complete, MIXER, 0)
    each(begin, MIXER, 1)
    each(complete, FEED, 0)
    each(begin, FEED, 1)
    each(pass_on, MIXER, 1)
    each(complete, MIXER, 1)
    each(begin, MIXER, 2)
    each(pass_on, FEED, 1)
    each(complete, FEED, 1)
    each(pass_on, MIXER, 2)
    each(begin, FEED, 2)
    each(complete, MIXER, 2)
    own_out = give_half(2, outw, slice(512, 1024))
    left = slice(0, 512)
    keep(full[0].at[(*REST, slice(None), left)], w_b, 18)
    keep(full[1], w_c, 19)
    keep(full[2].at[(*REST, slice(None), left)], w_x, 20)

    small[...] = dot_t(picker(), flat(full[0][:, :, :, :, :, 512:640]))
    own_tok.wait()
    arrived(toks.at[1 - core], 13 * count)
    keep(toks, tok_pair, 21)

    def norm_one(c, rows):
        t = toks[c, rows, :]
        hid1[c, rows, :] = (t * rms_inverse(t) * small[0:1, :]).astype(BF16)

    row_blocks(norm_one)

    def project(i):
        c, j = lax.div(i, 2), tile(lax.rem(i, 2))
        h = hid1[c]
        b = dot(h, flat(full[0][:, :, :, :, :, j]))
        x = dot(h, flat(full[2][:, :, :, :, :, j]))
        b_mat[c, :, j] = b
        x_mat[c, :, j] = x
        gated[c, pl.ds(8, ROWS), j] = b * x
        c_mat[c, pl.ds(0, ROWS), j] = dot(h, flat(full[1][:, :, :, :, :, j]))

    steps(4, project)
    send(gated.at[:, pl.ds(ROWS, 8), :], halo, next_block(1), 13 * count + 4)
    own_out.wait()
    arrived(outw.at[1 - core], 13 * count + 2)
    keep(outw, out_half, 22)
    arrived(halo, 13 * count + 4)
    starts = lax.axis_index("seq") == 0
    taps = [small[2 + i : 3 + i, tile(core, HALF)] for i in range(3)]
    for c in range(2):
        gated[c, 0:8, :] = jnp.where(starts, 0.0, halo[c])
        for r in range(0, ROWS, 64):
            conv = taps[0] * gated[c, r + 6 : r + 70, :]
            conv = conv + taps[1] * gated[c, r + 7 : r + 71, :]
            conv = conv + taps[2] * gated[c, r + 8 : r + 72, :]
            y_mat[c, r : r + 64, :] = (c_mat[c, r : r + 64, :] * conv).astype(BF16)

    def mixing(i):
        c, h, j = lax.div(i, 4), lax.rem(lax.div(i, 2), 2), lax.rem(i, 2)
        weight = outw[h, :, :, :, :, :, tile(j)]
        mix[c, :, tile(2 * h + j)] = dot(y_mat[c], flat(weight))

    steps(8, mixing)
    send(mix, mix2, sibling, 13 * count + 3)
    each(pass_on, FEED, 2)
    arrived(mix2, 13 * count + 3)

    def norm_two(c, rows):
        r = toks[c, rows, :] + (mix[c, rows, :] + mix2[c, rows, :])
        res[c, rows, :] = r
        hid2[c, rows, :] = (r * rms_inverse(r) * small[1:2, :]).astype(BF16)

    row_blocks(norm_two)
    each(complete, FEED, 2)
    give_half(5, down_half, slice(0, 512)).wait()
    arrived(down_half.at[1 - core], 13 * count + 5)
    arrived(cot_pair.at[1 - core], 13 * count + 1)
    for copy in sent:
        copy.wait_send()
    for copy in kept:
        copy.wait()


def gather(shards, tok, cot):
    count = len(ARRAYS)
    hbm, vmem = pl.BlockSpec(memory_space=pl.ANY), pl.BlockSpec(memory_space=pltpu.VMEM)
    shape = jax.ShapeDtypeStruct
    pair = (2, ROWS, WIDTH)
    outs = [shape((*CHIPS, 16, HALF), BF16)] * 3 + [shape((2, 2, 2, 4, 2, 16, HALF), BF16)]
    outs += [shape((*CHIPS, *ARRAYS[k][0]), BF16) for k in FEED]
    outs += [shape((2, 2, 2, 4, 2, 72, HALF), BF16), shape(pair, F32), shape(pair, F32)]
    in_hbm = len(outs)
    outs += [
        shape(pair, F32),
        shape(pair, BF16),
        shape(pair, BF16),
        shape((2, ROWS, HALF), F32),
        shape((2, ROWS + 8, HALF), F32),
        shape((2, ROWS, HALF), F32),
        shape((2, ROWS + 8, HALF), F32),
        shape((2, ROWS, HALF), BF16),
        shape((16, WIDTH), F32),
    ]
    blocks = [pltpu.VMEM(array, BF16) for array, _ in ARRAYS]
    return pl.pallas_call(
        gather_kernel,
        out_shape=outs,
        in_specs=[vmem] * count + [hbm] * 2,
        out_specs=[hbm] * 4 + [vmem] * 3 + [hbm] * (in_hbm - 7) + [vmem] * (len(outs) - in_hbm),
        scratch_shapes=[
            *blocks,
            *blocks,
            *[pltpu.VMEM((*CHIPS, *ARRAYS[k][0]), BF16) for k in MIXER],
            *[pltpu.VMEM(pair, F32)] * 3,
            pltpu.VMEM((2, 2, 2, 4, 2, 16, HALF), BF16),
            pltpu.VMEM((2, 8, HALF), F32),
            pltpu.SemaphoreType.DMA((14 * count,)),
            pltpu.SemaphoreType.DMA((14 * count,)),
            pltpu.SemaphoreType.DMA((24,)),
        ],
        compiler_params=pltpu.CompilerParams(
            collective_id=0, has_side_effects=True, vmem_limit_bytes=60 * 2**20
        ),
        name="gather_and_mix",
    )(*shards, tok, cot)


def reduce_kernel(*refs):
    count = len(ARRAYS)
    refs = list(refs)

    def take(n):
        taken = refs[:n]
        del refs[:n]
        return taken

    g_gate, g_up, g_down, d_hid2, in_hbm = *take(4), take(14)
    totals, (input_grad,) = take(count), take(1)
    data, arriving = take(count), take(12 * count)
    cot, res, hid1, b_mat, c_mat, x_mat, gated, y_mat, outw, small = held = take(10)
    dh, dh2, d1r, dres, g_out, halo = take(6)
    d_proj, (g_small,) = take(3), take(1)
    sends, recvs, local = refs
    at, core = position()
    sibling = device(at, 1 - core)
    enter(at, core)
    sent = []

    def send(src, dst, target, sem):
        copy = remote(src, dst, sends, recvs, target, sem)
        copy.start()
        sent.append(copy)

    def arrived(ref, sem):
        remote(ref, ref, sends, recvs, sibling, sem).wait_recv()

    def load(src, dst, sem):
        copy = pltpu.make_async_copy(src, dst, local.at[sem])
        copy.start()
        return copy

    def buffer(k, phase, which):
        return arriving[12 * k + 4 * phase + which]

    def add(k, phase, where, sources, columns, total=None):
        sizes = sources[0].shape[:4]

        def body(t):
            i3 = lax.rem(t, sizes[3])
            t3 = lax.div(t, sizes[3])
            i2 = lax.rem(t3, sizes[2])
            t2 = lax.div(t3, sizes[2])
            i1 = lax.rem(t2, sizes[1])
            i0 = lax.div(t2, sizes[1])
            spot = tuple(i + b for i, b in zip((i0, i1, i2, i3), where))
            value = data[k][(*spot, slice(None), columns)].astype(F32)
            for source in sources:
                value = value + source[i0, i1, i2, i3].astype(F32)
            if total is None:
                data[k][(*spot, slice(None), columns)] = value.astype(BF16)
            else:
                total[...] = value

        steps(math.prod(sizes), body)

    def start_of(place, whole):
        y = 0 if "y" in whole else place["y"]
        z = 0 if "z" in whole else place["z"]
        if "x" in whole:
            return (y, 0, z, 0)
        return (y, lax.rem(place["x"], 2), z, lax.div(place["x"], 2))

    def begin(k, phase):
        (_, columns), order = ARRAYS[k]
        axis, whole = order[2 - phase], order[: 2 - phase]
        across = chip_index(moved(at, axis, 2), whole)
        for part, which, by in zip(halves(columns), (0, 1), (1, 3)):
            send(
                data[k].at[(*across, slice(None), part)],
                buffer(k, phase, which),
                device(moved(at, axis, by), core),
                12 * k + 4 * phase + which,
            )

    def pass_on(k, phase):
        (_, columns), order = ARRAYS[k]
        axis, whole = order[2 - phase], order[: 2 - phase]
        base = 12 * k + 4 * phase
        for part, which, by in zip(halves(columns), (0, 1), (1, 3)):
            near = moved(at, axis, by)
            arrived(buffer(k, phase, which), base + which)
            add(k, phase, start_of(near, whole), [buffer(k, phase, which)], part)
            send(
                data[k].at[chip_index(near, whole)],
                buffer(k, phase, 2 + which),
                device(near, core),
                base + 2 + which,
            )

    def complete(k, phase):
        whole = ARRAYS[k][1][: 2 - phase]
        base = 12 * k + 4 * phase
        both = [buffer(k, phase, 2), buffer(k, phase, 3)]
        arrived(both[0], base + 2)
        arrived(both[1], base + 3)
        total = totals[k].at[core] if phase == 2 else None
        add(k, phase, start_of(at, whole), both, slice(None), total)
        if phase < 2:
            begin(k, phase + 1)
        else:
            send(total, total, sibling, 13 * count + k)

    def each(step, arrays, phase):
        for k in arrays:
            step(k, phase)

    mine = data[5].at[pl.ds(2 * core, 2)]
    send(g_down.at[1 - core], mine, sibling, 12 * count + 5)
    send(d_hid2, dh2, sibling, 12 * count)
    feed_loads = [
        load(g_gate, data[3], 3),
        load(g_up, data[4], 4),
        load(g_down.at[core], mine, 5),
    ]
    first_loads = [load(d_hid2, dh, 6)]
    first_loads += [load(in_hbm[i], held[i], 7 + i) for i in (0, 1, 9)]
    rest_loads = [load(in_hbm[i], held[i], 7 + i) for i in range(2, 9)]
    left = slice(0, HALF)
    for k in MIXER:
        dst = data[k] if k == 1 else data[k].at[(*REST, slice(None), left)]
        rest_loads.append(load(in_hbm[10 + k], dst, 17 + k))
    for k in FEED:
        feed_loads[k - 3].wait()
        if k == 5:
            arrived(data[5].at[pl.ds(2 - 2 * core, 2)], 12 * count + 5)
        begin(k, 0)
    for copy in first_loads:
        copy.wait()
    arrived(dh2, 12 * count)
    g_small[...] = jnp.zeros_like(g_small)

    def norm_two(c, rows):
        r = res[c, rows, :]
        inv = rms_inverse(r)
        normed = r * inv
        d = dh[c, rows, :] + dh2[c, rows, :]
        g_small[1:2, :] += 0.5 * jnp.sum(d * normed, axis=0, keepdims=True)
        scaled = d * small[1:2, :]
        mean = jnp.mean(scaled * normed, axis=-1, keepdims=True)
        out = cot[c, rows, :] + inv * (scaled - normed * mean)
        cot[c, rows, :] = out
        dres[c, rows, :] = out.astype(BF16)

    row_blocks(norm_two)
    tok_load = load(in_hbm[13], res, 20)
    each(pass_on, FEED, 0)
    for copy in rest_loads:
        copy.wait()

    taps = [small[2 + i : 3 + i, tile(core, HALF)] for i in range(3)]
    for c in range(2):
        for j in range(2):
            cols = slice(256 * j, 256 * j + 256)
            d_y = dot_t(dres[c, :, 0:HALF], flat(outw[0, j]))
            d_y = d_y + dot_t(dres[c, :, HALF:WIDTH], flat(outw[1, j]))
            conv = sum(taps[i][:, cols] * gated[c, 6 + i : 6 + i + ROWS, cols] for i in range(3))
            d_proj[1][c, :, cols] = (d_y * conv).astype(BF16)
            c_mat[c, 0:ROWS, cols] = d_y * c_mat[c, 0:ROWS, cols]
    send(c_mat.at[:, pl.ds(0, 8), :], halo, next_block(31), 12 * count + 3)

    def out_grad(i):
        f, j = lax.div(i, 2), lax.rem(i, 2)
        other = sum(
            t_dot(y_mat[c, :, tile(f)], dres[c, :, tile(2 - 2 * core + j)]) for c in range(2)
        )
        g_out[f, :, :, :, :, tile(j)] = other.astype(BF16).reshape(2, 4, 2, 16, 256)
        own = sum(t_dot(y_mat[c, :, tile(f)], dres[c, :, tile(2 * core + j)]) for c in range(2))
        data[2][2 * core + f, :, :, :, :, tile(2 + j)] = own.astype(BF16).reshape(2, 4, 2, 16, 256)

    steps(4, out_grad)
    right = slice(HALF, WIDTH)
    send(g_out, data[2].at[(pl.ds(2 * core, 2), *REST, right)], sibling, 12 * count + 2)
    arrived(halo, 12 * count + 3)
    ends = lax.axis_index("seq") == 31
    for c in range(2):
        c_mat[c, ROWS : ROWS + 8, :] = jnp.where(ends, 0.0, halo[c])
        for r in range(0, ROWS, 64):
            d_conv = c_mat[c, r : r + 64, :]
            for i in range(3):
                part = jnp.sum(
                    d_conv * gated[c, r + 6 + i : r + 70 + i, :], axis=0, keepdims=True
                )
                g_small[2 + i : 3 + i, tile(core, HALF)] += part
            d_gated = taps[0] * c_mat[c, r + 2 : r + 66, :]
            d_gated = d_gated + taps[1] * c_mat[c, r + 1 : r + 65, :] + taps[2] * d_conv
            d_proj[0][c, r : r + 64, :] = (d_gated * x_mat[c, r : r + 64, :]).astype(BF16)
            d_proj[2][c, r : r + 64, :] = (d_gated * b_mat[c, r : r + 64, :]).astype(BF16)

    def back(i):
        c, y = lax.div(i, 4), lax.rem(i, 4)
        value = None
        for k in MIXER:
            part = dot_t(d_proj[k][c], flat(data[k][y, :, :, :, :, 0:HALF]))
            value = part if value is None else value + part
        dh[c, :, tile(y)] = value

    steps(8, back)
    send(dh.at[1 - core], d1r, sibling, 12 * count + 1)

    def in_grad(i):
        y, j = lax.div(i, 2), tile(lax.rem(i, 2))
        for k in MIXER:
            value = sum(t_dot(hid1[c, :, tile(y)], d_proj[k][c, :, j]) for c in range(2))
            data[k][y, :, :, :, :, j] = value.astype(BF16).reshape(2, 4, 2, 16, 256)

    steps(8, in_grad)
    tok_load.wait()

    def gain_one(c, rows):
        t = res[c, rows, :]
        g_small[0:1, :] += jnp.sum(dh[c, rows, :] * (t * rms_inverse(t)), axis=0, keepdims=True)

    row_blocks(gain_one)
    turned = t_dot(g_small[...].astype(BF16), picker()).astype(BF16)
    data[0][:, :, :, :, :, HALF : HALF + 128] = turned.reshape(*CHIPS, 16, 128)
    arrived(data[2].at[(pl.ds(2 - 2 * core, 2), *REST, right)], 12 * count + 2)
    each(begin, MIXER, 0)
    each(complete, FEED, 0)
    each(pass_on, MIXER, 0)
    each(pass_on, FEED, 1)
    arrived(d1r, 12 * count + 1)

    def norm_one(i):
        rows = tile(i, 32)
        t = res[core, rows, :]
        inv = rms_inverse(t)
        normed = t * inv
        scaled = (dh[core, rows, :] + d1r[rows, :]) * small[0:1, :]
        mean = jnp.mean(scaled * normed, axis=-1, keepdims=True)
        input_grad[rows, :] = cot[core, rows, :] + inv * (scaled - normed * mean)

    steps(ROWS // 32, norm_one)
    each(complete, MIXER, 0)
    each(complete, FEED, 1)
    each(pass_on, MIXER, 1)
    each(pass_on, FEED, 2)
    each(complete, MIXER, 1)
    each(complete, FEED, 2)
    each(pass_on, MIXER, 2)
    each(complete, MIXER, 2)
    for k in range(count):
        arrived(totals[k].at[1 - core], 13 * count + k)
    for copy in sent:
        copy.wait_send()


def reduce(g_gate, g_up, g_down, d_hid2, *rest):
    count = len(ARRAYS)
    hbm, vmem = pl.BlockSpec(memory_space=pl.ANY), pl.BlockSpec(memory_space=pltpu.VMEM)
    buffers = []
    for (rows, columns), order in ARRAYS:
        for phase in range(3):
            whole = order[: 2 - phase]
            lead = (
                4 if "y" in whole else 1,
                2 if "x" in whole else 1,
                4 if "z" in whole else 1,
                2 if "x" in whole else 1,
            )
            for part in halves(columns):
                buffers.append(pltpu.VMEM((*lead, rows, part.stop - part.start), BF16))
            buffers += [pltpu.VMEM((*lead, rows, columns), BF16)] * 2
    pair = pltpu.VMEM((2, ROWS, WIDTH), F32)
    operands = (g_gate, g_up, g_down, d_hid2, *rest)
    return pl.pallas_call(
        reduce_kernel,
        out_shape=[jax.ShapeDtypeStruct((2, *shape), F32) for shape, _ in ARRAYS]
        + [jax.ShapeDtypeStruct((ROWS, WIDTH), F32)],
        in_specs=[hbm] * len(operands),
        out_specs=[vmem] * (count + 1),
        scratch_shapes=[
            *[pltpu.VMEM((*CHIPS, *shape), BF16) for shape, _ in ARRAYS],
            *buffers,
            *[pltpu.VMEM(value.shape, value.dtype) for value in rest[:10]],
            pair,
            pair,
            pltpu.VMEM((ROWS, WIDTH), F32),
            pltpu.VMEM((2, ROWS, WIDTH), BF16),
            pltpu.VMEM((2, 2, 4, 2, 16, HALF), BF16),
            pltpu.VMEM((2, 8, HALF), F32),
            *[pltpu.VMEM((2, ROWS, HALF), BF16)] * 3,
            pltpu.VMEM((16, WIDTH), F32),
            pltpu.SemaphoreType.DMA((14 * count,)),
            pltpu.SemaphoreType.DMA((14 * count,)),
            pltpu.SemaphoreType.DMA((24,)),
        ],
        compiler_params=pltpu.CompilerParams(
            collective_id=1, has_side_effects=True, vmem_limit_bytes=63 * 2**20
        ),
        name="sum_gradients",
    )(*operands)


def swap_pair(value):
    return lax.ppermute(value, "fsdp", [(0, 1), (1, 0), (2, 3), (3, 2)])


def rows_for_pair(shard, core):
    rows = shard.shape[0]
    both = jnp.concatenate([shard, shard], axis=0)
    mine = lax.broadcasted_iota(jnp.int32, both.shape, 0) // rows == core
    return jnp.where(mine, both, jnp.zeros_like(both))


def shards(
    tokens,
    cotangent,
    norm1_gain,
    in_weight,
    conv_taps,
    out_weight,
    norm2_gain,
    gate_weight,
    up_weight,
    down_weight,
):
    width = tokens.shape[-1]
    inputs = tokens.reshape(-1, width)
    upstream = cotangent.reshape(-1, width)
    rows = inputs.shape[0]
    total_rows = rows * lax.axis_size("seq") * lax.axis_size("fsdp")
    factor = 1.0 / math.sqrt(total_rows)
    core = lax.rem(lax.axis_index("fsdp"), 2)

    small = jnp.concatenate(
        [norm1_gain[:, None], norm2_gain[:, None], conv_taps.T, jnp.zeros((8, 123), BF16)], axis=1
    )

    def by_half(*columns):
        return jnp.stack(
            [
                rows_for_pair(
                    jnp.concatenate(
                        [
                            c if c.shape[1] == 128 else c[:, h * c.shape[1] // 2 : (h + 1) * c.shape[1] // 2]
                            for c in columns
                        ],
                        axis=1,
                    ),
                    core,
                )
                for h in range(2)
            ]
        )

    b_w, c_w, x_w = in_weight[:, :width], in_weight[:, width : 2 * width], in_weight[:, 2 * width :]
    pieces = (
        by_half(b_w, small),
        by_half(c_w),
        by_half(x_w, out_weight),
        by_half(gate_weight),
        by_half(up_weight),
        by_half(down_weight),
    )
    w_b, w_c, w_x, w_out, w_gate, w_up, _, w_down, tok, cot, *kept = gather(pieces, inputs, upstream)
    resid, hidden_one, hidden_two, b_mat, c_mat, x_mat, gated, y_mat, small = kept
    w_gate = w_gate.reshape(width, -1)
    w_up = w_up.reshape(width, -1)
    w_down = w_down.reshape(2, 2304, 512)
    hid2 = hidden_two.reshape(-1, width)
    gate, up_vals = dot(hid2, w_gate), dot(hid2, w_up)
    sigma = jax.nn.sigmoid(gate)
    act = (gate * sigma * up_vals).astype(BF16)
    out_part = jnp.concatenate([dot(act, w_down[0]), dot(act, w_down[1])], axis=1)

    def own(value):
        return lax.dynamic_slice_in_dim(value, core * rows, rows, axis=0)

    def others(value):
        return lax.dynamic_slice_in_dim(value, (1 - core) * rows, rows, axis=0)

    block_out = own(resid.reshape(-1, width)) + (own(out_part) + swap_pair(others(out_part)))

    cot_half = cot.reshape(-1, width).astype(BF16)
    g_down = jnp.stack([t_dot(act, cot_half[:, :512]), t_dot(act, cot_half[:, 512:])]).astype(BF16)
    d_act = dot_t(cot_half[:, :512], w_down[0]) + dot_t(cot_half[:, 512:], w_down[1])
    d_gate = (d_act * up_vals * sigma * (1.0 + gate * (1.0 - sigma))).astype(BF16)
    d_up = (d_act * gate * sigma).astype(BF16)
    g_gate = t_dot(hid2, d_gate).astype(BF16)
    g_up = t_dot(hid2, d_up).astype(BF16)
    d_hid2 = dot_t(d_gate, w_gate) + dot_t(d_up, w_up)
    *totals, input_grad = reduce(
        g_gate.reshape(*CHIPS, 16, 2304),
        g_up.reshape(*CHIPS, 16, 2304),
        g_down.reshape(2, 2, 2, 4, 2, 72, 512),
        d_hid2.reshape(2, rows, width),
        cot,
        resid,
        hidden_one,
        b_mat,
        c_mat,
        x_mat,
        gated,
        y_mat,
        w_out,
        small,
        w_b,
        w_c,
        w_x,
        tok,
    )

    def whole(total, columns=slice(None)):
        count = total.shape[1] // 2
        mine = lax.dynamic_slice_in_dim(total, core * count, count, axis=1)[:, :, columns]
        return jnp.concatenate([mine[0], mine[1]], axis=1) * factor

    t_b, t_c, t_x, t_gate, t_up, t_down = totals
    count = 8
    t_small = lax.dynamic_slice_in_dim(t_b[0] + t_b[1], core * count, count, axis=0)[:, 512:] * factor
    left = slice(0, 512)
    return (
        block_out.reshape(tokens.shape),
        input_grad.reshape(tokens.shape),
        t_small[:, 0],
        jnp.concatenate([whole(t_b, left), whole(t_c), whole(t_x, left)], axis=1),
        t_small[:, 2:5].T,
        whole(t_x, slice(512, 1024)),
        t_small[:, 1],
        whole(t_gate),
        whole(t_up),
        whole(t_down),
    )


def solution(mesh):
    tokens = P("fsdp", "seq", None)
    vector, matrix, taps = P(("seq", "fsdp")), P(("seq", "fsdp"), None), P(None, ("seq", "fsdp"))
    weights = (vector, matrix, taps, matrix, vector, matrix, matrix, matrix)
    return jax.shard_map(
        shards,
        mesh=mesh,
        in_specs=(tokens, tokens, *weights),
        out_specs=(tokens, tokens, *weights),
        check_vma=False,
    )
```

time: 324 us -> 290 us (0.90); the launches traced: 318 us -> 289 us
  Pallas kernels: 183 us -> 212 us
  local copies, waits for them, and re-layouts: 45.8 us -> 25.2 us
  matrix products: 52 us -> 35.3 us
  other arithmetic: 29.1 us -> 15.7 us
  starting transfers between devices: 4.3 us -> 0.01 us
    unnamed x109 -> x47, local copies, waits for them, and re-layouts: 26.3 us -> 9.41 us
    pallas_call x1, Pallas kernels: 91.2 us -> 107 us  [gather(): pl.pallas_call(gather_kernel, out_shape=outs, in_specs=[vmem] * count + [...]
    pallas_call x1, Pallas kernels: 91.4 us -> 106 us  [reduce(): pl.pallas_call(reduce_kernel, out_shape=[jax.ShapeDtypeStruct((2, *shape)...]
    dot_general x9 -> x4, matrix products: 20.8 us -> 8.07 us  [dot(): return jnp.dot(a, b, preferred_element_type=F32)]
    convert_element_type x9 -> x1, other arithmetic: 11 us -> 0.16 us  [shards(): cot_half = cot.reshape(-1, width).astype(BF16)]
    reduce_sum x5 -> x0, other arithmetic: 6.4 us -> none  [the longest x1 3.06 us: shards(): g_norm2 = jnp.sum(d_hid2 * normed_two, axis=0)]
    squeeze x6, local copies, waits for them, and re-layouts: 0.09 us -> 5.16 us  [whole(): return jnp.concatenate([mine[0], mine[1]], axis=1) * factor]
    slice x7 -> x0, local copies, waits for them, and re-layouts: 4.02 us -> none  [the longest x1 2.44 us: shards(): w_out[0]]
  transfers between devices with their start and end apart: 6 -> 1, of which waited for: 1 -> 0; matrix products, arithmetic and copies ran while one was open for 11% -> 13% of each run, Pallas kernels for 0% -> 36%
where the time goes in v2:
time: 290 us; the launch traced here: 289 us
  Pallas kernels  212 us (73%)
  matrix products  35.3 us (12%)
  local copies, waits for them, and re-layouts  25.2 us (9%)
  other arithmetic  15.7 us (5%)
    pallas_call x1, Pallas kernels, gather(): pl.pallas_call(gather_kernel, out_shape=outs, in_specs=[vmem] * count + [...  107 us
    pallas_call x1, Pallas kernels, reduce(): pl.pallas_call(reduce_kernel, out_shape=[jax.ShapeDtypeStruct((2, *shape)...  106 us
    dot_general x4, matrix products, t_dot(): lax.dot_general(a, b, (((0,), (0,)), ((), ())), preferred_element_type=F32)  14.7 us
    dot_general x4, matrix products, dot_t(): lax.dot_general(a, b, (((1,), (1,)), ((), ())), preferred_element_type=F32)  12.6 us
    unnamed x47, local copies, waits for them, and re-layouts  9.41 us
    dot_general x4, matrix products, dot(): return jnp.dot(a, b, preferred_element_type=F32)  8.07 us
  transfers between devices with their start and end apart: 1, of which 0 were waited for; matrix products, arithmetic and copies ran while one was open for 13% of the time, Pallas kernels for 36%

profile of v2, /device:TPU:1, one launch (start us, length us, event | category | flops | bytes accessed | tf_op | source)
XLA Modules:
  0.0 289.3 jit_solution(4914600962019489692)
XLA Ops:
  0.7 0.8 fusion.25
  1.5 0.7 fusion.26
  2.2 0.8 copy.35
  3.0 0.7 copy.36
  3.7 0.7 copy.37
  4.6 0.8 slice_bitcast_fusion.1
  5.5 0.6 pad_maximum_fusion.5.refs_2_
  6.9 0.8 slice_bitcast_fusion.3
  7.9 0.7 pad_maximum_fusion.2.refs_4_
  8.5 0.7 pad_maximum_fusion.1.refs_3_
  10.0 0.7 pad_maximum_fusion.3.refs_5_
  10.7 106.5 %gather_and_mix.1 = (bf16[4,2,4,2,16,512]{5,4,3,2,1,0:T(8,128)(2,1)}, bf16[4,2,4,2,16,512]{5,4,3,2,1,0:T(8,128)(2,1)}, bf16[4,2,4,2,16,512]{5,4,3,2,1,0:T(8,128)...) custom-call(bf16[2,16,640]{2,1,0:T(8,128)(2,1)} %pad_maximum_fusion., ...), custom_call_target="tpu_custom_call" | custom-call | tf_op jit(solution)/shard_map/gather_and_mix/pallas_call | solution.py:333
  117.3 2.9 %fusion.23 = (bf16[1,2,2,4,2,72,512]{6,5,4,3,2,1,0:T(8,128)(2,1)S(1)}, bf16[1,2,2,4,2,72,512]{6,5,4,3,2,1,0:T(8,128)(2,1)S(1)}) fusion(bf16[2,2,2,4,2,72,512]{6,5,4,3,2,1,0:T(8,128)(2,1)} %get-tuple-element.39), kind=kLoop, calls=%fused_computation.97 | loop fusion | bytes 9437184 | tf_op jit(solution)/shard_map/slice | solution.py:722
  120.4 1.2 copy-done.8
  122.1 2.6 fusion.28
  124.7 2.6 fusion.27
  127.3 1.4 fusion.8
  128.8 4.6 %multiply_convert_fusion = (bf16[512,2304]{1,0:T(8,128)(2,1)}, bf16[512,2304]{1,0:T(8,128)(2,1)}, bf16[512,2304]{1,0:T(8,128)(2,1)S(1)}) fusion(f32[512,2304]{1,0:T(8,128)S(1)} %fusion.27, f32[512,2304]{1,0:T(8,128)S(1)} %fusion.28, f32[512,2304]{1,0:T(8,128)S(1)} %fusion.8, bf16[2304,512]{1,0:T(8,128)(2,1)S(1)} %bitcast.105, bf16[512,1024]{1,0:T(8,128)(2,1)S(1)} %bitcast.100), kind=kOutput, calls=%fused_computation.4 | convolution fusion | flops 1228013568 | bytes 24117248 | tf_op jit(solution)/shard_map/dot_general | solution.py:88
  133.3 1.4 fusion.30
  134.8 1.4 fusion.29
  136.2 1.1 fusion
  137.3 1.3 copy-done.12
  138.7 2.9 convolution_convert_fusion.3
  141.5 2.9 convolution_convert_fusion.2
  144.4 2.6 fusion.31
  147.1 4.6 %convolution_convert_fusion.1 = bf16[1024,2304]{1,0:T(8,128)(2,1)} fusion(bf16[512,1024]{1,0:T(8,128)(2,1)S(1)} %bitcast.129, bf16[512,2304]{1,0:T(8,128)(2,1)S(1)} %copy-done.14), kind=kOutput, calls=%fused_computation.1 | convolution fusion | flops 2418278400 | bytes 8126464 | tf_op jit(solution)/shard_map/dot_general | solution.py:92
  151.7 4.3 %convolution_convert_fusion = bf16[1024,2304]{1,0:T(8,128)(2,1)} fusion(bf16[512,1024]{1,0:T(8,128)(2,1)S(1)} %bitcast.130, bf16[512,2304]{1,0:T(8,128)(2,1)S(1)} %copy-done.13), kind=kOutput, calls=%fused_computation | convolution fusion | flops 2418278400 | bytes 8126464 | tf_op jit(solution)/shard_map/dot_general | solution.py:92
  156.0 4.0 %convolution_add_fusion.1 = f32[512,1024]{1,0:T(8,128)} fusion(f32[512,1024]{1,0:T(8,128)S(1)} %fusion.31, bf16[512,2304]{1,0:T(8,128)(2,1)S(1)} %copy-done.13, bf16[1024,2304]{1,0:T(8,128)(2,1)S(1)} %bitcast.120), kind=kOutput, calls=%fused_computation.14 | convolution fusion | flops 2416443392 | bytes 11272192 | tf_op jit(solution)/shard_map/dot_general | solution.py:88
  160.0 4.2 %pad_maximum_fusion.refs_2_ = bf16[2,2,2,4,2,72,512]{6,5,4,3,2,1,0:T(8,128)(2,1)} fusion(bf16[1,2,2,4,2,72,512]{6,5,4,3,2,1,0:T(8,128)(2,1)} %bitcast.104, bf16[1,2,2,4,2,72,512]{6,5,4,3,2,1,0:T(8,128)(2,1)S(1)} %bitcast.103), kind=kLoop, calls=%fused_computation.3 | loop fusion | flops 2359296 | bytes 9437184 | tf_op jit(solution)/shard_map/stack | solution.py:733
  164.2 105.5 %sum_gradients.1 = (f32[2,16,640]{2,1,0:T(8,128)}, f32[2,16,512]{2,1,0:T(8,128)}, f32[2,16,1024]{2,1,0:T(8,128)}, f32[2,16,2304]{2,1,0:T(8,128)}, f32[2,16,2304]...) custom-call(bf16[4,2,4,2,16,2304]{5,4,3,2,1,0:T(8,128)(2,1)} %bitcast.97, ...), custom_call_target="tpu_custom_call" | custom-call | tf_op jit(solution)/shard_map/sum_gradients/pallas_call | solution.py:623
  269.7 0.8 fusion.24
  270.6 0.7 slice_reduce_fusion
  271.3 0.7 dynamic-slice_bitcast_fusion.13
  272.1 0.9 dynamic-slice_bitcast_fusion.3
  273.0 0.9 dynamic-slice_bitcast_fusion.5
  273.9 0.7 dynamic-slice_bitcast_fusion.11
  274.7 0.7 copy.42
  275.3 1.3 constant_dynamic-slice_fusion
  276.7 1.3 copy.43
  278.0 1.0 dynamic-slice_bitcast_fusion.1
  279.0 0.7 maximum_multiply_fusion
  279.7 0.8 dynamic-slice_bitcast_fusion.7
  281.1 0.6 pad_maximum_fusion.4
  281.8 0.7 maximum_multiply_fusion.2
  282.4 0.7 maximum_multiply_fusion.1
  283.1 2.5 fusion.4
  285.7 2.6 copy.41
  288.3 1.0 copy.45
  (68 shorter events, 3.4 us)
Async XLA Ops:
  117.2 3.0 %copy-start = (f32[2,256,1024]{2,1,0:T(8,128)S(1)}, f32[2,256,1024]{2,1,0:T(8,128)}, u32[]{:S(2)}) copy-start(f32[2,256,1024]{2,1,0:T(8,128)} %get-tuple-element.40.refs_4_) | copy-start | bytes 6291460
  117.2 4.4 %copy-start.8 = (bf16[4,2,4,2,16,2304]{5,4,3,2,1,0:T(8,128)(2,1)S(1)}, bf16[4,2,4,2,16,2304]{5,4,3,2,1,0:T(8,128)(2,1)}, u32[]{:S(2)}) copy-start(bf16[4,2,4,2,16,2304]{5,4,3,2,1,0:T(8,128)(2,1)} %get-tuple-element.38) | copy-start | bytes 14155780
  120.2 1.9 copy-start.9
  120.3 4.4 %slice-start.2 = ((s8[4718592]{0:T(1024)(128)(4,1)}), s8[4194304]{0:T(1024)(128)(4,1)S(1)}, s32[]{:S(2)}) async-start(s8[4718592]{0:T(1024)(128)(4,1)} %bitcast.121), calls=%async_computation.2 | async-start | bytes 8388608
  122.1 2.6 slice-start.3
  133.3 1.4 copy-start.11
  134.8 1.5 copy-start.1
  136.2 5.3 %copy-start.3 = (f32[512,512]{0,1:T(8,128)}, f32[512,512]{0,1:T(8,128)S(1)}, u32[]{:S(2)}) copy-start(f32[512,512]{0,1:T(8,128)S(1)} %fusion.29) | copy-start | bytes 3145732
  136.2 2.4 copy-start.12
  137.3 145.8 %collective-permute-start = (f32[256,1024]{0,1:T(8,128)}, f32[256,1024]{0,1:T(8,128)}, u32[]{:S(2)}, u32[]{:S(2)}) collective-permute-start(f32[256,1024]{0,1:T(8,128)} %fusion), channel_id=1, source_target_pairs={{0,1},{1,0},{2,3},{3,2},{4,5},{5,4},{6,7},{7,6},{8,9},{9,8},{10,11... | collective-permute-start | bytes 3145736 | tf_op jit(solution)/shard_map/ppermute | solution.py:653
  138.7 5.7 %slice-start.4 = ((s8[4718592]{0:T(1024)(128)(4,1)}), s8[4194304]{0:T(1024)(128)(4,1)S(1)}, s32[]{:S(2)}) async-start(s8[4718592]{0:T(1024)(128)(4,1)} %bitcast.124), calls=%async_computation.4 | async-start | bytes 8388608
  141.5 2.9 slice-start.5
  141.5 2.9 copy-start.14
  144.4 2.6 copy-start.10
  147.1 4.6 %copy-start.13 = (bf16[512,2304]{1,0:T(8,128)(2,1)S(1)}, bf16[512,2304]{1,0:T(8,128)(2,1)}, u32[]{:S(2)}) copy-start(bf16[512,2304]{1,0:T(8,128)(2,1)} %get-tuple-element.92) | copy-start | bytes 7077892
  147.1 8.9 %slice-start = ((s8[4718592]{0:T(1024)(128)(4,1)}), s8[4194304]{0:T(1024)(128)(4,1)S(1)}, s32[]{:S(2)}) async-start(s8[4718592]{0:T(1024)(128)(4,1)} %bitcast.118), calls=%async_computation | async-start | bytes 8388608
  151.7 4.3 %slice-start.1 = ((s8[4718592]{0:T(1024)(128)(4,1)}), s8[524288]{0:T(1024)(128)(4,1)S(1)}, s32[]{:S(2)}) async-start(s8[4718592]{0:T(1024)(128)(4,1)} %bitcast.118), calls=%async_computation.1 | async-start | bytes 1048576
  156.0 4.0 %copy-start.6 = (bf16[2304,512]{1,0:T(8,128)(2,1)S(1)}, bf16[2304,512]{1,0:T(8,128)(2,1)}, u32[]{:S(2)}) copy-start(bf16[2304,512]{1,0:T(8,128)(2,1)} %convolution_convert_fusion.3) | copy-start | bytes 7077892
  276.6 6.5 %copy-start.2 = (f32[512,512]{0,1:T(8,128)S(1)}, f32[512,512]{0,1:T(8,128)}, u32[]{:S(2)}) copy-start(f32[512,512]{0,1:T(8,128)} %copy-done.1) | copy-start | bytes 3145732
  276.7 6.5 %copy-start.4 = (f32[512,512]{0,1:T(8,128)S(1)}, f32[512,512]{0,1:T(8,128)}, u32[]{:S(2)}) copy-start(f32[512,512]{0,1:T(8,128)} %copy-done.3) | copy-start | bytes 3145732
  278.0 5.2 %copy-start.5 = (f32[256,1024]{0,1:T(8,128)S(1)}, f32[256,1024]{0,1:T(8,128)}, u32[]{:S(2)}) copy-start(f32[256,1024]{0,1:T(8,128)} %copy.43) | copy-start | bytes 3145732
  285.7 2.6 copy-start.7

commit v3 on v2

--- a/solution.py
+++ b/solution.py
@@ -1,3 +1,4 @@
+import functools
 import math
 
 import jax
@@ -14,8 +15,8 @@
 CHIPS = (4, 2, 4, 2)
 ARRAYS = (
     ((16, 640), "xyz"),
-    ((16, 512), "yzx"),
-    ((16, 1024), "zxy"),
+    ((16, 768), "yzx"),
+    ((16, 768), "zxy"),
     ((16, 2304), "xyz"),
     ((16, 2304), "yzx"),
     ((72, 512), "zxy"),
@@ -141,15 +142,14 @@
         del refs[:n]
         return taken
 
-    shards = take(count)
-    tok, cot = take(2)
-    w_b, w_c, w_x, out_half = take(4)
-    feed_full = take(3)
-    down_half, tok_pair, cot_pair = take(3)
-    res, hid1, hid2, b_mat, c_mat, x_mat, gated, y_mat, small = take(9)
-    theirs, block = take(count), take(count)
-    full = take(3) + feed_full
-    toks, mix, mix2, outw, halo = take(5)
+    small_rows, in_rows, out_rows, gate_rows, up_rows, down_rows, tok, cot = take(8)
+    w_b, w_c, w_x, out_half, gate_full, up_full, down_half, tok_pair, cot_pair = take(9)
+    results = take(9)
+    (small,) = take(1)
+    given, theirs, block, (down32,) = take(count), take(count), take(count), take(1)
+    full = take(count)
+    toks, mix, mix2, outw, halo, cots, landed = take(7)
+    res, hid1, hid2, b_mat, c_mat, x_mat, gated, y_mat, cot16 = held = take(9)
     sends, recvs, local = refs
     at, core = position()
     sibling = device(at, 1 - core)
@@ -170,13 +170,45 @@
         kept.append(start(pltpu.make_async_copy(src, dst, local.at[sem])))
         return kept[-1]
 
+    down32[...] = jnp.zeros_like(down32)
+    for c in range(2):
+
+        @pl.when(core == c)
+        def _():
+            down32[36 * c : 36 * c + 36, :] = down_rows[...].astype(F32)
+
+    def spread(rows):
+        both = jnp.concatenate([rows.astype(F32)] * 2, axis=0)
+        mine = lax.broadcasted_iota(jnp.int32, both.shape, 0) // 8 == core
+        return jnp.where(mine, both, 0.0).astype(BF16)
+
+    def fill(k, half, dst):
+        def columns(ref, first, size):
+            return ref[:, pl.ds(pl.multiple_of(first, 128), size)]
+
+        if k < 3:
+            dst[:, 0:HALF] = spread(columns(in_rows, k * WIDTH + half * HALF, HALF))
+        if k == 0:
+            dst[:, HALF : HALF + 128] = spread(small_rows[...])
+        elif k < 3:
+            dst[:, HALF : HALF + 256] = spread(
+                columns(out_rows, half * HALF + 256 * (k - 1), 256)
+            )
+        elif k < 5:
+            dst[...] = spread(columns(gate_rows if k == 3 else up_rows, half * 2304, 2304))
+        else:
+            dst[...] = columns(down32, half * HALF, HALF).astype(BF16)
+
     for k in range(count):
-        send(shards[k].at[1 - core], theirs[k], sibling, 12 * count + k)
+        fill(k, 1 - core, given[k])
+        send(given[k], theirs[k], sibling, 12 * count + k)
+    for k in range(count):
+        fill(k, core, block[k])
     own_copies = []
     here = (at["y"], lax.rem(at["x"], 2), at["z"], lax.div(at["x"], 2))
     for k in range(count):
         arrived(theirs[k], 12 * count + k)
-        block[k][...] = jnp.where(core == 0, shards[k][0], shards[k][1]) + theirs[k][...]
+        block[k][...] = block[k][...] + theirs[k][...]
         own_copies.append(
             start(pltpu.make_async_copy(block[k], full[k].at[here], local.at[k]))
         )
@@ -189,8 +221,8 @@
             )
     send(tok, toks.at[core], sibling, 13 * count)
     own_tok = start(pltpu.make_async_copy(tok, toks.at[core], local.at[count]))
-    send(cot, cot_pair.at[core], sibling, 13 * count + 1)
-    keep(cot, cot_pair.at[core], count + 1)
+    send(cot, cots.at[core], sibling, 13 * count + 1)
+    own_cot = start(pltpu.make_async_copy(cot, cots.at[core], local.at[count + 1]))
 
     def pass_on(k, phase):
         (_, columns), order = ARRAYS[k]
@@ -216,11 +248,11 @@
         for by, sem in ((1, 0), (3, 1)):
             send(mine, mine, device(moved(at, order[phase], by), core), 12 * k + 4 * phase + sem)
 
-    def give_half(k, dst, columns):
+    def give_half(k, dst, columns, sem):
         mine = full[k].at[(pl.ds(2 * core, 2), *REST, columns)]
         other = full[k].at[(pl.ds(2 - 2 * core, 2), *REST, columns)]
-        send(other, dst.at[core], sibling, 13 * count + k)
-        return start(pltpu.make_async_copy(mine, dst.at[core], local.at[count + k]))
+        send(other, dst, sibling, sem)
+        return start(pltpu.make_async_copy(mine, dst, local.at[10 + k]))
 
     def each(step, arrays, phase):
         for k in arrays:
@@ -240,10 +272,32 @@
     each(pass_on, MIXER, 2)
     each(begin, FEED, 2)
     each(complete, MIXER, 2)
-    own_out = give_half(2, outw, slice(512, 1024))
+    own_out = [
+        give_half(
+            k,
+            outw.at[(core, *REST, slice(None), slice(256 * k - 256, 256 * k))],
+            slice(HALF, HALF + 256),
+            14 * count + k,
+        )
+        for k in (1, 2)
+    ]
+    own_cot.wait()
+    arrived(cots.at[1 - core], 13 * count + 1)
+    keep(cots, cot_pair, 23)
+
+    def round_cot(c, rows):
+        cot16[c, rows, :] = cots[c, rows, :].astype(BF16)
+
+    row_blocks(round_cot)
     left = slice(0, 512)
+
+    def hand_over(*which):
+        for i in which:
+            keep(held[i], results[i], 24 + i)
+
+    hand_over(8)
     keep(full[0].at[(*REST, slice(None), left)], w_b, 18)
-    keep(full[1], w_c, 19)
+    keep(full[1].at[(*REST, slice(None), left)], w_c, 19)
     keep(full[2].at[(*REST, slice(None), left)], w_x, 20)
 
     small[...] = dot_t(picker(), flat(full[0][:, :, :, :, :, 512:640]))
@@ -269,8 +323,11 @@
 
     steps(4, project)
     send(gated.at[:, pl.ds(ROWS, 8), :], halo, next_block(1), 13 * count + 4)
-    own_out.wait()
-    arrived(outw.at[1 - core], 13 * count + 2)
+    hand_over(1, 3, 4, 5)
+    for k in (1, 2):
+        own_out[k - 1].wait()
+        part = (1 - core, *REST, slice(None), slice(256 * k - 256, 256 * k))
+        arrived(outw.at[part], 14 * count + k)
     keep(outw, out_half, 22)
     arrived(halo, 13 * count + 4)
     starts = lax.axis_index("seq") == 0
@@ -283,6 +340,8 @@
             conv = conv + taps[2] * gated[c, r + 8 : r + 72, :]
             y_mat[c, r : r + 64, :] = (c_mat[c, r : r + 64, :] * conv).astype(BF16)
 
+    hand_over(6, 7)
+
     def mixing(i):
         c, h, j = lax.div(i, 4), lax.rem(lax.div(i, 2), 2), lax.rem(i, 2)
         weight = outw[h, :, :, :, :, :, tile(j)]
@@ -291,6 +350,56 @@
     steps(8, mixing)
     send(mix, mix2, sibling, 13 * count + 3)
     each(pass_on, FEED, 2)
+
+    def columns(half):
+        return tile(half, HALF)
+
+    def feed_out(step):
+        for k, dst in ((3, gate_full), (4, up_full)):
+            order = ARRAYS[k][1]
+            spot = chip_index(moved(at, order[2], step), order[:2])
+            keep(full[k].at[spot], dst.at[spot], 33 + 4 * (k - 3) + step)
+        y = lax.rem(at["y"] + step, 4)
+        here, there = lax.div(y, 2), lax.rem(y, 2)
+
+        @pl.when(here == core)
+        def _():
+            out = down_half.at[(there, *REST[:3], slice(None), columns(core))]
+            pltpu.make_async_copy(full[5].at[y], out, local.at[41 + step]).start()
+
+        @pl.when(here != core)
+        def _():
+            remote(full[5].at[y], landed.at[there], sends, recvs, sibling, 15 * count + step).start()
+
+    def feed_land(step):
+        y = lax.rem(at["y"] + step, 4)
+        here, there = lax.div(y, 2), lax.rem(y, 2)
+
+        @pl.when(here == core)
+        def _():
+            arrived(landed.at[there], 15 * count + step)
+            out = down_half.at[(there, *REST[:3], slice(None), columns(1 - core))]
+            pltpu.make_async_copy(landed.at[there], out, local.at[45 + step]).start()
+
+    def feed_end(step):
+        y = lax.rem(at["y"] + step, 4)
+        here, there = lax.div(y, 2), lax.rem(y, 2)
+
+        @pl.when(here == core)
+        def _():
+            out = down_half.at[(there, *REST[:3], slice(None), columns(core))]
+            pltpu.make_async_copy(full[5].at[y], out, local.at[41 + step]).wait()
+            out = down_half.at[(there, *REST[:3], slice(None), columns(1 - core))]
+            pltpu.make_async_copy(landed.at[there], out, local.at[45 + step]).wait()
+
+        @pl.when(here != core)
+        def _():
+            remote(
+                full[5].at[y], landed.at[there], sends, recvs, sibling, 15 * count + step
+            ).wait_send()
+
+    for step in (0, 1, 3):
+        feed_out(step)
     arrived(mix2, 13 * count + 3)
 
     def norm_two(c, rows):
@@ -299,10 +408,14 @@
         hid2[c, rows, :] = (r * rms_inverse(r) * small[1:2, :]).astype(BF16)
 
     row_blocks(norm_two)
+    hand_over(0, 2)
+    for step in (0, 1, 3):
+        feed_land(step)
     each(complete, FEED, 2)
-    give_half(5, down_half, slice(0, 512)).wait()
-    arrived(down_half.at[1 - core], 13 * count + 5)
-    arrived(cot_pair.at[1 - core], 13 * count + 1)
+    feed_out(2)
+    feed_land(2)
+    for step in range(4):
+        feed_end(step)
     for copy in sent:
         copy.wait_send()
     for copy in kept:
@@ -315,10 +428,9 @@
     shape = jax.ShapeDtypeStruct
     pair = (2, ROWS, WIDTH)
     outs = [shape((*CHIPS, 16, HALF), BF16)] * 3 + [shape((2, 2, 2, 4, 2, 16, HALF), BF16)]
-    outs += [shape((*CHIPS, *ARRAYS[k][0]), BF16) for k in FEED]
-    outs += [shape((2, 2, 2, 4, 2, 72, HALF), BF16), shape(pair, F32), shape(pair, F32)]
-    in_hbm = len(outs)
-    outs += [
+    outs += [shape((*CHIPS, *ARRAYS[k][0]), BF16) for k in (3, 4)]
+    outs += [shape((2, 2, 4, 2, 72, WIDTH), BF16), shape(pair, F32), shape(pair, F32)]
+    held = [
         shape(pair, F32),
         shape(pair, BF16),
         shape(pair, BF16),
@@ -327,24 +439,32 @@
         shape((2, ROWS, HALF), F32),
         shape((2, ROWS + 8, HALF), F32),
         shape((2, ROWS, HALF), BF16),
-        shape((16, WIDTH), F32),
+        shape(pair, BF16),
     ]
+    outs += held
+    in_hbm = len(outs)
+    outs += [shape((16, WIDTH), F32)]
     blocks = [pltpu.VMEM(array, BF16) for array, _ in ARRAYS]
     return pl.pallas_call(
         gather_kernel,
         out_shape=outs,
-        in_specs=[vmem] * count + [hbm] * 2,
-        out_specs=[hbm] * 4 + [vmem] * 3 + [hbm] * (in_hbm - 7) + [vmem] * (len(outs) - in_hbm),
+        in_specs=[vmem] * len(shards) + [hbm] * 2,
+        out_specs=[hbm] * in_hbm + [vmem],
         scratch_shapes=[
             *blocks,
             *blocks,
-            *[pltpu.VMEM((*CHIPS, *ARRAYS[k][0]), BF16) for k in MIXER],
+            *blocks,
+            pltpu.VMEM((72, WIDTH), F32),
+            *[pltpu.VMEM((*CHIPS, *array), BF16) for array, _ in ARRAYS],
             *[pltpu.VMEM(pair, F32)] * 3,
             pltpu.VMEM((2, 2, 2, 4, 2, 16, HALF), BF16),
             pltpu.VMEM((2, 8, HALF), F32),
-            pltpu.SemaphoreType.DMA((14 * count,)),
-            pltpu.SemaphoreType.DMA((14 * count,)),
-            pltpu.SemaphoreType.DMA((24,)),
+            pltpu.VMEM(pair, F32),
+            pltpu.VMEM((2, 2, 4, 2, 72, HALF), BF16),
+            *[pltpu.VMEM(value.shape, value.dtype) for value in held],
+            pltpu.SemaphoreType.DMA((16 * count,)),
+            pltpu.SemaphoreType.DMA((16 * count,)),
+            pltpu.SemaphoreType.DMA((50,)),
         ],
         compiler_params=pltpu.CompilerParams(
             collective_id=0, has_side_effects=True, vmem_limit_bytes=60 * 2**20
@@ -353,7 +473,7 @@
     )(*shards, tok, cot)
 
 
-def reduce_kernel(*refs):
+def reduce_kernel(factor, *refs):
     count = len(ARRAYS)
     refs = list(refs)
 
@@ -362,11 +482,12 @@
         del refs[:n]
         return taken
 
-    g_gate, g_up, g_down, d_hid2, in_hbm = *take(4), take(14)
-    totals, (input_grad,) = take(count), take(1)
+    g_gate, g_up, g_down, d_hid2, out_part, in_hbm = *take(5), take(14)
+    block_out, input_grad, in_grads, out_grads, gate_grads, up_grads, down_grads, small_grads = take(8)
+    totals = take(count)
     data, arriving = take(count), take(12 * count)
     cot, res, hid1, b_mat, c_mat, x_mat, gated, y_mat, outw, small = held = take(10)
-    dh, dh2, d1r, dres, g_out, halo = take(6)
+    dh, dh2, d1r, dres, g_out, halo, ffn_own, ffn_other = take(8)
     d_proj, (g_small,) = take(3), take(1)
     sends, recvs, local = refs
     at, core = position()
@@ -462,26 +583,61 @@
         for k in arrays:
             step(k, phase)
 
-    mine = data[5].at[pl.ds(2 * core, 2)]
-    send(g_down.at[1 - core], mine, sibling, 12 * count + 5)
+    def slab(step, start):
+        y = lax.rem(at["y"] + step, 4)
+        here, there = lax.div(y, 2), lax.rem(y, 2)
+
+        def of(half):
+            return g_down.at[(there, *REST[:3], slice(None), tile(half, HALF))]
+
+        own = pltpu.make_async_copy(of(core), data[5].at[y], local.at[21 + step])
+        given = remote(of(1 - core), data[5].at[y], sends, recvs, sibling, 15 * count + step)
+
+        @pl.when(here == core)
+        def _():
+            if start:
+                given.start()
+                own.start()
+            else:
+                own.wait()
+
+        @pl.when(here != core)
+        def _():
+            if not start:
+                given.wait_recv()
+
+    def slab_sent(step):
+        y = lax.rem(at["y"] + step, 4)
+        there = lax.rem(y, 2)
+        src = g_down.at[(there, *REST[:3], slice(None), tile(1 - core, HALF))]
+
+        @pl.when(lax.div(y, 2) == core)
+        def _():
+            remote(src, data[5].at[y], sends, recvs, sibling, 15 * count + step).wait_send()
+
+    ring = (2, 1, 3, 0)
+    feed_loads = {}
+    for step in ring:
+        for k, src in ((3, g_gate), (4, g_up)):
+            order = ARRAYS[k][1]
+            spot = chip_index(moved(at, order[2], step), order[:2])
+            feed_loads[k, step] = load(src.at[spot], data[k].at[spot], 25 + 4 * (k - 3) + step)
+        slab(step, True)
     send(d_hid2, dh2, sibling, 12 * count)
-    feed_loads = [
-        load(g_gate, data[3], 3),
-        load(g_up, data[4], 4),
-        load(g_down.at[core], mine, 5),
-    ]
+    send(out_part.at[1 - core], ffn_other, sibling, 12 * count + 2)
     first_loads = [load(d_hid2, dh, 6)]
     first_loads += [load(in_hbm[i], held[i], 7 + i) for i in (0, 1, 9)]
     rest_loads = [load(in_hbm[i], held[i], 7 + i) for i in range(2, 9)]
     left = slice(0, HALF)
     for k in MIXER:
-        dst = data[k] if k == 1 else data[k].at[(*REST, slice(None), left)]
+        dst = data[k].at[(*REST, slice(None), left)]
         rest_loads.append(load(in_hbm[10 + k], dst, 17 + k))
-    for k in FEED:
-        feed_loads[k - 3].wait()
-        if k == 5:
-            arrived(data[5].at[pl.ds(2 - 2 * core, 2)], 12 * count + 5)
+    for k in (3, 4):
+        feed_loads[k, 2].wait()
         begin(k, 0)
+    slab(2, False)
+    begin(5, 0)
+    ffn_load = load(out_part.at[core], ffn_own, 33)
     for copy in first_loads:
         copy.wait()
     arrived(dh2, 12 * count)
@@ -500,7 +656,19 @@
         dres[c, rows, :] = out.astype(BF16)
 
     row_blocks(norm_two)
+    ffn_load.wait()
+    arrived(ffn_other, 12 * count + 2)
+
+    def add_ffn(i):
+        rows = tile(i, 32)
+        block_out[rows, :] = res[core, rows, :] + (ffn_own[rows, :] + ffn_other[rows, :])
+
+    steps(ROWS // 32, add_ffn)
     tok_load = load(in_hbm[13], res, 20)
+    for step in ring[1:]:
+        feed_loads[3, step].wait()
+        feed_loads[4, step].wait()
+        slab(step, False)
     each(pass_on, FEED, 0)
     for copy in rest_loads:
         copy.wait()
@@ -517,17 +685,30 @@
     send(c_mat.at[:, pl.ds(0, 8), :], halo, next_block(31), 12 * count + 3)
 
     def out_grad(i):
-        f, j = lax.div(i, 2), lax.rem(i, 2)
-        other = sum(
-            t_dot(y_mat[c, :, tile(f)], dres[c, :, tile(2 - 2 * core + j)]) for c in range(2)
+        f = i
+        for j in range(2):
+            other = sum(
+                t_dot(y_mat[c, :, tile(f)], dres[c, :, tile(2 - 2 * core + j)]) for c in range(2)
+            )
+            g_out[f, :, :, :, :, 256 * j : 256 * j + 256] = other.astype(BF16).reshape(
+                2, 4, 2, 16, 256
+            )
+            own = sum(
+                t_dot(y_mat[c, :, tile(f)], dres[c, :, tile(2 * core + j)]) for c in range(2)
+            )
+            data[1 + j][2 * core + f, :, :, :, :, HALF : HALF + 256] = own.astype(BF16).reshape(
+                2, 4, 2, 16, 256
+            )
+
+    steps(2, out_grad)
+    right = slice(HALF, HALF + 256)
+    for j in range(2):
+        send(
+            g_out.at[(slice(None), *REST, slice(256 * j, 256 * j + 256))],
+            data[1 + j].at[(pl.ds(2 * core, 2), *REST, right)],
+            sibling,
+            14 * count + j,
         )
-        g_out[f, :, :, :, :, tile(j)] = other.astype(BF16).reshape(2, 4, 2, 16, 256)
-        own = sum(t_dot(y_mat[c, :, tile(f)], dres[c, :, tile(2 * core + j)]) for c in range(2))
-        data[2][2 * core + f, :, :, :, :, tile(2 + j)] = own.astype(BF16).reshape(2, 4, 2, 16, 256)
-
-    steps(4, out_grad)
-    right = slice(HALF, WIDTH)
-    send(g_out, data[2].at[(pl.ds(2 * core, 2), *REST, right)], sibling, 12 * count + 2)
     arrived(halo, 12 * count + 3)
     ends = lax.axis_index("seq") == 31
     for c in range(2):
@@ -571,7 +752,8 @@
     row_blocks(gain_one)
     turned = t_dot(g_small[...].astype(BF16), picker()).astype(BF16)
     data[0][:, :, :, :, :, HALF : HALF + 128] = turned.reshape(*CHIPS, 16, 128)
-    arrived(data[2].at[(pl.ds(2 - 2 * core, 2), *REST, right)], 12 * count + 2)
+    for j in range(2):
+        arrived(data[1 + j].at[(pl.ds(2 - 2 * core, 2), *REST, right)], 14 * count + j)
     each(begin, MIXER, 0)
     each(complete, FEED, 0)
     each(pass_on, MIXER, 0)
@@ -598,11 +780,31 @@
     each(complete, MIXER, 2)
     for k in range(count):
         arrived(totals[k].at[1 - core], 13 * count + k)
+    mine = pl.ds(pl.multiple_of(8 * core, 8), 8)
+    for h in range(2):
+        at_half = slice(HALF * h, HALF * h + HALF)
+        for k in MIXER:
+            in_grads[:, WIDTH * k + HALF * h : WIDTH * k + HALF * h + HALF] = (
+                totals[k][h, mine, 0:HALF] * factor
+            )
+        for k in (1, 2):
+            first = HALF * h + 256 * (k - 1)
+            out_grads[:, first : first + 256] = totals[k][h, mine, HALF : HALF + 256] * factor
+        for k, dst in ((3, gate_grads), (4, up_grads)):
+            dst[:, 2304 * h : 2304 * h + 2304] = totals[k][h, mine, :] * factor
+        down_grads[:, at_half] = factor * jnp.where(
+            core == 0, totals[5][h, 0:36, :], totals[5][h, 36:72, :]
+        )
+    small_grads[...] = factor * (
+        totals[0][0, mine, HALF : HALF + 128] + totals[0][1, mine, HALF : HALF + 128]
+    )
+    for step in ring:
+        slab_sent(step)
     for copy in sent:
         copy.wait_send()
 
 
-def reduce(g_gate, g_up, g_down, d_hid2, *rest):
+def reduce(factor, g_gate, g_up, g_down, d_hid2, out_part, *rest):
     count = len(ARRAYS)
     hbm, vmem = pl.BlockSpec(memory_space=pl.ANY), pl.BlockSpec(memory_space=pltpu.VMEM)
     buffers = []
@@ -619,14 +821,26 @@
                 buffers.append(pltpu.VMEM((*lead, rows, part.stop - part.start), BF16))
             buffers += [pltpu.VMEM((*lead, rows, columns), BF16)] * 2
     pair = pltpu.VMEM((2, ROWS, WIDTH), F32)
-    operands = (g_gate, g_up, g_down, d_hid2, *rest)
+    operands = (g_gate, g_up, g_down, d_hid2, out_part, *rest)
     return pl.pallas_call(
-        reduce_kernel,
-        out_shape=[jax.ShapeDtypeStruct((2, *shape), F32) for shape, _ in ARRAYS]
-        + [jax.ShapeDtypeStruct((ROWS, WIDTH), F32)],
+        functools.partial(reduce_kernel, factor),
+        out_shape=[
+            jax.ShapeDtypeStruct(shape, F32)
+            for shape in (
+                (ROWS, WIDTH),
+                (ROWS, WIDTH),
+                (8, 3 * WIDTH),
+                (8, WIDTH),
+                (8, 4608),
+                (8, 4608),
+                (36, WIDTH),
+                (8, 128),
+            )
+        ],
         in_specs=[hbm] * len(operands),
-        out_specs=[vmem] * (count + 1),
+        out_specs=[vmem] * 8,
         scratch_shapes=[
+            *[pltpu.VMEM((2, *shape), F32) for shape, _ in ARRAYS],
             *[pltpu.VMEM((*CHIPS, *shape), BF16) for shape, _ in ARRAYS],
             *buffers,
             *[pltpu.VMEM(value.shape, value.dtype) for value in rest[:10]],
@@ -636,11 +850,13 @@
             pltpu.VMEM((2, ROWS, WIDTH), BF16),
             pltpu.VMEM((2, 2, 4, 2, 16, HALF), BF16),
             pltpu.VMEM((2, 8, HALF), F32),
+            pltpu.VMEM((ROWS, WIDTH), F32),
+            pltpu.VMEM((ROWS, WIDTH), F32),
             *[pltpu.VMEM((2, ROWS, HALF), BF16)] * 3,
             pltpu.VMEM((16, WIDTH), F32),
-            pltpu.SemaphoreType.DMA((14 * count,)),
-            pltpu.SemaphoreType.DMA((14 * count,)),
-            pltpu.SemaphoreType.DMA((24,)),
+            pltpu.SemaphoreType.DMA((16 * count,)),
+            pltpu.SemaphoreType.DMA((16 * count,)),
+            pltpu.SemaphoreType.DMA((34,)),
         ],
         compiler_params=pltpu.CompilerParams(
             collective_id=1, has_side_effects=True, vmem_limit_bytes=63 * 2**20
@@ -649,15 +865,27 @@
     )(*operands)
 
 
-def swap_pair(value):
-    return lax.ppermute(value, "fsdp", [(0, 1), (1, 0), (2, 3), (3, 2)])
-
-
-def rows_for_pair(shard, core):
-    rows = shard.shape[0]
-    both = jnp.concatenate([shard, shard], axis=0)
-    mine = lax.broadcasted_iota(jnp.int32, both.shape, 0) // rows == core
-    return jnp.where(mine, both, jnp.zeros_like(both))
+def finish_kernel(*refs):
+    count = (len(refs) - 1) // 2
+    copies = [
+        pltpu.make_async_copy(refs[i], refs[count + i], refs[-1].at[i]) for i in range(count)
+    ]
+    for copy in copies:
+        copy.start()
+    for copy in copies:
+        copy.wait()
+
+
+def finish(*values):
+    hbm, vmem = pl.BlockSpec(memory_space=pl.ANY), pl.BlockSpec(memory_space=pltpu.VMEM)
+    return pl.pallas_call(
+        finish_kernel,
+        out_shape=[jax.ShapeDtypeStruct(v.shape, v.dtype) for v in values],
+        in_specs=[vmem] * len(values),
+        out_specs=[hbm] * len(values),
+        scratch_shapes=[pltpu.SemaphoreType.DMA((len(values),))],
+        name="finish",
+    )(*values)
 
 
 def shards(
@@ -684,64 +912,32 @@
         [norm1_gain[:, None], norm2_gain[:, None], conv_taps.T, jnp.zeros((8, 123), BF16)], axis=1
     )
 
-    def by_half(*columns):
-        return jnp.stack(
-            [
-                rows_for_pair(
-                    jnp.concatenate(
-                        [
-                            c if c.shape[1] == 128 else c[:, h * c.shape[1] // 2 : (h + 1) * c.shape[1] // 2]
-                            for c in columns
-                        ],
-                        axis=1,
-                    ),
-                    core,
-                )
-                for h in range(2)
-            ]
-        )
-
-    b_w, c_w, x_w = in_weight[:, :width], in_weight[:, width : 2 * width], in_weight[:, 2 * width :]
-    pieces = (
-        by_half(b_w, small),
-        by_half(c_w),
-        by_half(x_w, out_weight),
-        by_half(gate_weight),
-        by_half(up_weight),
-        by_half(down_weight),
-    )
-    w_b, w_c, w_x, w_out, w_gate, w_up, _, w_down, tok, cot, *kept = gather(pieces, inputs, upstream)
-    resid, hidden_one, hidden_two, b_mat, c_mat, x_mat, gated, y_mat, small = kept
+    pieces = (small, in_weight, out_weight, gate_weight, up_weight, down_weight)
+    w_b, w_c, w_x, w_out, w_gate, w_up, w_down, tok, cot, *kept = gather(pieces, inputs, upstream)
+    resid, hidden_one, hidden_two, b_mat, c_mat, x_mat, gated, y_mat, cot_half, small = kept
     w_gate = w_gate.reshape(width, -1)
     w_up = w_up.reshape(width, -1)
-    w_down = w_down.reshape(2, 2304, 512)
+    w_down = w_down.reshape(-1, width)
     hid2 = hidden_two.reshape(-1, width)
     gate, up_vals = dot(hid2, w_gate), dot(hid2, w_up)
     sigma = jax.nn.sigmoid(gate)
     act = (gate * sigma * up_vals).astype(BF16)
-    out_part = jnp.concatenate([dot(act, w_down[0]), dot(act, w_down[1])], axis=1)
-
-    def own(value):
-        return lax.dynamic_slice_in_dim(value, core * rows, rows, axis=0)
-
-    def others(value):
-        return lax.dynamic_slice_in_dim(value, (1 - core) * rows, rows, axis=0)
-
-    block_out = own(resid.reshape(-1, width)) + (own(out_part) + swap_pair(others(out_part)))
-
-    cot_half = cot.reshape(-1, width).astype(BF16)
-    g_down = jnp.stack([t_dot(act, cot_half[:, :512]), t_dot(act, cot_half[:, 512:])]).astype(BF16)
-    d_act = dot_t(cot_half[:, :512], w_down[0]) + dot_t(cot_half[:, 512:], w_down[1])
+    out_part = dot(act, w_down)
+    cot_half = cot_half.reshape(-1, width)
+    g_down = t_dot(act, cot_half).astype(BF16)
+    d_act = dot_t(cot_half, w_down)
     d_gate = (d_act * up_vals * sigma * (1.0 + gate * (1.0 - sigma))).astype(BF16)
     d_up = (d_act * gate * sigma).astype(BF16)
     g_gate = t_dot(hid2, d_gate).astype(BF16)
     g_up = t_dot(hid2, d_up).astype(BF16)
     d_hid2 = dot_t(d_gate, w_gate) + dot_t(d_up, w_up)
-    *totals, input_grad = reduce(
+    block_out, input_grad, g_in, g_out, g_gate, g_up, g_down, g_small = reduce(
+        factor,
         g_gate.reshape(*CHIPS, 16, 2304),
         g_up.reshape(*CHIPS, 16, 2304),
-        g_down.reshape(2, 2, 2, 4, 2, 72, 512),
+        g_down.reshape(2, 2, 4, 2, 72, width),
         d_hid2.reshape(2, rows, width),
+        out_part.reshape(2, rows, width),
         cot,
         resid,
         hidden_one,
@@ -758,26 +954,20 @@
         tok,
     )
 
-    def whole(total, columns=slice(None)):
-        count = total.shape[1] // 2
-        mine = lax.dynamic_slice_in_dim(total, core * count, count, axis=1)[:, :, columns]
-        return jnp.concatenate([mine[0], mine[1]], axis=1) * factor
-
-    t_b, t_c, t_x, t_gate, t_up, t_down = totals
-    count = 8
-    t_small = lax.dynamic_slice_in_dim(t_b[0] + t_b[1], core * count, count, axis=0)[:, 512:] * factor
-    left = slice(0, 512)
+    block_out, input_grad, g_in, g_out, g_gate, g_up, g_down = finish(
+        block_out, input_grad, g_in, g_out, g_gate, g_up, g_down
+    )
     return (
         block_out.reshape(tokens.shape),
         input_grad.reshape(tokens.shape),
-        t_small[:, 0],
-        jnp.concatenate([whole(t_b, left), whole(t_c), whole(t_x, left)], axis=1),
-        t_small[:, 2:5].T,
-        whole(t_x, slice(512, 1024)),
-        t_small[:, 1],
-        whole(t_gate),
-        whole(t_up),
-        whole(t_down),
+        g_small[:, 0],
+        g_in,
+        g_small[:, 2:5].T,
+        g_out,
+        g_small[:, 1],
+        g_gate,
+        g_up,
+        g_down,
     )
 
 

time: 290 us -> 246 us (0.85)
  local copies, waits for them, and re-layouts: 25.2 us -> 5.25 us
  other arithmetic: 15.7 us -> 0.66 us
  Pallas kernels: 212 us -> 202 us
    pallas_call x2 -> x3, Pallas kernels: 212 us -> 202 us  [the longest x1 102 us: reduce(): pl.pallas_call(functools.partial(reduce_kernel, factor), out_shape=[jax.S...]
    another operation x7 -> x0, other arithmetic: 8.17 us -> none  [the longest x1 4.25 us: shards(): jnp.stack([t_dot(act, cot_half[:, :512]), t_dot(act, cot_half[:, 512:])])]
    unnamed x47 -> x16, local copies, waits for them, and re-layouts: 9.41 us -> 1.45 us
    squeeze x6 -> x0, local copies, waits for them, and re-layouts: 5.16 us -> none  [whole(): return jnp.concatenate([mine[0], mine[1]], axis=1) * factor]
    slice x5 -> x1, local copies, waits for them, and re-layouts: 5.94 us -> 1.48 us  [shards(): g_small[:, 1]]
    dot_general x4 -> x3, matrix products: 8.07 us -> 11.3 us  [dot(): return jnp.dot(a, b, preferred_element_type=F32)]
    dot_general x4 -> x3, matrix products: 14.7 us -> 13 us  [t_dot(): lax.dot_general(a, b, (((0,), (0,)), ((), ())), preferred_element_type=F32)]
    dot_general x4 -> x3, matrix products: 12.6 us -> 12 us  [dot_t(): lax.dot_general(a, b, (((1,), (1,)), ((), ())), preferred_element_type=F32)]
  transfers between devices with their start and end apart: 1 -> 0, of which waited for: 0 -> 0; matrix products, arithmetic and copies ran while one was open for 13% -> 0% of each run, Pallas kernels for 36% -> 0%
where the time goes in v3:
time: 246 us
  Pallas kernels  202 us (82%)
  matrix products  36.4 us (15%)
  local copies, waits for them, and re-layouts  5.25 us (2%)
    pallas_call x1, Pallas kernels, reduce(): pl.pallas_call(functools.partial(reduce_kernel, factor), out_shape=[jax.S...  102 us
    pallas_call x1, Pallas kernels, gather(): pl.pallas_call(gather_kernel, out_shape=outs, in_specs=[vmem] * len(shard...  97.5 us
    dot_general x3, matrix products, t_dot(): lax.dot_general(a, b, (((0,), (0,)), ((), ())), preferred_element_type=F32)  13 us
    dot_general x3, matrix products, dot_t(): lax.dot_general(a, b, (((1,), (1,)), ((), ())), preferred_element_type=F32)  12 us
    dot_general x3, matrix products, dot(): return jnp.dot(a, b, preferred_element_type=F32)  11.3 us

profile of v3, /device:TPU:1, one launch (start us, length us, event | category | flops | bytes accessed | tf_op | source)
XLA Modules:
  0.0 245.6 jit_solution(5097654887029480068)
XLA Ops:
  0.7 0.1 pad.3.clone
  0.7 0.7 copy.25
  1.5 0.8 copy.24
  2.2 0.7 copy.26
  3.0 0.7 maximum_maximum_fusion.refs_0_
  3.6 97.5 %gather_and_mix.1 = (bf16[4,2,4,2,16,512]{5,4,3,2,1,0:T(8,128)(2,1)}, bf16[4,2,4,2,16,512]{5,4,3,2,1,0:T(8,128)(2,1)}, bf16[4,2,4,2,16,512]{5,4,3,2,1,0:T(8,128)...) custom-call(bf16[8,128]{1,0:T(8,128)(2,1)} %maximum_maximum_fusion.r, ...), custom_call_target="tpu_custom_call" | custom-call | tf_op jit(solution)/shard_map/gather_and_mix/pallas_call | solution.py:448
  101.1 0.0 copy-start
  101.2 0.0 copy-start.1
  101.2 0.0 slice-start.2
  101.2 5.4 %fusion = f32[512,2304]{1,0:T(8,128)S(1)} fusion(bf16[512,1024]{1,0:T(8,128)(2,1)} %bitcast.62, bf16[2304,1024]{1,0:T(8,128)(2,1)} %bitcast.48), kind=kOutput, calls=%fused_computation.12 | convolution fusion | flops 2415919104 | bytes 10485760 | tf_op jit(solution)/shard_map/dot_general | solution.py:89
  106.6 0.0 copy-done
  106.6 0.0 copy-done.1
  106.6 0.0 slice-start.3
  106.7 2.6 %fusion.1 = f32[512,2304]{1,0:T(8,128)S(1)} fusion(bf16[512,1024]{1,0:T(8,128)(2,1)S(1)} %bitcast.58, bf16[1024,2304]{1,0:T(8,128)(2,1)S(1)} %bitcast.56), kind=kOutput, calls=%fused_computation.13 | convolution fusion | flops 2415919104 | bytes 10485760 | tf_op jit(solution)/shard_map/dot_general | solution.py:85
  109.3 0.0 slice-done.2
  109.3 0.0 slice-done.3
  109.3 4.7 %multiply_convert_fusion = (bf16[512,2304]{1,0:T(8,128)(2,1)S(1)}, bf16[512,2304]{1,0:T(8,128)(2,1)S(1)}, bf16[512,2304]{1,0:T(8,128)(2,1)S(1)}) fusion(f32[512,2304]{1,0:T(8,128)S(1)} %fusion.1, f32[512,2304]{1,0:T(8,128)S(1)} %fusion, bf16[512,1024]{1,0:T(8,128)(2,1)S(1)} %bitcast.59, bf16[1024,2304]{1,0:T(8,128)(2,1)S(1)} %bitcast.54), kind=kOutput, calls=%fused_computation.3 | convolution fusion | flops 2434793472 | bytes 22282240 | tf_op jit(solution)/shard_map/dot_general | solution.py:85
  114.0 0.0 slice-start
  114.0 2.6 %fusion.2 = f32[512,1024]{1,0:T(8,128)S(1)} fusion(bf16[512,2304]{1,0:T(8,128)(2,1)S(1)} %get-tuple-element.101, bf16[1024,2304]{1,0:T(8,128)(2,1)S(1)} %bitcast.57), kind=kOutput, calls=%fused_computation.14 | convolution fusion | flops 2415919104 | bytes 9175040 | tf_op jit(solution)/shard_map/dot_general | solution.py:89
  116.6 0.0 slice-start.1
  116.6 4.0 %convolution_add_fusion = f32[512,1024]{1,0:T(8,128)} fusion(f32[512,1024]{1,0:T(8,128)S(1)} %fusion.2, bf16[512,2304]{1,0:T(8,128)(2,1)S(1)} %get-tuple-element.102, bf16[1024,2304]{1,0:T(8,128)(2,1)S(1)} %bitcast.55), kind=kOutput, calls=%fused_computation.7 | convolution fusion | flops 2416443392 | bytes 11272192 | tf_op jit(solution)/shard_map/dot_general | solution.py:89
  120.6 0.0 slice-done
  120.6 0.0 slice-done.1
  120.6 0.0 copy-start.2
  120.6 4.0 %fusion.3.refs_4_ = f32[2,256,1024]{2,1,0:T(8,128)} fusion(bf16[2,256,2304]{2,1,0:T(8,128)(2,1)S(1)} %bitcast.66, bf16[2304,1024,1]{1,0,2:T(8,128)(2,1)S(1)} %bitcast.51), kind=kOutput, calls=%fused_computation.15 | convolution fusion | flops 2415919104 | bytes 9175040 | tf_op jit(solution)/shard_map/dot_general | solution.py:85
  124.6 0.0 copy-done.2
  124.6 4.3 %convolution_convert_fusion = bf16[2304,1024]{1,0:T(8,128)(2,1)} fusion(bf16[512,2304]{1,0:T(8,128)(2,1)S(1)} %get-tuple-element.100, bf16[512,1024]{1,0:T(8,128)(2,1)S(1)} %bitcast.63), kind=kOutput, calls=%fused_computation | convolution fusion | flops 2418278400 | bytes 8126464 | tf_op jit(solution)/shard_map/dot_general | solution.py:93
  129.0 4.3 %convolution_convert_fusion.2 = bf16[1024,2304]{1,0:T(8,128)(2,1)} fusion(bf16[512,1024]{1,0:T(8,128)(2,1)S(1)} %bitcast.60, bf16[512,2304]{1,0:T(8,128)(2,1)S(1)} %get-tuple-element.101), kind=kOutput, calls=%fused_computation.2 | convolution fusion | flops 2418278400 | bytes 8126464 | tf_op jit(solution)/shard_map/dot_general | solution.py:93
  133.3 4.4 %convolution_convert_fusion.1 = bf16[1024,2304]{1,0:T(8,128)(2,1)} fusion(bf16[512,1024]{1,0:T(8,128)(2,1)S(1)} %bitcast.61, bf16[512,2304]{1,0:T(8,128)(2,1)S(1)} %get-tuple-element.102), kind=kOutput, calls=%fused_computation.1 | convolution fusion | flops 2418278400 | bytes 8126464 | tf_op jit(solution)/shard_map/dot_general | solution.py:93
  137.7 101.8 %sum_gradients.1 = (f32[256,1024]{1,0:T(8,128)}, f32[256,1024]{1,0:T(8,128)}, f32[8,3072]{1,0:T(8,128)}, f32[8,1024]{1,0:T(8,128)}, f32[8,4608]{1,0:T(8,128)}, /...) custom-call(bf16[4,2,4,2,16,2304]{5,4,3,2,1,0:T(8,128)(2,1)} %bitcast.40, ...), custom_call_target="tpu_custom_call" | custom-call | tf_op jit(solution)/shard_map/sum_gradients/pallas_call | solution.py:825
  239.4 3.2 %finish.1 = (f32[256,1024]{1,0:T(8,128)}, f32[256,1024]{1,0:T(8,128)}, f32[8,3072]{1,0:T(8,128)}, f32[8,1024]{1,0:T(8,128)}, f32[8,4608]{1,0:T(8,128)}, /*index=5*/f32[8,4608]{1,0:T(8,128)}, f32[36,1024]{1,0:T(8,128)}) custom-call(f32[256,1024]{1,0:T(8,128)} %get-tuple-element.63.refs_0_, f32[256,1024]{1,0:T(8,128)} %get-tuple-element.64.refs_1_, ...), custom_call_target="tpu_custom_call" | custom-call | tf_op jit(solution)/shard_map/finish/pallas_call | solution.py:881
  242.7 1.5 slice_reduce_fusion
  244.2 0.8 slice_bitcast_fusion
  244.9 0.7 copy.27
  (3 shorter events, 0.0 us)
Async XLA Ops:
  101.1 5.5 %copy-start = (bf16[4,2,4,2,16,2304]{5,4,3,2,1,0:T(8,128)(2,1)S(1)}, bf16[4,2,4,2,16,2304]{5,4,3,2,1,0:T(8,128)(2,1)}, u32[]{:S(2)}) copy-start(bf16[4,2,4,2,16,2304]{5,4,3,2,1,0:T(8,128)(2,1)} %get-tuple-element.48) | copy-start | bytes 14155780
  101.2 5.5 %copy-start.1 = (bf16[2,256,1024]{2,1,0:T(8,128)(2,1)S(1)}, bf16[2,256,1024]{2,1,0:T(8,128)(2,1)}, u32[]{:S(2)}) copy-start(bf16[2,256,1024]{2,1,0:T(8,128)(2,1)} %get-tuple-element.44) | copy-start | bytes 3145732
  101.2 8.1 %slice-start.2 = ((s8[4718592]{0:T(1024)(128)(4,1)}), s8[4194304]{0:T(1024)(128)(4,1)S(1)}, s32[]{:S(2)}) async-start(s8[4718592]{0:T(1024)(128)(4,1)} %bitcast.52), calls=%async_computation.2 | async-start | bytes 8388608
  106.6 2.6 %slice-start.3 = ((s8[4718592]{0:T(1024)(128)(4,1)}), s8[524288]{0:T(1024)(128)(4,1)S(1)}, s32[]{:S(2)}) async-start(s8[4718592]{0:T(1024)(128)(4,1)} %bitcast.52), calls=%async_computation.3 | async-start | bytes 1048576
  114.0 6.6 %slice-start = ((s8[4718592]{0:T(1024)(128)(4,1)}), s8[4194304]{0:T(1024)(128)(4,1)S(1)}, s32[]{:S(2)}) async-start(s8[4718592]{0:T(1024)(128)(4,1)} %bitcast.49), calls=%async_computation | async-start | bytes 8388608
  116.6 4.0 %slice-start.1 = ((s8[4718592]{0:T(1024)(128)(4,1)}), s8[524288]{0:T(1024)(128)(4,1)S(1)}, s32[]{:S(2)}) async-start(s8[4718592]{0:T(1024)(128)(4,1)} %bitcast.49), calls=%async_computation.1 | async-start | bytes 1048576
  120.6 4.0 %copy-start.2 = (bf16[2,256,1024]{2,1,0:T(8,128)(2,1)S(1)}, bf16[2,256,1024]{2,1,0:T(8,128)(2,1)}, u32[]{:S(2)}) copy-start(bf16[2,256,1024]{2,1,0:T(8,128)(2,1)} %get-tuple-element.45) | copy-start | bytes 3145732

commit v4 on v3

--- a/solution.py
+++ b/solution.py
@@ -142,11 +142,12 @@
         del refs[:n]
         return taken
 
-    small_rows, in_rows, out_rows, gate_rows, up_rows, down_rows, tok, cot = take(8)
+    gain1, gain2, tap_rows, in_rows, out_rows, gate_rows, up_rows, down_rows, tok, cot = take(10)
     w_b, w_c, w_x, out_half, gate_full, up_full, down_half, tok_pair, cot_pair = take(9)
     results = take(9)
     (small,) = take(1)
-    given, theirs, block, (down32,) = take(count), take(count), take(count), take(1)
+    given, theirs, block = take(count), take(count), take(count)
+    down32, small32 = take(2)
     full = take(count)
     toks, mix, mix2, outw, halo, cots, landed = take(7)
     res, hid1, hid2, b_mat, c_mat, x_mat, gated, y_mat, cot16 = held = take(9)
@@ -177,6 +178,12 @@
         def _():
             down32[36 * c : 36 * c + 36, :] = down_rows[...].astype(F32)
 
+    small32[...] = jnp.zeros_like(small32)
+    small32[0:1, 0:8] = gain1[...].astype(F32)
+    small32[1:2, 0:8] = gain2[...].astype(F32)
+    small32[2:5, 0:8] = tap_rows[...].astype(F32)
+    small_rows = t_dot(small32[...].astype(BF16), picker())[0:8, :]
+
     def spread(rows):
         both = jnp.concatenate([rows.astype(F32)] * 2, axis=0)
         mine = lax.broadcasted_iota(jnp.int32, both.shape, 0) // 8 == core
@@ -189,7 +196,7 @@
         if k < 3:
             dst[:, 0:HALF] = spread(columns(in_rows, k * WIDTH + half * HALF, HALF))
         if k == 0:
-            dst[:, HALF : HALF + 128] = spread(small_rows[...])
+            dst[:, HALF : HALF + 128] = spread(small_rows)
         elif k < 3:
             dst[:, HALF : HALF + 256] = spread(
                 columns(out_rows, half * HALF + 256 * (k - 1), 256)
@@ -224,12 +231,30 @@
     send(cot, cots.at[core], sibling, 13 * count + 1)
     own_cot = start(pltpu.make_async_copy(cot, cots.at[core], local.at[count + 1]))
 
+    def piece_index(place, whole, late):
+        spot = list(chip_index(place, whole))
+        spot[0 if "y" in whole else 2] = pl.ds(3, 1) if late else pl.ds(0, 3)
+        return tuple(spot)
+
+    def begin_feed(late):
+        for k in FEED:
+            order = ARRAYS[k][1]
+            mine = full[k].at[piece_index(at, order[:2], late)]
+            for by, sem in ((1, 0), (3, 1)):
+                index = 16 * count + 2 * (k - 3) + sem if late else 12 * k + 8 + sem
+                send(mine, mine, device(moved(at, order[2], by), core), index)
+
     def pass_on(k, phase):
         (_, columns), order = ARRAYS[k]
         axis, whole, base = order[phase], order[:phase], 12 * k + 4 * phase
         right, left = moved(at, axis, 1), moved(at, axis, 3)
         for source, part, target, sem in zip((left, right), halves(columns), (right, left), (0, 1)):
-            arrived(full[k].at[chip_index(source, whole)], base + sem)
+            if phase == 2 and k in FEED:
+                for late in range(2):
+                    spot = piece_index(source, whole, late)
+                    arrived(full[k].at[spot], 16 * count + 2 * (k - 3) + sem if late else base + sem)
+            else:
+                arrived(full[k].at[chip_index(source, whole)], base + sem)
             piece = full[k].at[(*chip_index(source, whole), slice(None), part)]
             send(piece, piece, device(target, core), base + 2 + sem)
 
@@ -270,7 +295,7 @@
     each(pass_on, FEED, 1)
     each(complete, FEED, 1)
     each(pass_on, MIXER, 2)
-    each(begin, FEED, 2)
+    begin_feed(False)
     each(complete, MIXER, 2)
     own_out = [
         give_half(
@@ -323,13 +348,10 @@
 
     steps(4, project)
     send(gated.at[:, pl.ds(ROWS, 8), :], halo, next_block(1), 13 * count + 4)
+    begin_feed(True)
     hand_over(1, 3, 4, 5)
-    for k in (1, 2):
-        own_out[k - 1].wait()
-        part = (1 - core, *REST, slice(None), slice(256 * k - 256, 256 * k))
-        arrived(outw.at[part], 14 * count + k)
-    keep(outw, out_half, 22)
     arrived(halo, 13 * count + 4)
+    each(pass_on, FEED, 2)
     starts = lax.axis_index("seq") == 0
     taps = [small[2 + i : 3 + i, tile(core, HALF)] for i in range(3)]
     for c in range(2):
@@ -342,6 +364,12 @@
 
     hand_over(6, 7)
 
+    for k in (1, 2):
+        own_out[k - 1].wait()
+        part = (1 - core, *REST, slice(None), slice(256 * k - 256, 256 * k))
+        arrived(outw.at[part], 14 * count + k)
+    keep(outw, out_half, 22)
+
     def mixing(i):
         c, h, j = lax.div(i, 4), lax.rem(lax.div(i, 2), 2), lax.rem(i, 2)
         weight = outw[h, :, :, :, :, :, tile(j)]
@@ -349,7 +377,6 @@
 
     steps(8, mixing)
     send(mix, mix2, sibling, 13 * count + 3)
-    each(pass_on, FEED, 2)
 
     def columns(half):
         return tile(half, HALF)
@@ -455,6 +482,7 @@
             *blocks,
             *blocks,
             pltpu.VMEM((72, WIDTH), F32),
+            pltpu.VMEM((16, 128), F32),
             *[pltpu.VMEM((*CHIPS, *array), BF16) for array, _ in ARRAYS],
             *[pltpu.VMEM(pair, F32)] * 3,
             pltpu.VMEM((2, 2, 2, 4, 2, 16, HALF), BF16),
@@ -462,8 +490,8 @@
             pltpu.VMEM(pair, F32),
             pltpu.VMEM((2, 2, 4, 2, 72, HALF), BF16),
             *[pltpu.VMEM(value.shape, value.dtype) for value in held],
-            pltpu.SemaphoreType.DMA((16 * count,)),
-            pltpu.SemaphoreType.DMA((16 * count,)),
+            pltpu.SemaphoreType.DMA((17 * count,)),
+            pltpu.SemaphoreType.DMA((17 * count,)),
             pltpu.SemaphoreType.DMA((50,)),
         ],
         compiler_params=pltpu.CompilerParams(
@@ -488,7 +516,7 @@
     data, arriving = take(count), take(12 * count)
     cot, res, hid1, b_mat, c_mat, x_mat, gated, y_mat, outw, small = held = take(10)
     dh, dh2, d1r, dres, g_out, halo, ffn_own, ffn_other = take(8)
-    d_proj, (g_small,) = take(3), take(1)
+    d_proj, (g_small, small_sum) = take(3), take(2)
     sends, recvs, local = refs
     at, core = position()
     sibling = device(at, 1 - core)
@@ -665,11 +693,6 @@
 
     steps(ROWS // 32, add_ffn)
     tok_load = load(in_hbm[13], res, 20)
-    for step in ring[1:]:
-        feed_loads[3, step].wait()
-        feed_loads[4, step].wait()
-        slab(step, False)
-    each(pass_on, FEED, 0)
     for copy in rest_loads:
         copy.wait()
 
@@ -683,6 +706,11 @@
             d_proj[1][c, :, cols] = (d_y * conv).astype(BF16)
             c_mat[c, 0:ROWS, cols] = d_y * c_mat[c, 0:ROWS, cols]
     send(c_mat.at[:, pl.ds(0, 8), :], halo, next_block(31), 12 * count + 3)
+    for step in ring[1:]:
+        feed_loads[3, step].wait()
+        feed_loads[4, step].wait()
+        slab(step, False)
+    each(pass_on, FEED, 0)
 
     def out_grad(i):
         f = i
@@ -795,9 +823,11 @@
         down_grads[:, at_half] = factor * jnp.where(
             core == 0, totals[5][h, 0:36, :], totals[5][h, 36:72, :]
         )
-    small_grads[...] = factor * (
+    small_sum[...] = jnp.zeros_like(small_sum)
+    small_sum[0:8, :] = factor * (
         totals[0][0, mine, HALF : HALF + 128] + totals[0][1, mine, HALF : HALF + 128]
     )
+    small_grads[...] = small_sum[...].T[0:8, :]
     for step in ring:
         slab_sent(step)
     for copy in sent:
@@ -854,6 +884,7 @@
             pltpu.VMEM((ROWS, WIDTH), F32),
             *[pltpu.VMEM((2, ROWS, HALF), BF16)] * 3,
             pltpu.VMEM((16, WIDTH), F32),
+            pltpu.VMEM((128, 128), F32),
             pltpu.SemaphoreType.DMA((16 * count,)),
             pltpu.SemaphoreType.DMA((16 * count,)),
             pltpu.SemaphoreType.DMA((34,)),
@@ -866,23 +897,29 @@
 
 
 def finish_kernel(*refs):
-    count = (len(refs) - 1) // 2
+    count = (len(refs) - 5) // 2
+    small, (one, taps, two) = refs[count], refs[2 * count + 1 : 2 * count + 4]
     copies = [
-        pltpu.make_async_copy(refs[i], refs[count + i], refs[-1].at[i]) for i in range(count)
+        pltpu.make_async_copy(refs[i], refs[count + 1 + i], refs[-1].at[i]) for i in range(count)
     ]
     for copy in copies:
         copy.start()
+    one[...] = small[0:1, 0:8]
+    two[...] = small[1:2, 0:8]
+    taps[...] = small[2:5, 0:8]
     for copy in copies:
         copy.wait()
 
 
 def finish(*values):
     hbm, vmem = pl.BlockSpec(memory_space=pl.ANY), pl.BlockSpec(memory_space=pltpu.VMEM)
+    outs = [jax.ShapeDtypeStruct(v.shape, v.dtype) for v in values[:-1]]
+    rows = [jax.ShapeDtypeStruct((r, 8), F32) for r in (1, 3, 1)]
     return pl.pallas_call(
         finish_kernel,
-        out_shape=[jax.ShapeDtypeStruct(v.shape, v.dtype) for v in values],
+        out_shape=outs + rows,
         in_specs=[vmem] * len(values),
-        out_specs=[hbm] * len(values),
+        out_specs=[hbm] * len(outs) + [vmem] * 3,
         scratch_shapes=[pltpu.SemaphoreType.DMA((len(values),))],
         name="finish",
     )(*values)
@@ -908,11 +945,16 @@
     factor = 1.0 / math.sqrt(total_rows)
     core = lax.rem(lax.axis_index("fsdp"), 2)
 
-    small = jnp.concatenate(
-        [norm1_gain[:, None], norm2_gain[:, None], conv_taps.T, jnp.zeros((8, 123), BF16)], axis=1
+    pieces = (
+        norm1_gain.reshape(1, -1),
+        norm2_gain.reshape(1, -1),
+        conv_taps,
+        in_weight,
+        out_weight,
+        gate_weight,
+        up_weight,
+        down_weight,
     )
-
-    pieces = (small, in_weight, out_weight, gate_weight, up_weight, down_weight)
     w_b, w_c, w_x, w_out, w_gate, w_up, w_down, tok, cot, *kept = gather(pieces, inputs, upstream)
     resid, hidden_one, hidden_two, b_mat, c_mat, x_mat, gated, y_mat, cot_half, small = kept
     w_gate = w_gate.reshape(width, -1)
@@ -954,17 +996,17 @@
         tok,
     )
 
-    block_out, input_grad, g_in, g_out, g_gate, g_up, g_down = finish(
-        block_out, input_grad, g_in, g_out, g_gate, g_up, g_down
+    block_out, input_grad, g_in, g_out, g_gate, g_up, g_down, g_one, g_taps, g_two = finish(
+        block_out, input_grad, g_in, g_out, g_gate, g_up, g_down, g_small
     )
     return (
         block_out.reshape(tokens.shape),
         input_grad.reshape(tokens.shape),
-        g_small[:, 0],
+        g_one.reshape(-1),
         g_in,
-        g_small[:, 2:5].T,
+        g_taps,
         g_out,
-        g_small[:, 1],
+        g_two.reshape(-1),
         g_gate,
         g_up,
         g_down,

time: 246 us -> 224 us (0.911)
  Pallas kernels: 202 us -> 186 us
  local copies, waits for them, and re-layouts: 5.25 us -> 0.03 us
    pallas_call x1, Pallas kernels: 102 us -> 88.8 us  [reduce(): pl.pallas_call(functools.partial(reduce_kernel, factor), out_shape=[jax.S...]
    pallas_call x1, Pallas kernels: 97.5 us -> 93.8 us  [gather(): pl.pallas_call(gather_kernel, out_shape=outs, in_specs=[vmem] * len(shard...]
where the time goes in v4:
time: 224 us
  Pallas kernels  186 us (83%)
  matrix products  36.4 us (16%)
    pallas_call x1, Pallas kernels, gather(): pl.pallas_call(gather_kernel, out_shape=outs, in_specs=[vmem] * len(shard...  93.8 us
    pallas_call x1, Pallas kernels, reduce(): pl.pallas_call(functools.partial(reduce_kernel, factor), out_shape=[jax.S...  88.8 us
    dot_general x3, matrix products, t_dot(): lax.dot_general(a, b, (((0,), (0,)), ((), ())), preferred_element_type=F32)  13 us
    dot_general x3, matrix products, dot_t(): lax.dot_general(a, b, (((1,), (1,)), ((), ())), preferred_element_type=F32)  12.1 us
    dot_general x3, matrix products, dot(): return jnp.dot(a, b, preferred_element_type=F32)  11.3 us

profile of v4, /device:TPU:1, one launch (start us, length us, event | category | flops | bytes accessed | tf_op | source)
XLA Modules:
  0.0 223.8 jit_solution(4360540746175973991)
XLA Ops:
  0.6 93.8 %gather_and_mix.1 = (bf16[4,2,4,2,16,512]{5,4,3,2,1,0:T(8,128)(2,1)}, bf16[4,2,4,2,16,512]{5,4,3,2,1,0:T(8,128)(2,1)}, bf16[4,2,4,2,16,512]{5,4,3,2,1,0:T(8,128)...) custom-call(bf16[1,8]{1,0:T(2,128)(2,1)} %bitcast.44, ...), custom_call_target="tpu_custom_call" | custom-call | tf_op jit(solution)/shard_map/gather_and_mix/pallas_call | solution.py:475
  94.5 0.0 copy-start
  94.5 0.0 copy-start.1
  94.5 0.0 slice-start.2
  94.5 5.4 %fusion = f32[512,2304]{1,0:T(8,128)S(1)} fusion(bf16[512,1024]{1,0:T(8,128)(2,1)} %bitcast.60, bf16[2304,1024]{1,0:T(8,128)(2,1)} %bitcast.46), kind=kOutput, calls=%fused_computation.8 | convolution fusion | flops 2415919104 | bytes 10485760 | tf_op jit(solution)/shard_map/dot_general | solution.py:89
  100.0 0.0 copy-done
  100.0 0.0 copy-done.1
  100.0 0.0 slice-start.3
  100.0 2.6 %fusion.1 = f32[512,2304]{1,0:T(8,128)S(1)} fusion(bf16[512,1024]{1,0:T(8,128)(2,1)S(1)} %bitcast.56, bf16[1024,2304]{1,0:T(8,128)(2,1)S(1)} %bitcast.54), kind=kOutput, calls=%fused_computation.9 | convolution fusion | flops 2415919104 | bytes 10485760 | tf_op jit(solution)/shard_map/dot_general | solution.py:85
  102.6 0.0 slice-done.2
  102.6 0.0 slice-done.3
  102.6 4.7 %multiply_convert_fusion = (bf16[512,2304]{1,0:T(8,128)(2,1)S(1)}, bf16[512,2304]{1,0:T(8,128)(2,1)S(1)}, bf16[512,2304]{1,0:T(8,128)(2,1)S(1)}) fusion(f32[512,2304]{1,0:T(8,128)S(1)} %fusion.1, f32[512,2304]{1,0:T(8,128)S(1)} %fusion, bf16[512,1024]{1,0:T(8,128)(2,1)S(1)} %bitcast.57, bf16[1024,2304]{1,0:T(8,128)(2,1)S(1)} %bitcast.52), kind=kOutput, calls=%fused_computation.3 | convolution fusion | flops 2434793472 | bytes 22282240 | tf_op jit(solution)/shard_map/dot_general | solution.py:85
  107.3 0.0 slice-start
  107.3 2.6 %fusion.2 = f32[512,1024]{1,0:T(8,128)S(1)} fusion(bf16[512,2304]{1,0:T(8,128)(2,1)S(1)} %get-tuple-element.85, bf16[1024,2304]{1,0:T(8,128)(2,1)S(1)} %bitcast.55), kind=kOutput, calls=%fused_computation.10 | convolution fusion | flops 2415919104 | bytes 9175040 | tf_op jit(solution)/shard_map/dot_general | solution.py:89
  110.0 0.0 slice-start.1
  110.0 4.0 %convolution_add_fusion = f32[512,1024]{1,0:T(8,128)} fusion(f32[512,1024]{1,0:T(8,128)S(1)} %fusion.2, bf16[512,2304]{1,0:T(8,128)(2,1)S(1)} %get-tuple-element.86, bf16[1024,2304]{1,0:T(8,128)(2,1)S(1)} %bitcast.53), kind=kOutput, calls=%fused_computation.7 | convolution fusion | flops 2416443392 | bytes 11272192 | tf_op jit(solution)/shard_map/dot_general | solution.py:89
  114.0 0.0 slice-done
  114.0 0.0 slice-done.1
  114.0 0.0 copy-start.2
  114.0 4.0 %fusion.3.refs_4_ = f32[2,256,1024]{2,1,0:T(8,128)} fusion(bf16[2,256,2304]{2,1,0:T(8,128)(2,1)S(1)} %bitcast.66, bf16[2304,1024,1]{1,0,2:T(8,128)(2,1)S(1)} %bitcast.49), kind=kOutput, calls=%fused_computation.11 | convolution fusion | flops 2415919104 | bytes 9175040 | tf_op jit(solution)/shard_map/dot_general | solution.py:85
  118.0 0.0 copy-done.2
  118.0 4.4 %convolution_convert_fusion = bf16[2304,1024]{1,0:T(8,128)(2,1)} fusion(bf16[512,2304]{1,0:T(8,128)(2,1)S(1)} %get-tuple-element.84, bf16[512,1024]{1,0:T(8,128)(2,1)S(1)} %bitcast.61), kind=kOutput, calls=%fused_computation | convolution fusion | flops 2418278400 | bytes 8126464 | tf_op jit(solution)/shard_map/dot_general | solution.py:93
  122.3 4.3 %convolution_convert_fusion.2 = bf16[1024,2304]{1,0:T(8,128)(2,1)} fusion(bf16[512,1024]{1,0:T(8,128)(2,1)S(1)} %bitcast.58, bf16[512,2304]{1,0:T(8,128)(2,1)S(1)} %get-tuple-element.85), kind=kOutput, calls=%fused_computation.2 | convolution fusion | flops 2418278400 | bytes 8126464 | tf_op jit(solution)/shard_map/dot_general | solution.py:93
  126.6 4.4 %convolution_convert_fusion.1 = bf16[1024,2304]{1,0:T(8,128)(2,1)} fusion(bf16[512,1024]{1,0:T(8,128)(2,1)S(1)} %bitcast.59, bf16[512,2304]{1,0:T(8,128)(2,1)S(1)} %get-tuple-element.86), kind=kOutput, calls=%fused_computation.1 | convolution fusion | flops 2418278400 | bytes 8126464 | tf_op jit(solution)/shard_map/dot_general | solution.py:93
  131.0 88.8 %sum_gradients.1 = (f32[256,1024]{1,0:T(8,128)}, f32[256,1024]{1,0:T(8,128)}, f32[8,3072]{1,0:T(8,128)}, f32[8,1024]{1,0:T(8,128)}, f32[8,4608]{1,0:T(8,128)}, /...) custom-call(bf16[4,2,4,2,16,2304]{5,4,3,2,1,0:T(8,128)(2,1)} %bitcast.39, ...), custom_call_target="tpu_custom_call" | custom-call | tf_op jit(solution)/shard_map/sum_gradients/pallas_call | solution.py:855
  219.8 3.9 %finish.1 = (f32[256,1024]{1,0:T(8,128)}, f32[256,1024]{1,0:T(8,128)}, f32[8,3072]{1,0:T(8,128)}, f32[8,1024]{1,0:T(8,128)}, f32[8,4608]{1,0:T(8,128)}, /*index=...) custom-call(f32[256,1024]{1,0:T(8,128)} %get-tuple-element.66.refs_0_, ...), custom_call_target="tpu_custom_call" | custom-call | tf_op jit(solution)/shard_map/finish/pallas_call | solution.py:918
  (2 shorter events, 0.0 us)
Async XLA Ops:
  94.5 5.5 %copy-start = (bf16[4,2,4,2,16,2304]{5,4,3,2,1,0:T(8,128)(2,1)S(1)}, bf16[4,2,4,2,16,2304]{5,4,3,2,1,0:T(8,128)(2,1)}, u32[]{:S(2)}) copy-start(bf16[4,2,4,2,16,2304]{5,4,3,2,1,0:T(8,128)(2,1)} %get-tuple-element.51) | copy-start | bytes 14155780
  94.5 5.5 %copy-start.1 = (bf16[2,256,1024]{2,1,0:T(8,128)(2,1)S(1)}, bf16[2,256,1024]{2,1,0:T(8,128)(2,1)}, u32[]{:S(2)}) copy-start(bf16[2,256,1024]{2,1,0:T(8,128)(2,1)} %get-tuple-element.47) | copy-start | bytes 3145732
  94.5 8.1 %slice-start.2 = ((s8[4718592]{0:T(1024)(128)(4,1)}), s8[4194304]{0:T(1024)(128)(4,1)S(1)}, s32[]{:S(2)}) async-start(s8[4718592]{0:T(1024)(128)(4,1)} %bitcast.50), calls=%async_computation.2 | async-start | bytes 8388608
  100.0 2.6 %slice-start.3 = ((s8[4718592]{0:T(1024)(128)(4,1)}), s8[524288]{0:T(1024)(128)(4,1)S(1)}, s32[]{:S(2)}) async-start(s8[4718592]{0:T(1024)(128)(4,1)} %bitcast.50), calls=%async_computation.3 | async-start | bytes 1048576
  107.3 6.6 %slice-start = ((s8[4718592]{0:T(1024)(128)(4,1)}), s8[4194304]{0:T(1024)(128)(4,1)S(1)}, s32[]{:S(2)}) async-start(s8[4718592]{0:T(1024)(128)(4,1)} %bitcast.47), calls=%async_computation | async-start | bytes 8388608
  110.0 4.0 %slice-start.1 = ((s8[4718592]{0:T(1024)(128)(4,1)}), s8[524288]{0:T(1024)(128)(4,1)S(1)}, s32[]{:S(2)}) async-start(s8[4718592]{0:T(1024)(128)(4,1)} %bitcast.47), calls=%async_computation.1 | async-start | bytes 1048576
  114.0 4.0 %copy-start.2 = (bf16[2,256,1024]{2,1,0:T(8,128)(2,1)S(1)}, bf16[2,256,1024]{2,1,0:T(8,128)(2,1)}, u32[]{:S(2)}) copy-start(bf16[2,256,1024]{2,1,0:T(8,128)(2,1)} %get-tuple-element.48) | copy-start | bytes 3145732

commit v5 on v4

--- a/solution.py
+++ b/solution.py
@@ -54,16 +54,19 @@
     return slice(0, first), slice(first, columns)
 
 
-def enter(at, core):
+def arrive(at, core):
     barrier = pltpu.get_barrier_semaphore()
     for axis in "xyz":
-        for by in (1, 3):
+        for by in (1, 2, 3):
             pl.semaphore_signal(
                 barrier, inc=1, device_id=device(moved(at, axis, by), core), device_id_type=MESH
             )
     for other in (device(at, 1 - core), next_block(1), next_block(31)):
         pl.semaphore_signal(barrier, inc=1, device_id=other, device_id_type=MESH)
-    pl.semaphore_wait(barrier, 9)
+
+
+def meet():
+    pl.semaphore_wait(pltpu.get_barrier_semaphore(), 12)
 
 
 def next_block(by):
@@ -154,7 +157,7 @@
     sends, recvs, local = refs
     at, core = position()
     sibling = device(at, 1 - core)
-    enter(at, core)
+    arrive(at, core)
     sent, kept = [], []
 
     def start(copy):
@@ -208,9 +211,10 @@
 
     for k in range(count):
         fill(k, 1 - core, given[k])
+        fill(k, core, block[k])
+    meet()
+    for k in range(count):
         send(given[k], theirs[k], sibling, 12 * count + k)
-    for k in range(count):
-        fill(k, core, block[k])
     own_copies = []
     here = (at["y"], lax.rem(at["x"], 2), at["z"], lax.div(at["x"], 2))
     for k in range(count):
@@ -219,7 +223,7 @@
         own_copies.append(
             start(pltpu.make_async_copy(block[k], full[k].at[here], local.at[k]))
         )
-        for by, sem in ((1, 0), (3, 1)):
+        for by, sem in ((1, 0), (3, 1), (2, 2)):
             send(
                 block[k],
                 full[k].at[here],
@@ -261,11 +265,14 @@
     def complete(k, phase):
         (_, columns), order = ARRAYS[k]
         whole, base = order[:phase], 12 * k + 4 * phase
+        if phase == 0:
+            for by, sem in ((3, 0), (1, 1), (2, 2)):
+                arrived(full[k].at[chip_index(moved(at, order[0], by), whole)], base + sem)
+            own_copies[k].wait()
+            return
         across = moved(at, order[phase], 2)
         for part, sem in zip(halves(columns), (2, 3)):
             arrived(full[k].at[(*chip_index(across, whole), slice(None), part)], base + sem)
-        if phase == 0:
-            own_copies[k].wait()
 
     def begin(k, phase):
         order = ARRAYS[k][1]
@@ -283,8 +290,6 @@
         for k in arrays:
             step(k, phase)
 
-    each(pass_on, MIXER, 0)
-    each(pass_on, FEED, 0)
     each(complete, MIXER, 0)
     each(begin, MIXER, 1)
     each(complete, FEED, 0)
@@ -520,7 +525,7 @@
     sends, recvs, local = refs
     at, core = position()
     sibling = device(at, 1 - core)
-    enter(at, core)
+    arrive(at, core)
     sent = []
 
     def send(src, dst, target, sem):
@@ -570,6 +575,12 @@
     def begin(k, phase):
         (_, columns), order = ARRAYS[k]
         axis, whole = order[2 - phase], order[: 2 - phase]
+        if phase == 2:
+            for by, which in ((1, 0), (3, 1), (2, 2)):
+                other = moved(at, axis, by)
+                src = data[k].at[chip_index(other, whole)]
+                send(src, buffer(k, 2, which), device(other, core), 12 * k + 8 + which)
+            return
         across = chip_index(moved(at, axis, 2), whole)
         for part, which, by in zip(halves(columns), (0, 1), (1, 3)):
             send(
@@ -597,9 +608,10 @@
     def complete(k, phase):
         whole = ARRAYS[k][1][: 2 - phase]
         base = 12 * k + 4 * phase
-        both = [buffer(k, phase, 2), buffer(k, phase, 3)]
-        arrived(both[0], base + 2)
-        arrived(both[1], base + 3)
+        which = (0, 1, 2) if phase == 2 else (2, 3)
+        both = [buffer(k, phase, w) for w in which]
+        for w, source in zip(which, both):
+            arrived(source, base + w)
         total = totals[k].at[core] if phase == 2 else None
         add(k, phase, start_of(at, whole), both, slice(None), total)
         if phase < 2:
@@ -611,7 +623,7 @@
         for k in arrays:
             step(k, phase)
 
-    def slab(step, start):
+    def slab(step, action):
         y = lax.rem(at["y"] + step, 4)
         here, there = lax.div(y, 2), lax.rem(y, 2)
 
@@ -623,15 +635,16 @@
 
         @pl.when(here == core)
         def _():
-            if start:
+            if action == "load":
+                own.start()
+            elif action == "give":
                 given.start()
-                own.start()
             else:
                 own.wait()
 
         @pl.when(here != core)
         def _():
-            if not start:
+            if action == "wait":
                 given.wait_recv()
 
     def slab_sent(step):
@@ -650,9 +663,7 @@
             order = ARRAYS[k][1]
             spot = chip_index(moved(at, order[2], step), order[:2])
             feed_loads[k, step] = load(src.at[spot], data[k].at[spot], 25 + 4 * (k - 3) + step)
-        slab(step, True)
-    send(d_hid2, dh2, sibling, 12 * count)
-    send(out_part.at[1 - core], ffn_other, sibling, 12 * count + 2)
+        slab(step, "load")
     first_loads = [load(d_hid2, dh, 6)]
     first_loads += [load(in_hbm[i], held[i], 7 + i) for i in (0, 1, 9)]
     rest_loads = [load(in_hbm[i], held[i], 7 + i) for i in range(2, 9)]
@@ -660,11 +671,17 @@
     for k in MIXER:
         dst = data[k].at[(*REST, slice(None), left)]
         rest_loads.append(load(in_hbm[10 + k], dst, 17 + k))
+    meet()
+    slab(2, "give")
     for k in (3, 4):
         feed_loads[k, 2].wait()
         begin(k, 0)
-    slab(2, False)
+    send(d_hid2, dh2, sibling, 12 * count)
+    slab(2, "wait")
     begin(5, 0)
+    for step in ring[1:]:
+        slab(step, "give")
+    send(out_part.at[1 - core], ffn_other, sibling, 12 * count + 2)
     ffn_load = load(out_part.at[core], ffn_own, 33)
     for copy in first_loads:
         copy.wait()
@@ -709,7 +726,7 @@
     for step in ring[1:]:
         feed_loads[3, step].wait()
         feed_loads[4, step].wait()
-        slab(step, False)
+        slab(step, "wait")
     each(pass_on, FEED, 0)
 
     def out_grad(i):
@@ -801,10 +818,8 @@
     each(complete, MIXER, 0)
     each(complete, FEED, 1)
     each(pass_on, MIXER, 1)
-    each(pass_on, FEED, 2)
     each(complete, MIXER, 1)
     each(complete, FEED, 2)
-    each(pass_on, MIXER, 2)
     each(complete, MIXER, 2)
     for k in range(count):
         arrived(totals[k].at[1 - core], 13 * count + k)
@@ -847,6 +862,10 @@
                 4 if "z" in whole else 1,
                 2 if "x" in whole else 1,
             )
+            if phase == 2:
+                buffers += [pltpu.VMEM((*lead, rows, columns), BF16)] * 3
+                buffers.append(pltpu.VMEM((16, 128), BF16))
+                continue
             for part in halves(columns):
                 buffers.append(pltpu.VMEM((*lead, rows, part.stop - part.start), BF16))
             buffers += [pltpu.VMEM((*lead, rows, columns), BF16)] * 2

time: 224 us -> 222 us (level)
    pallas_call x1, Pallas kernels: 88.8 us -> 85.6 us  [reduce(): pl.pallas_call(functools.partial(reduce_kernel, factor), out_shape=[jax.S...]
where the time goes in v5:
time: 222 us
  Pallas kernels  184 us (83%)
  matrix products  36.4 us (16%)
    pallas_call x1, Pallas kernels, gather(): pl.pallas_call(gather_kernel, out_shape=outs, in_specs=[vmem] * len(shard...  94.7 us
    pallas_call x1, Pallas kernels, reduce(): pl.pallas_call(functools.partial(reduce_kernel, factor), out_shape=[jax.S...  85.6 us
    dot_general x3, matrix products, t_dot(): lax.dot_general(a, b, (((0,), (0,)), ((), ())), preferred_element_type=F32)  13 us
    dot_general x3, matrix products, dot_t(): lax.dot_general(a, b, (((1,), (1,)), ((), ())), preferred_element_type=F32)  12.1 us
    dot_general x3, matrix products, dot(): return jnp.dot(a, b, preferred_element_type=F32)  11.3 us

profile of v5, /device:TPU:1, one launch (start us, length us, event | category | flops | bytes accessed | tf_op | source)
XLA Modules:
  0.0 221.6 jit_solution(15139299290276316776)
XLA Ops:
  0.6 94.7 %gather_and_mix.1 = (bf16[4,2,4,2,16,512]{5,4,3,2,1,0:T(8,128)(2,1)}, bf16[4,2,4,2,16,512]{5,4,3,2,1,0:T(8,128)(2,1)}, bf16[4,2,4,2,16,512]{5,4,3,2,1,0:T(8,128)...) custom-call(bf16[1,8]{1,0:T(2,128)(2,1)} %bitcast.44, ...), custom_call_target="tpu_custom_call" | custom-call | tf_op jit(solution)/shard_map/gather_and_mix/pallas_call | solution.py:480
  95.4 0.0 copy-start
  95.4 0.0 copy-start.1
  95.4 0.0 slice-start.2
  95.4 5.4 %fusion = f32[512,2304]{1,0:T(8,128)S(1)} fusion(bf16[512,1024]{1,0:T(8,128)(2,1)} %bitcast.60, bf16[2304,1024]{1,0:T(8,128)(2,1)} %bitcast.46), kind=kOutput, calls=%fused_computation.8 | convolution fusion | flops 2415919104 | bytes 10485760 | tf_op jit(solution)/shard_map/dot_general | solution.py:92
  100.9 0.0 copy-done
  100.9 0.0 copy-done.1
  100.9 0.0 slice-start.3
  100.9 2.6 %fusion.1 = f32[512,2304]{1,0:T(8,128)S(1)} fusion(bf16[512,1024]{1,0:T(8,128)(2,1)S(1)} %bitcast.56, bf16[1024,2304]{1,0:T(8,128)(2,1)S(1)} %bitcast.54), kind=kOutput, calls=%fused_computation.9 | convolution fusion | flops 2415919104 | bytes 10485760 | tf_op jit(solution)/shard_map/dot_general | solution.py:88
  103.5 0.0 slice-done.2
  103.5 0.0 slice-done.3
  103.6 4.7 %multiply_convert_fusion = (bf16[512,2304]{1,0:T(8,128)(2,1)S(1)}, bf16[512,2304]{1,0:T(8,128)(2,1)S(1)}, bf16[512,2304]{1,0:T(8,128)(2,1)S(1)}) fusion(f32[512,2304]{1,0:T(8,128)S(1)} %fusion.1, f32[512,2304]{1,0:T(8,128)S(1)} %fusion, bf16[512,1024]{1,0:T(8,128)(2,1)S(1)} %bitcast.57, bf16[1024,2304]{1,0:T(8,128)(2,1)S(1)} %bitcast.52), kind=kOutput, calls=%fused_computation.3 | convolution fusion | flops 2434793472 | bytes 22282240 | tf_op jit(solution)/shard_map/dot_general | solution.py:88
  108.3 0.0 slice-start
  108.3 2.6 %fusion.2 = f32[512,1024]{1,0:T(8,128)S(1)} fusion(bf16[512,2304]{1,0:T(8,128)(2,1)S(1)} %get-tuple-element.85, bf16[1024,2304]{1,0:T(8,128)(2,1)S(1)} %bitcast.55), kind=kOutput, calls=%fused_computation.10 | convolution fusion | flops 2415919104 | bytes 9175040 | tf_op jit(solution)/shard_map/dot_general | solution.py:92
  110.9 0.0 slice-start.1
  110.9 4.0 %convolution_add_fusion = f32[512,1024]{1,0:T(8,128)} fusion(f32[512,1024]{1,0:T(8,128)S(1)} %fusion.2, bf16[512,2304]{1,0:T(8,128)(2,1)S(1)} %get-tuple-element.86, bf16[1024,2304]{1,0:T(8,128)(2,1)S(1)} %bitcast.53), kind=kOutput, calls=%fused_computation.7 | convolution fusion | flops 2416443392 | bytes 11272192 | tf_op jit(solution)/shard_map/dot_general | solution.py:92
  114.9 0.0 slice-done
  114.9 0.0 slice-done.1
  114.9 0.0 copy-start.2
  114.9 4.0 %fusion.3.refs_4_ = f32[2,256,1024]{2,1,0:T(8,128)} fusion(bf16[2,256,2304]{2,1,0:T(8,128)(2,1)S(1)} %bitcast.66, bf16[2304,1024,1]{1,0,2:T(8,128)(2,1)S(1)} %bitcast.49), kind=kOutput, calls=%fused_computation.11 | convolution fusion | flops 2415919104 | bytes 9175040 | tf_op jit(solution)/shard_map/dot_general | solution.py:88
  118.9 0.0 copy-done.2
  118.9 4.4 %convolution_convert_fusion = bf16[2304,1024]{1,0:T(8,128)(2,1)} fusion(bf16[512,2304]{1,0:T(8,128)(2,1)S(1)} %get-tuple-element.84, bf16[512,1024]{1,0:T(8,128)(2,1)S(1)} %bitcast.61), kind=kOutput, calls=%fused_computation | convolution fusion | flops 2418278400 | bytes 8126464 | tf_op jit(solution)/shard_map/dot_general | solution.py:96
  123.2 4.3 %convolution_convert_fusion.2 = bf16[1024,2304]{1,0:T(8,128)(2,1)} fusion(bf16[512,1024]{1,0:T(8,128)(2,1)S(1)} %bitcast.58, bf16[512,2304]{1,0:T(8,128)(2,1)S(1)} %get-tuple-element.85), kind=kOutput, calls=%fused_computation.2 | convolution fusion | flops 2418278400 | bytes 8126464 | tf_op jit(solution)/shard_map/dot_general | solution.py:96
  127.6 4.4 %convolution_convert_fusion.1 = bf16[1024,2304]{1,0:T(8,128)(2,1)} fusion(bf16[512,1024]{1,0:T(8,128)(2,1)S(1)} %bitcast.59, bf16[512,2304]{1,0:T(8,128)(2,1)S(1)} %get-tuple-element.86), kind=kOutput, calls=%fused_computation.1 | convolution fusion | flops 2418278400 | bytes 8126464 | tf_op jit(solution)/shard_map/dot_general | solution.py:96
  131.9 85.6 %sum_gradients.1 = (f32[256,1024]{1,0:T(8,128)}, f32[256,1024]{1,0:T(8,128)}, f32[8,3072]{1,0:T(8,128)}, f32[8,1024]{1,0:T(8,128)}, f32[8,4608]{1,0:T(8,128)}, /...) custom-call(bf16[4,2,4,2,16,2304]{5,4,3,2,1,0:T(8,128)(2,1)} %bitcast.39, ...), custom_call_target="tpu_custom_call" | custom-call | tf_op jit(solution)/shard_map/sum_gradients/pallas_call | solution.py:874
  217.5 3.9 %finish.1 = (f32[256,1024]{1,0:T(8,128)}, f32[256,1024]{1,0:T(8,128)}, f32[8,3072]{1,0:T(8,128)}, f32[8,1024]{1,0:T(8,128)}, f32[8,4608]{1,0:T(8,128)}, /*index=...) custom-call(f32[256,1024]{1,0:T(8,128)} %get-tuple-element.66.refs_0_, ...), custom_call_target="tpu_custom_call" | custom-call | tf_op jit(solution)/shard_map/finish/pallas_call | solution.py:937
  (2 shorter events, 0.0 us)
Async XLA Ops:
  95.4 5.5 %copy-start = (bf16[4,2,4,2,16,2304]{5,4,3,2,1,0:T(8,128)(2,1)S(1)}, bf16[4,2,4,2,16,2304]{5,4,3,2,1,0:T(8,128)(2,1)}, u32[]{:S(2)}) copy-start(bf16[4,2,4,2,16,2304]{5,4,3,2,1,0:T(8,128)(2,1)} %get-tuple-element.51) | copy-start | bytes 14155780
  95.4 5.5 %copy-start.1 = (bf16[2,256,1024]{2,1,0:T(8,128)(2,1)S(1)}, bf16[2,256,1024]{2,1,0:T(8,128)(2,1)}, u32[]{:S(2)}) copy-start(bf16[2,256,1024]{2,1,0:T(8,128)(2,1)} %get-tuple-element.47) | copy-start | bytes 3145732
  95.4 8.1 %slice-start.2 = ((s8[4718592]{0:T(1024)(128)(4,1)}), s8[4194304]{0:T(1024)(128)(4,1)S(1)}, s32[]{:S(2)}) async-start(s8[4718592]{0:T(1024)(128)(4,1)} %bitcast.50), calls=%async_computation.2 | async-start | bytes 8388608
  100.9 2.6 %slice-start.3 = ((s8[4718592]{0:T(1024)(128)(4,1)}), s8[524288]{0:T(1024)(128)(4,1)S(1)}, s32[]{:S(2)}) async-start(s8[4718592]{0:T(1024)(128)(4,1)} %bitcast.50), calls=%async_computation.3 | async-start | bytes 1048576
  108.3 6.6 %slice-start = ((s8[4718592]{0:T(1024)(128)(4,1)}), s8[4194304]{0:T(1024)(128)(4,1)S(1)}, s32[]{:S(2)}) async-start(s8[4718592]{0:T(1024)(128)(4,1)} %bitcast.47), calls=%async_computation | async-start | bytes 8388608
  110.9 4.0 %slice-start.1 = ((s8[4718592]{0:T(1024)(128)(4,1)}), s8[524288]{0:T(1024)(128)(4,1)S(1)}, s32[]{:S(2)}) async-start(s8[4718592]{0:T(1024)(128)(4,1)} %bitcast.47), calls=%async_computation.1 | async-start | bytes 1048576
  114.9 4.0 %copy-start.2 = (bf16[2,256,1024]{2,1,0:T(8,128)(2,1)S(1)}, bf16[2,256,1024]{2,1,0:T(8,128)(2,1)}, u32[]{:S(2)}) copy-start(bf16[2,256,1024]{2,1,0:T(8,128)(2,1)} %get-tuple-element.48) | copy-start | bytes 3145732

commit v6 on v5

--- a/solution.py
+++ b/solution.py
@@ -237,7 +237,7 @@
 
     def piece_index(place, whole, late):
         spot = list(chip_index(place, whole))
-        spot[0 if "y" in whole else 2] = pl.ds(3, 1) if late else pl.ds(0, 3)
+        spot[0 if "y" in whole else 2] = pl.ds(2, 2) if late else pl.ds(0, 2)
         return tuple(spot)
 
     def begin_feed(late):
@@ -296,8 +296,8 @@
     each(begin, FEED, 1)
     each(pass_on, MIXER, 1)
     each(complete, MIXER, 1)
+    each(pass_on, FEED, 1)
     each(begin, MIXER, 2)
-    each(pass_on, FEED, 1)
     each(complete, FEED, 1)
     each(pass_on, MIXER, 2)
     begin_feed(False)

time: 222 us -> 221 us (level)
  no operation moved by 1% of the time
where the time goes in v6:
time: 221 us
  Pallas kernels  183 us (83%)
  matrix products  36.4 us (16%)
    pallas_call x1, Pallas kernels, gather(): pl.pallas_call(gather_kernel, out_shape=outs, in_specs=[vmem] * len(shard...  93.4 us
    pallas_call x1, Pallas kernels, reduce(): pl.pallas_call(functools.partial(reduce_kernel, factor), out_shape=[jax.S...  86 us
    dot_general x3, matrix products, t_dot(): lax.dot_general(a, b, (((0,), (0,)), ((), ())), preferred_element_type=F32)  13 us
    dot_general x3, matrix products, dot_t(): lax.dot_general(a, b, (((1,), (1,)), ((), ())), preferred_element_type=F32)  12.1 us
    dot_general x3, matrix products, dot(): return jnp.dot(a, b, preferred_element_type=F32)  11.3 us

profile of v6, /device:TPU:1, one launch (start us, length us, event | category | flops | bytes accessed | tf_op | source)
XLA Modules:
  0.0 220.6 jit_solution(5522956680421032536)
XLA Ops:
  0.6 93.4 %gather_and_mix.1 = (bf16[4,2,4,2,16,512]{5,4,3,2,1,0:T(8,128)(2,1)}, bf16[4,2,4,2,16,512]{5,4,3,2,1,0:T(8,128)(2,1)}, bf16[4,2,4,2,16,512]{5,4,3,2,1,0:T(8,128)...) custom-call(bf16[1,8]{1,0:T(2,128)(2,1)} %bitcast.44, ...), custom_call_target="tpu_custom_call" | custom-call | tf_op jit(solution)/shard_map/gather_and_mix/pallas_call | solution.py:480
  94.0 0.0 copy-start
  94.0 0.0 copy-start.1
  94.1 0.0 slice-start.2
  94.1 5.4 %fusion = f32[512,2304]{1,0:T(8,128)S(1)} fusion(bf16[512,1024]{1,0:T(8,128)(2,1)} %bitcast.60, bf16[2304,1024]{1,0:T(8,128)(2,1)} %bitcast.46), kind=kOutput, calls=%fused_computation.8 | convolution fusion | flops 2415919104 | bytes 10485760 | tf_op jit(solution)/shard_map/dot_general | solution.py:92
  99.5 0.0 copy-done
  99.5 0.0 copy-done.1
  99.5 0.0 slice-start.3
  99.6 2.6 %fusion.1 = f32[512,2304]{1,0:T(8,128)S(1)} fusion(bf16[512,1024]{1,0:T(8,128)(2,1)S(1)} %bitcast.56, bf16[1024,2304]{1,0:T(8,128)(2,1)S(1)} %bitcast.54), kind=kOutput, calls=%fused_computation.9 | convolution fusion | flops 2415919104 | bytes 10485760 | tf_op jit(solution)/shard_map/dot_general | solution.py:88
  102.2 0.0 slice-done.2
  102.2 0.0 slice-done.3
  102.2 4.7 %multiply_convert_fusion = (bf16[512,2304]{1,0:T(8,128)(2,1)S(1)}, bf16[512,2304]{1,0:T(8,128)(2,1)S(1)}, bf16[512,2304]{1,0:T(8,128)(2,1)S(1)}) fusion(f32[512,2304]{1,0:T(8,128)S(1)} %fusion.1, f32[512,2304]{1,0:T(8,128)S(1)} %fusion, bf16[512,1024]{1,0:T(8,128)(2,1)S(1)} %bitcast.57, bf16[1024,2304]{1,0:T(8,128)(2,1)S(1)} %bitcast.52), kind=kOutput, calls=%fused_computation.3 | convolution fusion | flops 2434793472 | bytes 22282240 | tf_op jit(solution)/shard_map/dot_general | solution.py:88
  106.9 0.0 slice-start
  106.9 2.6 %fusion.2 = f32[512,1024]{1,0:T(8,128)S(1)} fusion(bf16[512,2304]{1,0:T(8,128)(2,1)S(1)} %get-tuple-element.85, bf16[1024,2304]{1,0:T(8,128)(2,1)S(1)} %bitcast.55), kind=kOutput, calls=%fused_computation.10 | convolution fusion | flops 2415919104 | bytes 9175040 | tf_op jit(solution)/shard_map/dot_general | solution.py:92
  109.5 0.0 slice-start.1
  109.5 4.0 %convolution_add_fusion = f32[512,1024]{1,0:T(8,128)} fusion(f32[512,1024]{1,0:T(8,128)S(1)} %fusion.2, bf16[512,2304]{1,0:T(8,128)(2,1)S(1)} %get-tuple-element.86, bf16[1024,2304]{1,0:T(8,128)(2,1)S(1)} %bitcast.53), kind=kOutput, calls=%fused_computation.7 | convolution fusion | flops 2416443392 | bytes 11272192 | tf_op jit(solution)/shard_map/dot_general | solution.py:92
  113.5 0.0 slice-done
  113.5 0.0 slice-done.1
  113.5 0.0 copy-start.2
  113.5 4.0 %fusion.3.refs_4_ = f32[2,256,1024]{2,1,0:T(8,128)} fusion(bf16[2,256,2304]{2,1,0:T(8,128)(2,1)S(1)} %bitcast.66, bf16[2304,1024,1]{1,0,2:T(8,128)(2,1)S(1)} %bitcast.49), kind=kOutput, calls=%fused_computation.11 | convolution fusion | flops 2415919104 | bytes 9175040 | tf_op jit(solution)/shard_map/dot_general | solution.py:88
  117.5 0.0 copy-done.2
  117.5 4.3 %convolution_convert_fusion = bf16[2304,1024]{1,0:T(8,128)(2,1)} fusion(bf16[512,2304]{1,0:T(8,128)(2,1)S(1)} %get-tuple-element.84, bf16[512,1024]{1,0:T(8,128)(2,1)S(1)} %bitcast.61), kind=kOutput, calls=%fused_computation | convolution fusion | flops 2418278400 | bytes 8126464 | tf_op jit(solution)/shard_map/dot_general | solution.py:96
  121.9 4.3 %convolution_convert_fusion.2 = bf16[1024,2304]{1,0:T(8,128)(2,1)} fusion(bf16[512,1024]{1,0:T(8,128)(2,1)S(1)} %bitcast.58, bf16[512,2304]{1,0:T(8,128)(2,1)S(1)} %get-tuple-element.85), kind=kOutput, calls=%fused_computation.2 | convolution fusion | flops 2418278400 | bytes 8126464 | tf_op jit(solution)/shard_map/dot_general | solution.py:96
  126.2 4.4 %convolution_convert_fusion.1 = bf16[1024,2304]{1,0:T(8,128)(2,1)} fusion(bf16[512,1024]{1,0:T(8,128)(2,1)S(1)} %bitcast.59, bf16[512,2304]{1,0:T(8,128)(2,1)S(1)} %get-tuple-element.86), kind=kOutput, calls=%fused_computation.1 | convolution fusion | flops 2418278400 | bytes 8126464 | tf_op jit(solution)/shard_map/dot_general | solution.py:96
  130.6 86.0 %sum_gradients.1 = (f32[256,1024]{1,0:T(8,128)}, f32[256,1024]{1,0:T(8,128)}, f32[8,3072]{1,0:T(8,128)}, f32[8,1024]{1,0:T(8,128)}, f32[8,4608]{1,0:T(8,128)}, /...) custom-call(bf16[4,2,4,2,16,2304]{5,4,3,2,1,0:T(8,128)(2,1)} %bitcast.39, ...), custom_call_target="tpu_custom_call" | custom-call | tf_op jit(solution)/shard_map/sum_gradients/pallas_call | solution.py:874
  216.5 3.9 %finish.1 = (f32[256,1024]{1,0:T(8,128)}, f32[256,1024]{1,0:T(8,128)}, f32[8,3072]{1,0:T(8,128)}, f32[8,1024]{1,0:T(8,128)}, f32[8,4608]{1,0:T(8,128)}, /*index=...) custom-call(f32[256,1024]{1,0:T(8,128)} %get-tuple-element.66.refs_0_, ...), custom_call_target="tpu_custom_call" | custom-call | tf_op jit(solution)/shard_map/finish/pallas_call | solution.py:937
  (2 shorter events, 0.0 us)
Async XLA Ops:
  94.0 5.5 %copy-start = (bf16[4,2,4,2,16,2304]{5,4,3,2,1,0:T(8,128)(2,1)S(1)}, bf16[4,2,4,2,16,2304]{5,4,3,2,1,0:T(8,128)(2,1)}, u32[]{:S(2)}) copy-start(bf16[4,2,4,2,16,2304]{5,4,3,2,1,0:T(8,128)(2,1)} %get-tuple-element.51) | copy-start | bytes 14155780
  94.0 5.5 %copy-start.1 = (bf16[2,256,1024]{2,1,0:T(8,128)(2,1)S(1)}, bf16[2,256,1024]{2,1,0:T(8,128)(2,1)}, u32[]{:S(2)}) copy-start(bf16[2,256,1024]{2,1,0:T(8,128)(2,1)} %get-tuple-element.47) | copy-start | bytes 3145732
  94.1 8.1 %slice-start.2 = ((s8[4718592]{0:T(1024)(128)(4,1)}), s8[4194304]{0:T(1024)(128)(4,1)S(1)}, s32[]{:S(2)}) async-start(s8[4718592]{0:T(1024)(128)(4,1)} %bitcast.50), calls=%async_computation.2 | async-start | bytes 8388608
  99.5 2.6 %slice-start.3 = ((s8[4718592]{0:T(1024)(128)(4,1)}), s8[524288]{0:T(1024)(128)(4,1)S(1)}, s32[]{:S(2)}) async-start(s8[4718592]{0:T(1024)(128)(4,1)} %bitcast.50), calls=%async_computation.3 | async-start | bytes 1048576
  106.9 6.6 %slice-start = ((s8[4718592]{0:T(1024)(128)(4,1)}), s8[4194304]{0:T(1024)(128)(4,1)S(1)}, s32[]{:S(2)}) async-start(s8[4718592]{0:T(1024)(128)(4,1)} %bitcast.47), calls=%async_computation | async-start | bytes 8388608
  109.5 4.0 %slice-start.1 = ((s8[4718592]{0:T(1024)(128)(4,1)}), s8[524288]{0:T(1024)(128)(4,1)S(1)}, s32[]{:S(2)}) async-start(s8[4718592]{0:T(1024)(128)(4,1)} %bitcast.47), calls=%async_computation.1 | async-start | bytes 1048576
  113.5 4.0 %copy-start.2 = (bf16[2,256,1024]{2,1,0:T(8,128)(2,1)S(1)}, bf16[2,256,1024]{2,1,0:T(8,128)(2,1)}, u32[]{:S(2)}) copy-start(bf16[2,256,1024]{2,1,0:T(8,128)(2,1)} %get-tuple-element.48) | copy-start | bytes 3145732
